TPU v7x, 256 devices: a whole 4x4x8 slice. The times are simulated.
256 devices in a mesh: grp: 4 (over z_lo, core), tm: 64 (over x, y, z_hi).
Axes of the slice: x: 4, y: 4, z: 8 (z_hi: 4, z_lo: 2; z = z_hi * 2 + z_lo), core: 2. Of those that a mesh axis runs over, the one named last changes fastest.
Arguments:
- seed_field: float32 [4, 2, 8388608], P('grp', None, 'tm'), may hold values from -4 to 4
Outputs:
- spectrogram: float32 [4, 8192, 2048], P('grp', 'tm')
- correlation: float32 [16384, 16384], P('tm', 'grp')
All inputs are finite; a program needn't handle non-finite values.
Results may differ from a plain program's by a relative error of at most 0.0003.
Values sent between devices are 32-bit elements; how exact they have to be, the bound alone decides.
No kernel may reach another device: no remote copies, remote signals or barrier semaphores. Data moves between devices by JAX's collectives and lax.ppermute only.
A program may use at most 128 MiB of HBM per device.

v0:
```python
import functools
import math

import jax
import jax.numpy as jnp
import ml_dtypes
import numpy as np
from jax import lax
from jax.experimental import pallas as pl
from jax.experimental.pallas import tpu as pltpu
from jax.sharding import PartitionSpec as P

NT = 1 << 23
LOCAL = 1 << 17
HOPS = 128
HOP = 1024
W = 2048
BINS = 16384
TAPS = 512
BIN_WIDTH = 512
PEAK_AMPLITUDE = 2.0
KERR_GAIN = 0.5
RAMAN_SHARE = 0.18
RESPONSE_FAST = 12.2
RESPONSE_SLOW = 32.0
RESPONSE_SCALE = (12.2 * 12.2 + 32.0 * 32.0) / (12.2 * 32.0 * 32.0)
FLOOR_SHARE = 0.5
F32 = jnp.float32
BF16 = jnp.bfloat16
VMEM = pl.BlockSpec(memory_space=pltpu.VMEM)
HBM = pl.BlockSpec(memory_space=pltpu.HBM)
PARAMS = pltpu.CompilerParams(vmem_limit_bytes=48 * 1024 * 1024)


def split_const(table):
    table = np.asarray(table, np.float64)
    high = table.astype(ml_dtypes.bfloat16)
    low = (table - high.astype(np.float64)).astype(ml_dtypes.bfloat16)
    return np.stack([high, low])


def left_form(matrix):
    return np.block([[matrix.real, -matrix.imag], [matrix.imag, matrix.real]])


def right_form(matrix):
    return np.block([[matrix.real, matrix.imag], [-matrix.imag, matrix.real]])


def dft(size, sign):
    index = np.arange(size)
    return np.exp(sign * 2j * np.pi * (index[:, None] * index[None, :] % size) / size)


def row_order():
    row = np.arange(256)
    return row // 16 + 16 * (row % 16)


@functools.lru_cache(maxsize=None)
def tables():
    out = {}
    lag = np.arange(256)[None, :] - np.arange(256)[:, None]
    taps = np.arange(TAPS)
    response = RESPONSE_SCALE * np.exp(-taps / RESPONSE_SLOW) * np.sin(taps / RESPONSE_FAST)
    blocks = []
    for step in range(3):
        position = 256 * step + lag
        inside = (position >= 0) & (position < TAPS)
        blocks.append(np.where(inside, response[np.clip(position, 0, TAPS - 1)], 0.0))
    out["toeplitz"] = split_const(np.concatenate(blocks, 0))
    out["hop_fwd"] = split_const(left_form(dft(128, -1)))
    out["sub_fwd"] = split_const(right_form(dft(256, -1)))
    out["sub_inv"] = split_const(left_form(dft(256, 1)[row_order()]) / NT)
    out["hop_inv"] = split_const(right_form(dft(128, 1)))
    inner = np.arange(128)
    window = np.sin(np.pi / W * np.arange(W)) ** 2
    frames = []
    for a in range(16):
        block = np.exp(-2j * np.pi * (inner[:, None] * inner[None, :] % 128) / 128)
        block = block * window[a + 16 * inner][None, :]
        block = block * np.exp(-2j * np.pi * a * inner / 2048)[:, None]
        frames.append(left_form(block))
    out["frames"] = split_const(np.stack(frames))
    return out


def halves(value):
    high = value.astype(BF16)
    low = (value - high.astype(F32)).astype(BF16)
    return high, low


def dims(contract):
    return (contract, ((), ()))


NN = ((1,), (0,))
NT_FORM = ((1,), (1,))


def dot_right(value, table, contract=NN):
    high, low = halves(value)
    dot = lambda a, b: lax.dot_general(a, b, dims(contract), preferred_element_type=F32)
    return dot(high, table[0]) + (dot(high, table[1]) + dot(low, table[0]))


def dot_left(table, value, contract=NN):
    high, low = halves(value)
    dot = lambda a, b: lax.dot_general(a, b, dims(contract), preferred_element_type=F32)
    return dot(table[0], high) + (dot(table[1], high) + dot(table[0], low))


def cmul(a, b):
    return (a[0] * b[0] - a[1] * b[1], a[0] * b[1] + a[1] * b[0])


def quad(x, sign):
    s02 = (x[0][0] + x[2][0], x[0][1] + x[2][1])
    d02 = (x[0][0] - x[2][0], x[0][1] - x[2][1])
    s13 = (x[1][0] + x[3][0], x[1][1] + x[3][1])
    d13 = (x[1][0] - x[3][0], x[1][1] - x[3][1])
    turned = (-sign * d13[1], sign * d13[0])
    return [
        (s02[0] + s13[0], s02[1] + s13[1]),
        (d02[0] + turned[0], d02[1] + turned[1]),
        (s02[0] - s13[0], s02[1] - s13[1]),
        (d02[0] - turned[0], d02[1] - turned[1]),
    ]


def powers(first):
    second = (first[0] * first[0] - first[1] * first[1], 2.0 * first[0] * first[1])
    return [None, first, second, cmul(first, second)]


def twist(values, factors):
    return [values[0]] + [cmul(values[k], factors[k]) for k in (1, 2, 3)]


def sincos(x):
    turns = jnp.floor(x * (2.0 / math.pi) + 0.5)
    rest = ((x - turns * 1.5703125) - turns * 4.837512969970703125e-4) - turns * 7.549789948768648e-8
    sq = rest * rest
    sine = rest + rest * sq * (
        -1.6666654611e-1 + sq * (8.3321608736e-3 + sq * -1.9515295891e-4)
    )
    cosine = 1.0 - 0.5 * sq + sq * sq * (
        4.166664568298827e-2 + sq * (-1.388731625493765e-3 + sq * 2.443315711809948e-5)
    )
    part = turns.astype(jnp.int32)
    odd = (part & 1) == 1
    s_val = jnp.where(odd, cosine, sine)
    c_val = jnp.where(odd, sine, cosine)
    s_val = jnp.where((part & 2) == 2, -s_val, s_val)
    c_val = jnp.where(((part + 1) & 2) == 2, -c_val, c_val)
    return s_val, c_val


def pulse_of(position):
    offset = (position - NT // 2).astype(F32) * (16.0 / NT)
    fall = jnp.exp(-jnp.abs(offset))
    return (2.0 * PEAK_AMPLITUDE) * fall / (1.0 + fall * fall)


SHIFT = {"x": 4, "y": 2, "z": 0}


def digits():
    tm = lax.axis_index("tm")
    return {axis: (tm >> SHIFT[axis]) & 3 for axis in SHIFT}


def iota(shape, axis):
    return lax.broadcasted_iota(jnp.int32, shape, axis)


def phasor(number, span, sign):
    sine, cosine = sincos((sign * 2.0 * math.pi / span) * number.astype(F32))
    return cosine, sine


def turn(number, span, sign):
    angle = sign * 2.0 * math.pi * number / span
    return math.cos(angle), math.sin(angle)


def span_of(axis, place):
    if axis == "x":
        return 1 << 23, place["y"] * (1 << 19) + place["z"] * (1 << 17) + 256 * place["x"]
    if axis == "y":
        return 1 << 21, place["z"] * (1 << 17) + 256 * place["x"]
    return 1 << 19, 256 * place["x"]


def fwd_first(axis, place):
    span, base = span_of(axis, place)
    first = phasor(base + 1024 * iota((8, 256), 0) + iota((8, 256), 1), span, -1)
    return first, turn(8 * 1024, span, -1)


def inv_first(axis, place):
    span, base = span_of(axis, place)
    first = phasor(base + 16 * iota((8, 128), 0) + 1024 * iota((8, 128), 1), span, 1)
    return first, turn(1, span, 1), turn(128, span, 1)


def eight(start):
    return pl.ds(pl.multiple_of(start, 8), 8)


def start_kernel(seed, halo, toep_hbm, o0, o1, o2, o3, buf, fre, sc_out, toep, sem):
    copy = pltpu.make_async_copy(toep_hbm, toep, sem)
    copy.start()
    place = digits()
    out_at = place["x"]
    base = lax.axis_index("tm") * LOCAL
    buf[0:8, 512:1024] = jnp.broadcast_to(halo[...], (8, 512))

    def fill(step, carry):
        rows = eight(step * 8)
        row = iota((8, 1024), 0) + step * 8
        value = seed[0, rows, :] + pulse_of(base + row * 1024 + iota((8, 1024), 1))
        other = seed[1, rows, :]
        fre[rows, :] = value
        buf[eight(step * 8 + 8), :] = value * value + other * other
        return carry

    lax.fori_loop(0, 16, fill, 0)
    copy.wait()
    own = [halves(buf[8:136, 256 * e : 256 * e + 256]) for e in range(4)]
    back = {e: halves(buf[7:135, 256 * e : 256 * e + 256]) for e in (2, 3)}
    for e in range(4):
        total = None
        for step in range(3):
            at = e - step
            high, low = own[at] if at >= 0 else back[at + 4]
            t_high = toep[0, 256 * step : 256 * step + 256, :]
            t_low = toep[1, 256 * step : 256 * step + 256, :]
            term = (
                jnp.dot(high, t_high, preferred_element_type=F32)
                + jnp.dot(high, t_low, preferred_element_type=F32)
                + jnp.dot(low, t_high, preferred_element_type=F32)
            )
            total = term if total is None else total + term
        lanes = slice(256 * e, 256 * e + 256)
        phase = KERR_GAIN * ((1.0 - RAMAN_SHARE) * buf[8:136, lanes] + RAMAN_SHARE * total)
        sine, cosine = sincos(phase)
        value = fre[:, lanes]
        other = seed[1, :, lanes]
        slot = (e - out_at) & 3
        sc_out[slot, 0] = value * cosine - other * sine
        sc_out[slot, 1] = value * sine + other * cosine
    for step, out in enumerate((o0, o1, o2, o3)):
        out[...] = sc_out[step]


def take_fwd(where, blocks, scratch, rows):
    for step in range(4):
        scratch[(where - step) & 3, :, rows, :] = blocks[step][:, rows, :]
    return [(scratch[t, 0, rows, :], scratch[t, 1, rows, :]) for t in range(4)]


def fwd_kernel(axis, to, r0, r1, r2, r3, o0, o1, o2, o3, sc_in, sc_out):
    place = digits()
    first, forward = fwd_first(axis, place)

    def body(step, factor):
        rows = eight(step * 8)
        x = take_fwd(place[axis], (r0, r1, r2, r3), sc_in, rows)
        y = twist(quad(x, -1.0), powers(factor))
        for k in range(4):
            slot = (k - place[to]) & 3
            sc_out[slot, 0, rows, :] = y[k][0]
            sc_out[slot, 1, rows, :] = y[k][1]
        for j, out in enumerate((o0, o1, o2, o3)):
            out[:, rows, :] = sc_out[j, :, rows, :]
        return cmul(factor, forward)

    lax.fori_loop(0, 16, body, first)


def hop_kernel(r0, r1, r2, r3, mat, o0, o1, o2, o3, sc_in, work, sc_out, cross):
    place = digits()
    first, forward = fwd_first("z", place)
    number = 256 * place["x"] + iota((8, 256), 1)
    cross_first = phasor(iota((8, 256), 0) * number, LOCAL, -1)
    cross_step = phasor(8 * number, LOCAL, -1)

    def body(step, carry):
        factor, other = carry
        rows = eight(step * 8)
        x = take_fwd(place["z"], (r0, r1, r2, r3), sc_in, rows)
        y = twist(quad(x, -1.0), powers(factor))
        for k in range(4):
            work[k, rows, :] = y[k][0]
            work[k, eight(step * 8 + 128), :] = y[k][1]
        cross[0, rows, :] = other[0]
        cross[1, rows, :] = other[1]
        return cmul(factor, forward), cmul(other, cross_step)

    lax.fori_loop(0, 16, body, (first, cross_first))
    for k in range(4):
        got = dot_left(mat, work[k])
        re, im = cmul((got[:128], got[128:]), (cross[0], cross[1]))
        slot = (k - place["x"]) & 3
        sc_out[slot, 0] = re
        sc_out[slot, 1] = im
    for step, out in enumerate((o0, o1, o2, o3)):
        out[...] = sc_out[step]


def give_inv(outs, y, where, scratch, rows, low_rows):
    for k in range(4):
        slot = (k - where) & 3
        scratch[slot, rows, :] = y[k][0]
        scratch[slot, low_rows, :] = y[k][1]
    for j, out in enumerate(outs):
        out[rows, :] = scratch[j, rows, :]
        out[low_rows, :] = scratch[j, low_rows, :]


def spectrum_kernel(
    r0, r1, r2, r3, mat, disp, inv, o0, o1, o2, o3, sc_in, work, back, sc_out, bins, flip, flat
):
    place = digits()
    outs = (o0, o1, o2, o3)
    lanes = phasor(iota((8, 256), 1), 1024, -1)

    def body(step, carry):
        rows = eight(step * 8)
        x = take_fwd(place["x"], (r0, r1, r2, r3), sc_in, rows)
        y = twist(quad(x, -1.0), powers(lanes))
        for k in range(4):
            at = eight(step * 8 + 128 * k)
            work[at, 0:256] = y[k][0]
            work[at, 256:512] = y[k][1]
        return carry

    lax.fori_loop(0, 16, body, 0)
    bins[64:128, :] = jnp.zeros((64, 256), F32)
    for k in range(4):
        rows = slice(128 * k, 128 * k + 128)
        got = dot_right(work[rows, :], mat)
        re, im = got[:, :256], got[:, 256:]
        power = (re * re + im * im).reshape(16, 8, 256)
        bins[16 * k : 16 * k + 16, :] = jnp.sum(power, axis=1) * (1.0 / (NT * BIN_WIDTH))
        re, im = cmul((re, im), (disp[0, rows, :], disp[1, rows, :]))
        work[rows, 0:256] = re
        work[rows, 256:512] = im
    for half in range(2):
        flip[128 * half : 128 * half + 128, :] = bins[:, 128 * half : 128 * half + 128].T
    flat[...] = flip[pl.ds(0, 128, stride=2), :] + pltpu.roll(flip[pl.ds(1, 128, stride=2), :], 64, 1)
    for j, out in enumerate(outs):
        at = pl.multiple_of(((place["x"] + j) & 3) * 32, 32)
        out[512:544, :] = flat[pl.ds(at, 32), :]
    back[...] = dot_left(inv, work[...], NT_FORM)
    first = phasor(16 * iota((8, 128), 0), 1024, 1)
    forward, half_turn = turn(1, 1024, 1), turn(128, 1024, 1)

    def tail(a, factor):
        for half in range(2):
            rows, low_rows = eight(a * 16 + 8 * half), eight(a * 16 + 8 * half + 256)
            x = [
                (back[rows, 128 * k : 128 * k + 128], back[low_rows, 128 * k : 128 * k + 128])
                for k in range(4)
            ]
            now = cmul(factor, half_turn) if half else factor
            y = quad(twist(x, powers(now)), 1.0)
            give_inv(outs, y, place["x"], sc_out, rows, low_rows)
        return cmul(factor, forward)

    lax.fori_loop(0, 16, tail, first)


def take_inv(where, blocks, scratch, rows, low_rows):
    for step in range(4):
        at = (where - step) & 3
        scratch[at, rows, :] = blocks[step][rows, :]
        scratch[at, low_rows, :] = blocks[step][low_rows, :]
    return [(scratch[k, rows, :], scratch[k, low_rows, :]) for k in range(4)]


def bins_on(blocks, outs):
    total = (blocks[0][512:544, :] + blocks[1][512:544, :]) + (
        blocks[2][512:544, :] + blocks[3][512:544, :]
    )
    for out in outs:
        out[512:544, :] = total


def unhop_kernel(r0, r1, r2, r3, mat, o0, o1, o2, o3, sc_in, work, sc_out):
    place = digits()
    blocks, outs = (r0, r1, r2, r3), (o0, o1, o2, o3)
    bins_on(blocks, outs)
    freq = iota((8, 128), 1)
    cross = phasor((256 * place["x"] + 16 * iota((8, 128), 0)) * freq, LOCAL, 1)
    cross_step, cross_half = phasor(freq, LOCAL, 1), phasor(128 * freq, LOCAL, 1)

    def body(a, factor):
        for half in range(2):
            rows, low_rows = eight(a * 16 + 8 * half), eight(a * 16 + 8 * half + 256)
            x = take_inv(place["x"], blocks, sc_in, rows, low_rows)
            now = cmul(factor, cross_half) if half else factor
            for k in range(4):
                re, im = cmul(x[k], now)
                work[k, rows, 0:128] = re
                work[k, rows, 128:256] = im
        return cmul(factor, cross_step)

    lax.fori_loop(0, 16, body, cross)
    for k in range(4):
        work[k] = dot_right(work[k], mat)
    first, forward, half_turn = inv_first("z", place)

    def tail(a, factor):
        for half in range(2):
            rows, low_rows = eight(a * 16 + 8 * half), eight(a * 16 + 8 * half + 256)
            x = [(work[k, rows, 0:128], work[k, rows, 128:256]) for k in range(4)]
            now = cmul(factor, half_turn) if half else factor
            y = quad(twist(x, powers(now)), 1.0)
            give_inv(outs, y, place["z"], sc_out, rows, low_rows)
        return cmul(factor, forward)

    lax.fori_loop(0, 16, tail, first)


def inv_kernel(axis, to, last, *refs):
    blocks, outs, (sc_in, sc_out) = refs[:4], refs[4:8], refs[-2:]
    bins_on(blocks, outs if not last else ())
    if last:
        refs[8][...] = (blocks[0][512:544, :] + blocks[1][512:544, :]) + (
            blocks[2][512:544, :] + blocks[3][512:544, :]
        )
    place = digits()
    first, forward, half_turn = inv_first(to, place)

    def body(a, factor):
        for half in range(2):
            rows, low_rows = eight(a * 16 + 8 * half), eight(a * 16 + 8 * half + 256)
            x = take_inv(place[axis], blocks, sc_in, rows, low_rows)
            now = cmul(factor, half_turn) if half else factor
            y = quad(twist(x, powers(now)), 1.0)
            give_inv(outs, y, place[to], sc_out, rows, low_rows)
        return cmul(factor, forward)

    lax.fori_loop(0, 16, body, first)


def frames_kernel(r0, r1, r2, r3, tail, mat, out, sc_in, nxt, got):
    place = digits()
    for step, block in enumerate((r0, r1, r2, r3)):
        sc_in[(place["x"] - step) & 3] = block[...]
    columns = tail[...].T
    lane = iota((128, 128), 1)
    for step in range(4):
        p = (place["x"] - step) & 3
        for quarter in range(4):
            at = step * 4 + quarter
            rows = slice(128 * quarter, 128 * quarter + 128)
            rolled = pltpu.roll(sc_in[p, rows, :], 127, 1)
            nxt[p, rows, :] = jnp.where(lane == 127, columns[:, at : at + 1], rolled)
    for a in range(16):
        pieces = []
        for part in range(2):
            rows = slice(256 * part + 16 * a, 256 * part + 16 * a + 16)
            pieces += [sc_in[p, rows, :] for p in range(4)]
            pieces += [nxt[p, rows, :] for p in range(4)]
        got[a] = dot_left(mat.at[:, a], jnp.concatenate(pieces, axis=0))

    def body(step, carry):
        rows = eight(step * 8)
        low_rows = eight(step * 8 + 128)
        inner = []
        for a0 in range(4):
            x = [(got[4 * a1 + a0, rows, :], got[4 * a1 + a0, low_rows, :]) for a1 in range(4)]
            inner.append(quad(x, -1.0))
        for c0 in range(4):
            x = []
            for a0 in range(4):
                value = inner[a0][c0]
                if a0 * c0:
                    value = cmul(value, turn(a0 * c0, 16, -1))
                x.append(value)
            for c1, value in enumerate(quad(x, -1.0)):
                got[c0 + 4 * c1, rows, :] = (value[0] * value[0] + value[1] * value[1]) * (1.0 / W)
        return carry

    lax.fori_loop(0, 16, body, 0)
    for c in range(16):
        out[:, 128 * c : 128 * c + 128] = got[c, 0:128, :].T


def normal_kernel(b0, b1, b2, b3, out):
    blocks = [b[...] for b in (b0, b1, b2, b3)]
    total = (blocks[0] + blocks[1]) + (blocks[2] + blocks[3])
    average = total * 0.25
    centred = [b - average for b in blocks]
    sq = [c * c for c in centred]
    variance = ((sq[0] + sq[1]) + (sq[2] + sq[3])) * 0.25
    spread = jnp.sqrt(jnp.maximum(variance, FLOOR_SHARE * average * average / BIN_WIDTH))
    grp = lax.axis_index("grp")
    for step in range(4):
        out[(grp - step) & 3] = centred[step] / spread


def correlation_kernel(own, cols, out, side, pad):
    step = pl.program_id(0)

    @pl.when(step == 0)
    def _():
        at = (lax.axis_index("tm") & 15) * 2
        pad[...] = jnp.zeros((128, 128), F32)
        for r in range(4):
            for half in range(2):
                pad[2 * r + half : 2 * r + half + 1, :] = own[r, pl.ds(at + half, 1), :] * 0.25
        flipped = pad[...].T
        for r in range(4):
            for half in range(2):
                column = flipped[:, 2 * r + half : 2 * r + half + 1]
                side[r, 128 * half : 128 * half + 128, :] = jnp.broadcast_to(column, (128, 128))

    for group in range(4):
        rows = eight(step * 32 + group * 8)
        factors = [side[r, rows, :] for r in range(4)]
        for k in range(32):
            total = factors[0] * cols[0, k : k + 1, :]
            for r in range(1, 4):
                total = total + factors[r] * cols[r, k : k + 1, :]
            out[8 * group : 8 * group + 8, 128 * k : 128 * k + 128] = total


def call(kernel, outs, scratch, *args, flops=1 << 20, specs=None):
    size = sum(int(np.prod(s)) * 4 for s in outs)
    return pl.pallas_call(
        kernel,
        out_shape=[jax.ShapeDtypeStruct(s, F32) for s in outs],
        in_specs=specs or [VMEM] * len(args),
        out_specs=[VMEM] * len(outs),
        scratch_shapes=[pltpu.VMEM(s, F32) if isinstance(s, tuple) else s for s in scratch],
        compiler_params=PARAMS,
        cost_estimate=pl.CostEstimate(flops=flops, bytes_accessed=2 * size, transcendentals=0),
    )(*args)


def ring(axis, step):
    stride = 1 << SHIFT[axis]
    pairs = []
    for device in range(64):
        digit = device // stride % 4
        pairs.append((device, device + ((digit + step) % 4 - digit) * stride))
    return pairs


def swap_blocks(blocks, axis):
    moved = {step: lax.ppermute(blocks[step], "tm", ring(axis, step)) for step in (1, 3, 2)}
    return [blocks[0], moved[1], moved[2], moved[3]]


FWD = (2, 128, 256)
INV = (512, 128)
MORE = (544, 128)


def on_device(seed_field):
    table = tables()
    tm = lax.axis_index("tm")
    ix, iy, iz = tm // 16, tm // 4 % 4, tm % 4

    seed = seed_field.reshape(2, HOPS, HOP)
    last = seed_field[0, :, LOCAL - TAPS :].reshape(8, 128)
    last = lax.ppermute(last, "tm", [(d, (d + 1) % 64) for d in range(64)]).reshape(2, TAPS)
    spots = (tm * LOCAL - TAPS + jnp.arange(TAPS, dtype=jnp.int32)) & (NT - 1)
    halo = ((last[0] + pulse_of(spots)) ** 2 + last[1] ** 2)[None, :]

    blocks = call(
        start_kernel, [FWD] * 4,
        [(136, 1024), (128, 1024), (4,) + FWD, pltpu.VMEM((2, 768, 256), BF16), pltpu.SemaphoreType.DMA],
        seed, halo, table["toeplitz"], specs=[VMEM, VMEM, HBM],
    )
    blocks = swap_blocks(blocks, "x")
    blocks = call(functools.partial(fwd_kernel, "x", "y"), [FWD] * 4, [(4,) + FWD] * 2, *blocks)
    blocks = swap_blocks(blocks, "y")
    blocks = call(functools.partial(fwd_kernel, "y", "z"), [FWD] * 4, [(4,) + FWD] * 2, *blocks)
    blocks = swap_blocks(blocks, "z")
    blocks = call(
        hop_kernel, [FWD] * 4, [(4,) + FWD, (4, 256, 256), (4,) + FWD, FWD], *blocks, table["hop_fwd"]
    )
    blocks = swap_blocks(blocks, "x")
    number = (
        (iy + 4 * iz + 16 * ix)
        + 8192 * jnp.arange(4, dtype=jnp.int32)[:, None, None]
        + 64 * jnp.arange(128, dtype=jnp.int32)[None, :, None]
        + 32768 * jnp.arange(256, dtype=jnp.int32)[None, None, :]
    ).reshape(512, 256)
    freq = jnp.where(number < NT // 2, number, number - NT)
    angle = (2.0 * math.pi / (1 << 28)) * (freq * freq & ((1 << 28) - 1)).astype(F32)
    disp = jnp.stack([jnp.cos(angle), jnp.sin(angle)])
    blocks = call(
        spectrum_kernel, [MORE] * 4,
        [(4,) + FWD, (512, 512), (512, 512), (4,) + INV, (128, 256), (256, 128), (128, 128)],
        *blocks, table["sub_fwd"], disp, table["sub_inv"],
    )
    blocks = swap_blocks(blocks, "x")
    blocks = call(
        unhop_kernel, [MORE] * 4, [(4,) + INV, (4, 256, 256), (4,) + INV], *blocks, table["hop_inv"]
    )
    blocks = swap_blocks(blocks, "z")
    blocks = call(
        functools.partial(inv_kernel, "z", "y", False), [MORE] * 4, [(4,) + INV] * 2, *blocks
    )
    blocks = swap_blocks(blocks, "y")
    *blocks, bins = call(
        functools.partial(inv_kernel, "y", "x", True), [INV] * 4 + [(32, 128)], [(4,) + INV] * 2, *blocks
    )
    sent = blocks
    blocks = swap_blocks(sent, "x")

    edges = jnp.stack([b[:, 0] for b in sent]).reshape(4, 4, 128)
    behind = [(d // 16 * 16 + (d % 16 + 1) % 16, d) for d in range(64)]
    edges = lax.ppermute(edges, "tm", behind)
    edges = jnp.where(tm % 16 == 15, jnp.roll(edges, -1, axis=0), edges)
    tail = jnp.stack(swap_blocks([edges[j] for j in range(4)], "x")).reshape(16, 128)

    alike = [bins] + [
        lax.ppermute(bins, "grp", [(g, (g + step) % 4) for g in range(4)]) for step in (1, 2, 3)
    ]
    normal = call(normal_kernel, [(4, 32, 128)], [], *alike)[0]
    pairs = []
    for g in range(4):
        for d in range(64):
            pairs.append((g * 64 + d, d // 16 * 64 + g * 16 + d % 16))
    columns = lax.ppermute(normal, ("grp", "tm"), pairs)

    spectrogram = call(
        frames_kernel, [(HOPS, W)], [(4,) + INV, (4,) + INV, (16, 256, 128)],
        *blocks, tail, table["frames"],
    )[0]
    correlation = pl.pallas_call(
        correlation_kernel,
        grid=(8,),
        out_shape=jax.ShapeDtypeStruct((256, 4096), F32),
        in_specs=[pl.BlockSpec((4, 32, 128), lambda i: (0, 0, 0))] * 2,
        out_specs=pl.BlockSpec((32, 4096), lambda i: (i, 0)),
        scratch_shapes=[pltpu.VMEM((4, 256, 128), F32), pltpu.VMEM((128, 128), F32)],
        compiler_params=PARAMS,
        cost_estimate=pl.CostEstimate(flops=1 << 23, bytes_accessed=1 << 22, transcendentals=0),
    )(normal, columns)
    return spectrogram[None], correlation


def solution(mesh):
    return jax.shard_map(
        on_device,
        mesh=mesh,
        in_specs=(P("grp", None, "tm"),),
        out_specs=(P("grp", "tm", None), P("tm", "grp")),
        check_vma=False,
    )
```

profile of v0, /device:TPU:4, one launch (start us, length us, event | category | flops | bytes accessed | tf_op | source)
XLA Modules:
  0.0 201.5 jit_solution(16104314352764504676)
XLA Ops:
  1.4 3.3 %collective-permute-start = (f32[8,128]{1,0:T(8,128)S(1)}, f32[8,128]{1,0:T(8,128)S(1)}, u32[]{:S(2)}, u32[]{:S(2)}) collective-permute-start(f32[8,128]{1,0:T(8,128)S(1)} %reshape_squeeze.3), channel_id=1, source_target_pairs={{0,1},{1,2},{2,3},{3,4},{4,5},{5,6},{6,7},{7,8},{8,9},{9,10},{10,1... | collective-permute-start | bytes 12296 | tf_op jit(solution)/shard_map/ppermute | solution.py:572
  6.2 5.5 %collective-permute-done = f32[8,128]{1,0:T(8,128)S(1)} collective-permute-done((f32[8,128]{1,0:T(8,128)S(1)}, f32[8,128]{1,0:T(8,128)S(1)}, u32[]{:S(2)}, u32[]{:S(2)}) %collective-permute-start) | collective-permute-done | bytes 4128 | tf_op jit(solution)/shard_map/ppermute | solution.py:572
  23.5 5.5 %collective-permute-done.2.r2 = f32[2,128,256]{2,1,0:T(8,128)S(1)} collective-permute-done((f32[2,128,256]{2,1,0:T(8,128)S(1)}, f32[2,128,256]{2,1,0:T(8,128)S(1)}, u32[]{:S(2)}, u32[]{:S(2)}) %collective-permute-start.2) | collective-permute-done | bytes 262176 | tf_op jit(solution)/shard_map/ppermute | solution.py:556
  34.7 10.6 %collective-permute-done.4.r1 = f32[2,128,256]{2,1,0:T(8,128)S(1)} collective-permute-done((f32[2,128,256]{2,1,0:T(8,128)}, f32[2,128,256]{2,1,0:T(8,128)S(1)}, u32[]{:S(2)}, u32[]{:S(2)}) %collective-permute-start.4) | collective-permute-done | bytes 262176 | tf_op jit(solution)/shard_map/ppermute | solution.py:556
  48.6 3.9 %collective-permute-start.9 = (f32[2,128,256]{2,1,0:T(8,128)S(1)}, f32[2,128,256]{2,1,0:T(8,128)S(1)}, u32[]{:S(2)}, u32[]{:S(2)}) collective-permute-start(f32[2,128,256]{2,1,0:T(8,128)S(1)} %get-tuple-element.46), channel_id=1, source_target_pairs={{0,3},{1,0},{2,1},{3,2},{4,7},{5,4},{6,5},{7,6},{8,11},{9,8},{10,9... | collective-permute-start | bytes 786440 | tf_op jit(solution)/shard_map/ppermute | solution.py:556
  52.6 13.6 %collective-permute-done.7.r1 = f32[2,128,256]{2,1,0:T(8,128)S(1)} collective-permute-done((f32[2,128,256]{2,1,0:T(8,128)S(1)}, f32[2,128,256]{2,1,0:T(8,128)S(1)}, u32[]{:S(2)}, u32[]{:S(2)}) %collective-permute-start.7) | collective-permute-done | bytes 262176 | tf_op jit(solution)/shard_map/ppermute | solution.py:556
  66.2 8.0 %collective-permute-done.9.r3 = f32[2,128,256]{2,1,0:T(8,128)S(1)} collective-permute-done((f32[2,128,256]{2,1,0:T(8,128)S(1)}, f32[2,128,256]{2,1,0:T(8,128)S(1)}, u32[]{:S(2)}, u32[]{:S(2)}) %collective-permute-start.9) | collective-permute-done | bytes 262176 | tf_op jit(solution)/shard_map/ppermute | solution.py:556
  75.5 4.1 %collective-permute-start.10 = (f32[2,128,256]{2,1,0:T(8,128)S(1)}, f32[2,128,256]{2,1,0:T(8,128)S(1)}, u32[]{:S(2)}, u32[]{:S(2)}) collective-permute-start(f32[2,128,256]{2,1,0:T(8,128)S(1)} %get-tuple-element.48), channel_id=1, source_target_pairs={{0,16},{1,17},{2,18},{3,19},{4,20},{5,21},{6,22},{7,23},{8,24},{9,... | collective-permute-start | bytes 786440 | tf_op jit(solution)/shard_map/ppermute | solution.py:556
  83.3 3.1 %collective-permute-done.10.r1 = f32[2,128,256]{2,1,0:T(8,128)S(1)} collective-permute-done((f32[2,128,256]{2,1,0:T(8,128)S(1)}, f32[2,128,256]{2,1,0:T(8,128)S(1)}, u32[]{:S(2)}, u32[]{:S(2)}) %collective-permute-start.10) | collective-permute-done | bytes 262176 | tf_op jit(solution)/shard_map/ppermute | solution.py:556
  86.3 4.7 %collective-permute-done.11.r2 = f32[2,128,256]{2,1,0:T(8,128)S(1)} collective-permute-done((f32[2,128,256]{2,1,0:T(8,128)S(1)}, f32[2,128,256]{2,1,0:T(8,128)S(1)}, u32[]{:S(2)}, u32[]{:S(2)}) %collective-permute-start.11) | collective-permute-done | bytes 262176 | tf_op jit(solution)/shard_map/ppermute | solution.py:556
  91.8 3.0 %shard_map.90 = (f32[544,128]{1,0:T(8,128)S(1)}, f32[544,128]{1,0:T(8,128)S(1)}, f32[544,128]{1,0:T(8,128)S(1)}, f32[544,128]{1,0:T(8,128)S(1)}) custom-call(f32[2,128,256]{2,1,0:T(8,128)S(1)} %get-tuple-element.47.r0, f32[2,128,256]{2,1,0:T(8,128)S(1)} %collective-permute-done.10.r1, f32[2,128,256]{2,1,0:T(8,128)S(1)} %collective-permute-done.11.r2, ...), custom_call_target="tpu_custom_call" | custom-call | flops 1048576 | bytes 2228224 | tf_op jit(solution)/shard_map/pallas_call | solution.py:535
  100.4 4.5 %collective-permute-done.13.r1 = f32[544,128]{1,0:T(8,128)S(1)} collective-permute-done((f32[544,128]{1,0:T(8,128)S(1)}, f32[544,128]{1,0:T(8,128)S(1)}, u32[]{:S(2)}, u32[]{:S(2)}) %collective-permute-start.13) | collective-permute-done | bytes 278560 | tf_op jit(solution)/shard_map/ppermute | solution.py:556
  104.8 5.4 %collective-permute-done.14.r2 = f32[544,128]{1,0:T(8,128)S(1)} collective-permute-done((f32[544,128]{1,0:T(8,128)S(1)}, f32[544,128]{1,0:T(8,128)S(1)}, u32[]{:S(2)}, u32[]{:S(2)}) %collective-permute-start.14) | collective-permute-done | bytes 278560 | tf_op jit(solution)/shard_map/ppermute | solution.py:556
  115.0 4.0 %collective-permute-start.18 = (f32[544,128]{1,0:T(8,128)S(1)}, f32[544,128]{1,0:T(8,128)S(1)}, u32[]{:S(2)}, u32[]{:S(2)}) collective-permute-start(f32[544,128]{1,0:T(8,128)S(1)} %get-tuple-element.58), channel_id=1, source_target_pairs={{0,3},{1,0},{2,1},{3,2},{4,7},{5,4},{6,5},{7,6},{8,11},{9,8},{10,9... | collective-permute-start | bytes 835592 | tf_op jit(solution)/shard_map/ppermute | solution.py:556
  119.0 5.4 %collective-permute-done.16.refs_1_ = f32[544,128]{1,0:T(8,128)S(1)} collective-permute-done((f32[544,128]{1,0:T(8,128)S(1)}, f32[544,128]{1,0:T(8,128)S(1)}, u32[]{:S(2)}, u32[]{:S(2)}) %collective-permute-start.16) | collective-permute-done | bytes 278560 | tf_op jit(solution)/shard_map/ppermute | solution.py:556
  124.5 11.6 %collective-permute-done.17.refs_2_ = f32[544,128]{1,0:T(8,128)S(1)} collective-permute-done((f32[544,128]{1,0:T(8,128)S(1)}, f32[544,128]{1,0:T(8,128)S(1)}, u32[]{:S(2)}, u32[]{:S(2)}) %collective-permute-start.17) | collective-permute-done | bytes 278560 | tf_op jit(solution)/shard_map/ppermute | solution.py:556
  143.1 4.2 %collective-permute-done.19.refs_1_ = f32[544,128]{1,0:T(8,128)S(1)} collective-permute-done((f32[544,128]{1,0:T(8,128)S(1)}, f32[544,128]{1,0:T(8,128)S(1)}, u32[]{:S(2)}, u32[]{:S(2)}) %collective-permute-start.19) | collective-permute-done | bytes 278560 | tf_op jit(solution)/shard_map/ppermute | solution.py:556
  147.2 7.1 %collective-permute-done.20.refs_2_ = f32[544,128]{1,0:T(8,128)S(1)} collective-permute-done((f32[544,128]{1,0:T(8,128)S(1)}, f32[544,128]{1,0:T(8,128)S(1)}, u32[]{:S(2)}, u32[]{:S(2)}) %collective-permute-start.20) | collective-permute-done | bytes 278560 | tf_op jit(solution)/shard_map/ppermute | solution.py:556
  158.7 3.1 %collective-permute-start.22 = (f32[512,128]{1,0:T(8,128)S(1)}, f32[512,128]{1,0:T(8,128)S(1)}, u32[]{:S(2)}, u32[]{:S(2)}) collective-permute-start(f32[512,128]{1,0:T(8,128)S(1)} %get-tuple-element.64), channel_id=1, source_target_pairs={{0,16},{1,17},{2,18},{3,19},{4,20},{5,21},{6,22},{7,23},{8,24},{9,... | collective-permute-start | bytes 786440 | tf_op jit(solution)/shard_map/ppermute | solution.py:556
  165.9 8.9 %collective-permute-done.28 = f32[4,128]{1,0:T(4,128)S(1)} collective-permute-done((f32[4,128]{1,0:T(4,128)S(1)}, f32[4,128]{1,0:T(4,128)S(1)}, u32[]{:S(2)}, u32[]{:S(2)}) %collective-permute-start.28) | collective-permute-done | bytes 2080 | tf_op jit(solution)/shard_map/ppermute | solution.py:556
  174.8 3.7 %collective-permute-done.30.b2 = f32[32,128]{1,0:T(8,128)S(1)} collective-permute-done((f32[32,128]{1,0:T(8,128)S(1)}, f32[32,128]{1,0:T(8,128)S(1)}, u32[]{:S(2)}, u32[]{:S(2)}) %collective-permute-start.30) | collective-permute-done | bytes 16416 | tf_op jit(solution)/shard_map/ppermute | solution.py:626
  186.5 6.4 %collective-permute-done.32.cols = f32[4,32,128]{2,1,0:T(8,128)S(1)} collective-permute-done((f32[4,32,128]{2,1,0:T(8,128)S(1)}, f32[4,32,128]{2,1,0:T(8,128)S(1)}, u32[]{:S(2)}, u32[]{:S(2)}) %collective-permute-start.32) | collective-permute-done | bytes 65568 | tf_op jit(solution)/shard_map/ppermute | solution.py:633
  192.9 4.2 %shard_map.96 = f32[256,4096]{1,0:T(8,128)} custom-call(f32[4,32,128]{2,1,0:T(8,128)S(1)} %shard_map.95.own, f32[4,32,128]{2,1,0:T(8,128)S(1)} %collective-permute-done.32.cols), custom_call_target="tpu_custom_call" | custom-call | flops 8388608 | bytes 4194304 | tf_op jit(solution)/shard_map/pallas_call | solution.py:639
  197.1 4.4 %shard_map.94 = f32[128,2048]{1,0:T(8,128)} custom-call(f32[512,128]{1,0:T(8,128)S(1)} %get-tuple-element.63.r0, f32[512,128]{1,0:T(8,128)S(1)} %collective-permute-done.22.r1, f32[512,128]{1,0:T(8,128)S(1)} %collective-permute-done.23.r2, f32[512,128]{1,0:T(8,128)S(1)} %collective-permute-done.24.r3, f32[16,128]{1,0:T(8,128)S(1)} %bitcast.26, ...), custom_call_target="tpu_custom_call" | custom-call | flops 1048576 | bytes 2097152 | tf_op jit(solution)/shard_map/pallas_call | solution.py:535
  (85 shorter events, 62.4 us)
Async XLA Ops:
  16.7 12.3 %collective-permute-start.2 = (f32[2,128,256]{2,1,0:T(8,128)S(1)}, f32[2,128,256]{2,1,0:T(8,128)S(1)}, u32[]{:S(2)}, u32[]{:S(2)}) collective-permute-start(f32[2,128,256]{2,1,0:T(8,128)S(1)} %get-tuple-element.37), channel_id=1, source_target_pairs={{0,32},{1,33},{2,34},{3,35},{4,36},{5,37},{6,38},{7,39},{8,40},{9,... | collective-permute-start | bytes 786440 | tf_op jit(solution)/shard_map/ppermute | solution.py:556
  18.1 11.9 %collective-permute-start.3 = (f32[2,128,256]{2,1,0:T(8,128)S(1)}, f32[2,128,256]{2,1,0:T(8,128)S(1)}, u32[]{:S(2)}, u32[]{:S(2)}) collective-permute-start(f32[2,128,256]{2,1,0:T(8,128)S(1)} %get-tuple-element.38), channel_id=1, source_target_pairs={{0,48},{1,49},{2,50},{3,51},{4,52},{5,53},{6,54},{7,55},{8,56},{9,... | collective-permute-start | bytes 786440 | tf_op jit(solution)/shard_map/ppermute | solution.py:556
  31.4 13.9 %collective-permute-start.4 = (f32[2,128,256]{2,1,0:T(8,128)}, f32[2,128,256]{2,1,0:T(8,128)S(1)}, u32[]{:S(2)}, u32[]{:S(2)}) collective-permute-start(f32[2,128,256]{2,1,0:T(8,128)} %get-tuple-element.40), channel_id=1, source_target_pairs={{0,4},{1,5},{2,6},{3,7},{4,8},{5,9},{6,10},{7,11},{8,12},{9,13},{1... | collective-permute-start | bytes 786440 | tf_op jit(solution)/shard_map/ppermute | solution.py:556
  31.4 13.9 %collective-permute-start.5 = (f32[2,128,256]{2,1,0:T(8,128)}, f32[2,128,256]{2,1,0:T(8,128)S(1)}, u32[]{:S(2)}, u32[]{:S(2)}) collective-permute-start(f32[2,128,256]{2,1,0:T(8,128)} %get-tuple-element.41), channel_id=1, source_target_pairs={{0,8},{1,9},{2,10},{3,11},{4,12},{5,13},{6,14},{7,15},{8,0},{9,1},... | collective-permute-start | bytes 786440 | tf_op jit(solution)/shard_map/ppermute | solution.py:556
  33.6 12.3 %collective-permute-start.6 = (f32[2,128,256]{2,1,0:T(8,128)}, f32[2,128,256]{2,1,0:T(8,128)S(1)}, u32[]{:S(2)}, u32[]{:S(2)}) collective-permute-start(f32[2,128,256]{2,1,0:T(8,128)} %get-tuple-element.42), channel_id=1, source_target_pairs={{0,12},{1,13},{2,14},{3,15},{4,0},{5,1},{6,2},{7,3},{8,4},{9,5},{1... | collective-permute-start | bytes 786440 | tf_op jit(solution)/shard_map/ppermute | solution.py:556
  46.5 19.7 %collective-permute-start.7 = (f32[2,128,256]{2,1,0:T(8,128)S(1)}, f32[2,128,256]{2,1,0:T(8,128)S(1)}, u32[]{:S(2)}, u32[]{:S(2)}) collective-permute-start(f32[2,128,256]{2,1,0:T(8,128)S(1)} %get-tuple-element.44), channel_id=1, source_target_pairs={{0,1},{1,2},{2,3},{3,0},{4,5},{5,6},{6,7},{7,4},{8,9},{9,10},{10,1... | collective-permute-start | bytes 786440 | tf_op jit(solution)/shard_map/ppermute | solution.py:556
  46.6 19.6 %collective-permute-start.8 = (f32[2,128,256]{2,1,0:T(8,128)S(1)}, f32[2,128,256]{2,1,0:T(8,128)S(1)}, u32[]{:S(2)}, u32[]{:S(2)}) collective-permute-start(f32[2,128,256]{2,1,0:T(8,128)S(1)} %get-tuple-element.45), channel_id=1, source_target_pairs={{0,2},{1,3},{2,0},{3,1},{4,6},{5,7},{6,4},{7,5},{8,10},{9,11},{10,... | collective-permute-start | bytes 786440 | tf_op jit(solution)/shard_map/ppermute | solution.py:556
  48.6 25.6 %collective-permute-start.9 = (f32[2,128,256]{2,1,0:T(8,128)S(1)}, f32[2,128,256]{2,1,0:T(8,128)S(1)}, u32[]{:S(2)}, u32[]{:S(2)}) collective-permute-start(f32[2,128,256]{2,1,0:T(8,128)S(1)} %get-tuple-element.46), channel_id=1, source_target_pairs={{0,3},{1,0},{2,1},{3,2},{4,7},{5,4},{6,5},{7,6},{8,11},{9,8},{10,9... | collective-permute-start | bytes 786440 | tf_op jit(solution)/shard_map/ppermute | solution.py:556
  75.5 10.8 %collective-permute-start.10 = (f32[2,128,256]{2,1,0:T(8,128)S(1)}, f32[2,128,256]{2,1,0:T(8,128)S(1)}, u32[]{:S(2)}, u32[]{:S(2)}) collective-permute-start(f32[2,128,256]{2,1,0:T(8,128)S(1)} %get-tuple-element.48), channel_id=1, source_target_pairs={{0,16},{1,17},{2,18},{3,19},{4,20},{5,21},{6,22},{7,23},{8,24},{9,... | collective-permute-start | bytes 786440 | tf_op jit(solution)/shard_map/ppermute | solution.py:556
  79.6 11.4 %collective-permute-start.11 = (f32[2,128,256]{2,1,0:T(8,128)S(1)}, f32[2,128,256]{2,1,0:T(8,128)S(1)}, u32[]{:S(2)}, u32[]{:S(2)}) collective-permute-start(f32[2,128,256]{2,1,0:T(8,128)S(1)} %get-tuple-element.49), channel_id=1, source_target_pairs={{0,32},{1,33},{2,34},{3,35},{4,36},{5,37},{6,38},{7,39},{8,40},{9,... | collective-permute-start | bytes 786440 | tf_op jit(solution)/shard_map/ppermute | solution.py:556
  79.6 12.2 %collective-permute-start.12 = (f32[2,128,256]{2,1,0:T(8,128)S(1)}, f32[2,128,256]{2,1,0:T(8,128)S(1)}, u32[]{:S(2)}, u32[]{:S(2)}) collective-permute-start(f32[2,128,256]{2,1,0:T(8,128)S(1)} %get-tuple-element.50), channel_id=1, source_target_pairs={{0,48},{1,49},{2,50},{3,51},{4,52},{5,53},{6,54},{7,55},{8,56},{9,... | collective-permute-start | bytes 786440 | tf_op jit(solution)/shard_map/ppermute | solution.py:556
  97.8 12.5 %collective-permute-start.14 = (f32[544,128]{1,0:T(8,128)S(1)}, f32[544,128]{1,0:T(8,128)S(1)}, u32[]{:S(2)}, u32[]{:S(2)}) collective-permute-start(f32[544,128]{1,0:T(8,128)S(1)} %get-tuple-element.53), channel_id=1, source_target_pairs={{0,32},{1,33},{2,34},{3,35},{4,36},{5,37},{6,38},{7,39},{8,40},{9,... | collective-permute-start | bytes 835592 | tf_op jit(solution)/shard_map/ppermute | solution.py:556
  97.8 13.2 %collective-permute-start.15 = (f32[544,128]{1,0:T(8,128)S(1)}, f32[544,128]{1,0:T(8,128)S(1)}, u32[]{:S(2)}, u32[]{:S(2)}) collective-permute-start(f32[544,128]{1,0:T(8,128)S(1)} %get-tuple-element.54), channel_id=1, source_target_pairs={{0,48},{1,49},{2,50},{3,51},{4,52},{5,53},{6,54},{7,55},{8,56},{9,... | collective-permute-start | bytes 835592 | tf_op jit(solution)/shard_map/ppermute | solution.py:556
  112.7 11.8 %collective-permute-start.16 = (f32[544,128]{1,0:T(8,128)S(1)}, f32[544,128]{1,0:T(8,128)S(1)}, u32[]{:S(2)}, u32[]{:S(2)}) collective-permute-start(f32[544,128]{1,0:T(8,128)S(1)} %get-tuple-element.56), channel_id=1, source_target_pairs={{0,1},{1,2},{2,3},{3,0},{4,5},{5,6},{6,7},{7,4},{8,9},{9,10},{10,1... | collective-permute-start | bytes 835592 | tf_op jit(solution)/shard_map/ppermute | solution.py:556
  113.9 22.2 %collective-permute-start.17 = (f32[544,128]{1,0:T(8,128)S(1)}, f32[544,128]{1,0:T(8,128)S(1)}, u32[]{:S(2)}, u32[]{:S(2)}) collective-permute-start(f32[544,128]{1,0:T(8,128)S(1)} %get-tuple-element.57), channel_id=1, source_target_pairs={{0,2},{1,3},{2,0},{3,1},{4,6},{5,7},{6,4},{7,5},{8,10},{9,11},{10,... | collective-permute-start | bytes 835592 | tf_op jit(solution)/shard_map/ppermute | solution.py:556
  115.0 21.0 %collective-permute-start.18 = (f32[544,128]{1,0:T(8,128)S(1)}, f32[544,128]{1,0:T(8,128)S(1)}, u32[]{:S(2)}, u32[]{:S(2)}) collective-permute-start(f32[544,128]{1,0:T(8,128)S(1)} %get-tuple-element.58), channel_id=1, source_target_pairs={{0,3},{1,0},{2,1},{3,2},{4,7},{5,4},{6,5},{7,6},{8,11},{9,8},{10,9... | collective-permute-start | bytes 835592 | tf_op jit(solution)/shard_map/ppermute | solution.py:556
  136.8 10.4 %collective-permute-start.19 = (f32[544,128]{1,0:T(8,128)S(1)}, f32[544,128]{1,0:T(8,128)S(1)}, u32[]{:S(2)}, u32[]{:S(2)}) collective-permute-start(f32[544,128]{1,0:T(8,128)S(1)} %get-tuple-element.60), channel_id=1, source_target_pairs={{0,4},{1,5},{2,6},{3,7},{4,8},{5,9},{6,10},{7,11},{8,12},{9,13},{1... | collective-permute-start | bytes 835592 | tf_op jit(solution)/shard_map/ppermute | solution.py:556
  139.1 15.3 %collective-permute-start.20 = (f32[544,128]{1,0:T(8,128)S(1)}, f32[544,128]{1,0:T(8,128)S(1)}, u32[]{:S(2)}, u32[]{:S(2)}) collective-permute-start(f32[544,128]{1,0:T(8,128)S(1)} %get-tuple-element.61), channel_id=1, source_target_pairs={{0,8},{1,9},{2,10},{3,11},{4,12},{5,13},{6,14},{7,15},{8,0},{9,1},... | collective-permute-start | bytes 835592 | tf_op jit(solution)/shard_map/ppermute | solution.py:556
  141.8 12.5 %collective-permute-start.21 = (f32[544,128]{1,0:T(8,128)S(1)}, f32[544,128]{1,0:T(8,128)S(1)}, u32[]{:S(2)}, u32[]{:S(2)}) collective-permute-start(f32[544,128]{1,0:T(8,128)S(1)} %get-tuple-element.62), channel_id=1, source_target_pairs={{0,12},{1,13},{2,14},{3,15},{4,0},{5,1},{6,2},{7,3},{8,4},{9,5},{1... | collective-permute-start | bytes 835592 | tf_op jit(solution)/shard_map/ppermute | solution.py:556
  158.7 38.4 %collective-permute-start.22 = (f32[512,128]{1,0:T(8,128)S(1)}, f32[512,128]{1,0:T(8,128)S(1)}, u32[]{:S(2)}, u32[]{:S(2)}) collective-permute-start(f32[512,128]{1,0:T(8,128)S(1)} %get-tuple-element.64), channel_id=1, source_target_pairs={{0,16},{1,17},{2,18},{3,19},{4,20},{5,21},{6,22},{7,23},{8,24},{9,... | collective-permute-start | bytes 786440 | tf_op jit(solution)/shard_map/ppermute | solution.py:556
  161.7 35.3 %collective-permute-start.23 = (f32[512,128]{1,0:T(8,128)S(1)}, f32[512,128]{1,0:T(8,128)S(1)}, u32[]{:S(2)}, u32[]{:S(2)}) collective-permute-start(f32[512,128]{1,0:T(8,128)S(1)} %get-tuple-element.65), channel_id=1, source_target_pairs={{0,32},{1,33},{2,34},{3,35},{4,36},{5,37},{6,38},{7,39},{8,40},{9,... | collective-permute-start | bytes 786440 | tf_op jit(solution)/shard_map/ppermute | solution.py:556
  162.6 34.5 %collective-permute-start.24 = (f32[512,128]{1,0:T(8,128)S(1)}, f32[512,128]{1,0:T(8,128)S(1)}, u32[]{:S(2)}, u32[]{:S(2)}) collective-permute-start(f32[512,128]{1,0:T(8,128)S(1)} %get-tuple-element.66), channel_id=1, source_target_pairs={{0,48},{1,49},{2,50},{3,51},{4,52},{5,53},{6,54},{7,55},{8,56},{9,... | collective-permute-start | bytes 786440 | tf_op jit(solution)/shard_map/ppermute | solution.py:556
  163.4 11.4 %collective-permute-start.31 = (f32[32,128]{1,0:T(8,128)S(1)}, f32[32,128]{1,0:T(8,128)S(1)}, u32[]{:S(2)}, u32[]{:S(2)}) collective-permute-start(f32[32,128]{1,0:T(8,128)S(1)} %get-tuple-element.67.b0), channel_id=1, source_target_pairs={{0,192},{64,0},{128,64},{192,128},{1,193},{65,1},{129,65},{193,129... | collective-permute-start | bytes 49160 | tf_op jit(solution)/shard_map/ppermute | solution.py:626
  163.5 11.4 %collective-permute-start.28 = (f32[4,128]{1,0:T(4,128)S(1)}, f32[4,128]{1,0:T(4,128)S(1)}, u32[]{:S(2)}, u32[]{:S(2)}) collective-permute-start(f32[4,128]{1,0:T(4,128)S(1)} %get-tuple-element.69), channel_id=1, source_target_pairs={{0,48},{1,49},{2,50},{3,51},{4,52},{5,53},{6,54},{7,55},{8,56},{9,... | collective-permute-start | bytes 6152 | tf_op jit(solution)/shard_map/ppermute | solution.py:556
  (15 other events, 373.9 us)
where the time goes:
time: 202 us; the launch traced here: 201 us
  waiting for transfers between devices  116 us (57%)
  starting transfers between devices  58.3 us (29%)
  Pallas kernels  20.5 us (10%)
  local copies, waits for them, and re-layouts  3.9 us (2%)
  other arithmetic  2.23 us (1%)
    ppermute x27, waiting for transfers between devices, swap_blocks(): lax.ppermute(blocks[step], 'tm', ring(axis, step))  100 us
    ppermute x27, starting transfers between devices, swap_blocks(): lax.ppermute(blocks[step], 'tm', ring(axis, step))  49.2 us
    pallas_call x10, Pallas kernels, call(): pl.pallas_call(kernel, out_shape=[jax.ShapeDtypeStruct(s, F32) for s in o...  16.3 us
    ppermute x1, waiting for transfers between devices, on_device(): columns = lax.ppermute(normal, ('grp', 'tm'), pairs)  6.41 us
    ppermute x1, waiting for transfers between devices, on_device(): lax.ppermute(last, 'tm', [(d, (d + 1) % 64) for d in range(64)])  5.47 us
    pallas_call x1, Pallas kernels, on_device(): pl.pallas_call(correlation_kernel, grid=(8,), out_shape=jax.ShapeDtypeStr...  4.18 us
  transfers between devices with their start and end apart: 33, of which 22 were waited for; matrix products, arithmetic and copies ran while one was open for 2% of the time, Pallas kernels for 2%

commit v1 on v0

v1 whole, which is shorter than its diff:
```python
import functools
import math

import jax
import jax.numpy as jnp
import ml_dtypes
import numpy as np
from jax import lax
from jax.experimental import pallas as pl
from jax.experimental.pallas import tpu as pltpu
from jax.sharding import PartitionSpec as P

NT = 1 << 23
LOCAL = 1 << 17
HOPS = 128
HOP = 1024
W = 2048
BINS = 16384
TAPS = 512
BIN_WIDTH = 512
PEAK_AMPLITUDE = 2.0
KERR_GAIN = 0.5
RAMAN_SHARE = 0.18
RESPONSE_FAST = 12.2
RESPONSE_SLOW = 32.0
RESPONSE_SCALE = (12.2 * 12.2 + 32.0 * 32.0) / (12.2 * 32.0 * 32.0)
FLOOR_SHARE = 0.5
F32 = jnp.float32
BF16 = jnp.bfloat16
VMEM = pl.BlockSpec(memory_space=pltpu.VMEM)
HBM = pl.BlockSpec(memory_space=pltpu.HBM)
PARAMS = pltpu.CompilerParams(vmem_limit_bytes=48 * 1024 * 1024)


def split_const(table):
    table = np.asarray(table, np.float64)
    high = table.astype(ml_dtypes.bfloat16)
    low = (table - high.astype(np.float64)).astype(ml_dtypes.bfloat16)
    return np.stack([high, low])


def left_form(matrix):
    return np.block([[matrix.real, -matrix.imag], [matrix.imag, matrix.real]])


def right_form(matrix):
    return np.block([[matrix.real, matrix.imag], [-matrix.imag, matrix.real]])


def dft(size, sign):
    index = np.arange(size)
    return np.exp(sign * 2j * np.pi * (index[:, None] * index[None, :] % size) / size)


def row_order():
    row = np.arange(256)
    return row // 16 + 16 * (row % 16)


@functools.lru_cache(maxsize=None)
def tables():
    out = {}
    lag = np.arange(256)[None, :] - np.arange(256)[:, None]
    taps = np.arange(TAPS)
    response = RESPONSE_SCALE * np.exp(-taps / RESPONSE_SLOW) * np.sin(taps / RESPONSE_FAST)
    blocks = []
    for step in range(3):
        position = 256 * step + lag
        inside = (position >= 0) & (position < TAPS)
        blocks.append(np.where(inside, response[np.clip(position, 0, TAPS - 1)], 0.0))
    out["toeplitz"] = split_const(np.concatenate(blocks, 0))
    rows = np.arange(256).reshape(2, 16, 8).transpose(1, 0, 2).reshape(256)
    out["hop_fwd"] = split_const(left_form(dft(128, -1))[:, rows])
    cross = np.exp(-2j * np.pi * np.arange(128)[:, None] * np.arange(1024)[None, :] / LOCAL)
    out["cross"] = np.stack([cross.real, cross.imag]).astype(np.float32)
    out["sub_fwd"] = split_const(right_form(dft(256, -1)))
    out["sub_inv"] = split_const(left_form(dft(256, 1)[row_order()]) / NT)
    out["hop_inv"] = split_const(right_form(dft(128, 1)))
    order = np.arange(256).reshape(2, 2, 64).transpose(1, 0, 2).reshape(256)
    inner = np.arange(128)
    window = np.sin(np.pi / W * np.arange(W)) ** 2
    frames = []
    for a in range(16):
        block = np.exp(-2j * np.pi * (inner[:, None] * inner[None, :] % 128) / 128)
        block = block * window[a + 16 * inner][None, :]
        block = block * np.exp(-2j * np.pi * a * inner / 2048)[:, None]
        frames.append(left_form(block)[:, order])
    out["frames"] = split_const(np.stack(frames))
    return out


def halves(value):
    high = value.astype(BF16)
    low = (value - high.astype(F32)).astype(BF16)
    return high, low


def dims(contract):
    return (contract, ((), ()))


NN = ((1,), (0,))
NT_FORM = ((1,), (1,))


def dot_right(value, table, contract=NN):
    high, low = halves(value)
    dot = lambda a, b: lax.dot_general(a, b, dims(contract), preferred_element_type=F32)
    return dot(high, table[0]) + (dot(high, table[1]) + dot(low, table[0]))


def dot_left(table, value, contract=NN):
    high, low = halves(value)
    dot = lambda a, b: lax.dot_general(a, b, dims(contract), preferred_element_type=F32)
    return dot(table[0], high) + (dot(table[1], high) + dot(table[0], low))


def cmul(a, b):
    return (a[0] * b[0] - a[1] * b[1], a[0] * b[1] + a[1] * b[0])


def quad(x, sign):
    s02 = (x[0][0] + x[2][0], x[0][1] + x[2][1])
    d02 = (x[0][0] - x[2][0], x[0][1] - x[2][1])
    s13 = (x[1][0] + x[3][0], x[1][1] + x[3][1])
    d13 = (x[1][0] - x[3][0], x[1][1] - x[3][1])
    turned = (-sign * d13[1], sign * d13[0])
    return [
        (s02[0] + s13[0], s02[1] + s13[1]),
        (d02[0] + turned[0], d02[1] + turned[1]),
        (s02[0] - s13[0], s02[1] - s13[1]),
        (d02[0] - turned[0], d02[1] - turned[1]),
    ]


def powers(first):
    second = (first[0] * first[0] - first[1] * first[1], 2.0 * first[0] * first[1])
    return [None, first, second, cmul(first, second)]


def twist(values, factors):
    return [values[0]] + [cmul(values[k], factors[k]) for k in (1, 2, 3)]


def sincos(x):
    turns = jnp.floor(x * (2.0 / math.pi) + 0.5)
    rest = ((x - turns * 1.5703125) - turns * 4.837512969970703125e-4) - turns * 7.549789948768648e-8
    sq = rest * rest
    sine = rest + rest * sq * (
        -1.6666654611e-1 + sq * (8.3321608736e-3 + sq * -1.9515295891e-4)
    )
    cosine = 1.0 - 0.5 * sq + sq * sq * (
        4.166664568298827e-2 + sq * (-1.388731625493765e-3 + sq * 2.443315711809948e-5)
    )
    part = turns.astype(jnp.int32)
    odd = (part & 1) == 1
    s_val = jnp.where(odd, cosine, sine)
    c_val = jnp.where(odd, sine, cosine)
    s_val = jnp.where((part & 2) == 2, -s_val, s_val)
    c_val = jnp.where(((part + 1) & 2) == 2, -c_val, c_val)
    return s_val, c_val


def pulse_of(position):
    offset = (position - NT // 2).astype(F32) * (16.0 / NT)
    fall = jnp.exp(-jnp.abs(offset))
    return (2.0 * PEAK_AMPLITUDE) * fall / (1.0 + fall * fall)


SHIFT = {"x": 4, "y": 2, "z": 0}


def digits():
    tm = lax.axis_index("tm")
    return {axis: (tm >> SHIFT[axis]) & 3 for axis in SHIFT}


def iota(shape, axis):
    return lax.broadcasted_iota(jnp.int32, shape, axis)


def phasor(number, span, sign):
    sine, cosine = sincos((sign * 2.0 * math.pi / span) * number.astype(F32))
    return cosine, sine


def turn(number, span, sign):
    angle = sign * 2.0 * math.pi * number / span
    return math.cos(angle), math.sin(angle)


def eight(start):
    return pl.ds(pl.multiple_of(start, 8), 8)


def start_kernel(seed, halo, toep_hbm, out, buf, fre, toep, sem):
    copy = pltpu.make_async_copy(toep_hbm, toep, sem)
    copy.start()
    base = lax.axis_index("tm") * LOCAL
    buf[0:8, 512:1024] = jnp.broadcast_to(halo[...], (8, 512))

    def fill(step, carry):
        rows = eight(step * 8)
        row = iota((8, 1024), 0) + step * 8
        value = seed[0, rows, :] + pulse_of(base + row * 1024 + iota((8, 1024), 1))
        other = seed[1, rows, :]
        fre[rows, :] = value
        buf[eight(step * 8 + 8), :] = value * value + other * other
        return carry

    lax.fori_loop(0, 16, fill, 0)
    copy.wait()
    own = [halves(buf[8:136, 256 * e : 256 * e + 256]) for e in range(4)]
    back = {e: halves(buf[7:135, 256 * e : 256 * e + 256]) for e in (2, 3)}
    for e in range(4):
        total = None
        for step in range(3):
            at = e - step
            high, low = own[at] if at >= 0 else back[at + 4]
            t_high = toep[0, 256 * step : 256 * step + 256, :]
            t_low = toep[1, 256 * step : 256 * step + 256, :]
            term = (
                jnp.dot(high, t_high, preferred_element_type=F32)
                + jnp.dot(high, t_low, preferred_element_type=F32)
                + jnp.dot(low, t_high, preferred_element_type=F32)
            )
            total = term if total is None else total + term
        lanes = slice(256 * e, 256 * e + 256)
        phase = KERR_GAIN * ((1.0 - RAMAN_SHARE) * buf[8:136, lanes] + RAMAN_SHARE * total)
        sine, cosine = sincos(phase)
        value = fre[:, lanes]
        other = seed[1, :, lanes]
        out[:, 0:8, lanes] = (value * cosine - other * sine).reshape(16, 8, 256)
        out[:, 8:16, lanes] = (value * sine + other * cosine).reshape(16, 8, 256)


def sixteen(x, sign):
    inner = [quad([x[4 * a1 + a0] for a1 in range(4)], sign) for a0 in range(4)]
    out = []
    for c0 in range(4):
        row = [inner[a0][c0] for a0 in range(4)]
        row = [cmul(v, turn(a0 * c0, 16, sign)) if a0 * c0 else v for a0, v in enumerate(row)]
        out.append(quad(row, sign))
    return out


def many_powers(first):
    out = [None, first]
    for k in range(2, 16):
        out.append(cmul(out[k // 2], out[k - k // 2]))
    return out


def lanes_at(step):
    return pl.ds(pl.multiple_of(step * 128, 128), 128)


def fwd_kernel(blocks, o0, o1, o2, o3, scratch):
    place = digits()
    block = 4 * place["x"] + place["y"]
    number = place["z"] * LOCAL + (8 * block + iota((8, 128), 0)) * 1024 + iota((8, 128), 1)
    forward = turn(128, NT, -1)

    def body(step, factor):
        lanes = lanes_at(step)
        y = sixteen([(blocks[t, 0:8, lanes], blocks[t, 8:16, lanes]) for t in range(16)], -1.0)
        factors = many_powers(factor)
        for c0 in range(4):
            slot = (c0 - place["z"]) & 3
            for c1 in range(4):
                value = y[c0][c1]
                if c0 + c1:
                    value = cmul(value, factors[c0 + 4 * c1])
                scratch[slot, c1, 0:8, lanes] = value[0]
                scratch[slot, c1, 8:16, lanes] = value[1]
        for j, out in enumerate((o0, o1, o2, o3)):
            out[:, :, lanes] = scratch[j, :, :, lanes]
        return cmul(factor, forward)

    lax.fori_loop(0, 8, body, phasor(number, NT, -1))


def mid_kernel(r0, r1, r2, r3, out):
    place = digits()
    block = 4 * place["x"] + place["y"]
    number = (8 * block + iota((8, 128), 0)) * 1024 + iota((8, 128), 1) + place["z"] * LOCAL
    forward = turn(128, 4 * LOCAL, -1)

    def body(step, factor):
        lanes = lanes_at(step)
        factors = powers(factor)
        for kk in range(4):
            x = [(r[kk, 0:8, lanes], r[kk, 8:16, lanes]) for r in (r0, r1, r2, r3)]
            for ka, value in enumerate(twist(quad(x, 1.0), factors)):
                out[4 * ka + kk, 0:8, lanes] = value[0]
                out[4 * ka + kk, 8:16, lanes] = value[1]
        return cmul(factor, forward)

    lax.fori_loop(0, 8, body, phasor(number, 4 * LOCAL, -1))


def spectrum_kernel(
    blocks, hop, cross, mat, disp, inv, unhop, out, wide, work, back, rows_w, bins, flip, flat
):
    for part in range(4):
        lanes = slice(256 * part, 256 * part + 256)
        wide[:, lanes] = dot_left(hop, blocks[:, :, lanes].reshape(256, 256))
    lane_f = powers(phasor(iota((8, 256), 1), 1024, -1))

    def body(step, carry):
        rows, low_rows = eight(step * 8), eight(step * 8 + 128)
        x = []
        for part in range(4):
            lanes = slice(256 * part, 256 * part + 256)
            factor = (cross[0, rows, lanes], cross[1, rows, lanes])
            x.append(cmul((wide[rows, lanes], wide[low_rows, lanes]), factor))
        y = twist(quad(x, -1.0), lane_f)
        for k in range(4):
            at = eight(step * 8 + 128 * k)
            work[at, 0:256] = y[k][0]
            work[at, 256:512] = y[k][1]
        return carry

    lax.fori_loop(0, 16, body, 0)
    bins[64:128, :] = jnp.zeros((64, 256), F32)
    for k in range(4):
        rows = slice(128 * k, 128 * k + 128)
        got = dot_right(work[rows, :], mat)
        re, im = got[:, :256], got[:, 256:]
        power = (re * re + im * im).reshape(16, 8, 256)
        bins[16 * k : 16 * k + 16, :] = jnp.sum(power, axis=1) * (1.0 / (NT * BIN_WIDTH))
        re, im = cmul((re, im), (disp[0, rows, :], disp[1, rows, :]))
        work[rows, 0:256] = re
        work[rows, 256:512] = im
    for half in range(2):
        flip[128 * half : 128 * half + 128, :] = bins[:, 128 * half : 128 * half + 128].T
    flat[...] = flip[pl.ds(0, 128, stride=2), :] + pltpu.roll(flip[pl.ds(1, 128, stride=2), :], 64, 1)
    for dest in range(16):
        out[dest, 128:136, :] = flat[8 * dest : 8 * dest + 8, :]
    back[...] = dot_left(inv, work[...], NT_FORM)
    first = phasor(16 * iota((8, 128), 0), 1024, 1)
    forward, half_turn = turn(1, 1024, 1), turn(128, 1024, 1)
    freq = iota((8, 128), 1)
    cross_first = phasor(16 * iota((8, 128), 0) * freq, LOCAL, 1)
    cross_step, cross_half = phasor(freq, LOCAL, 1), phasor(128 * freq, LOCAL, 1)
    cross_part = powers(phasor(256 * freq, LOCAL, 1))

    def tail(a, carry):
        factor, other = carry
        for half in range(2):
            rows, low_rows = eight(a * 16 + 8 * half), eight(a * 16 + 8 * half + 256)
            x = [
                (back[rows, 128 * k : 128 * k + 128], back[low_rows, 128 * k : 128 * k + 128])
                for k in range(4)
            ]
            now = cmul(factor, half_turn) if half else factor
            after = cmul(other, cross_half) if half else other
            y = twist(quad(twist(x, powers(now)), 1.0), cross_part)
            for part in range(4):
                value = cmul(y[part], after)
                at = eight(a * 64 + part * 16 + 8 * half)
                rows_w[at, 0:128] = value[0]
                rows_w[at, 128:256] = value[1]
        return cmul(factor, forward), cmul(other, cross_step)

    lax.fori_loop(0, 16, tail, (first, cross_first))
    for part in range(4):
        got = dot_right(rows_w[256 * part : 256 * part + 256, :], unhop)
        for a in range(4):
            out[4 * part + a, 0:64, :] = got[64 * a : 64 * a + 64, 0:128]
            out[4 * part + a, 64:128, :] = got[64 * a : 64 * a + 64, 128:256]


def unmid_kernel(blocks, o0, o1, o2, o3):
    place = digits()
    outs = (o0, o1, o2, o3)
    total = blocks[0, 128:136, :]
    for k in range(1, 16):
        total = total + blocks[k, 128:136, :]
    for out in outs:
        out[512:520, :] = total
    block = 4 * place["x"] + place["y"]
    number = block + 16 * iota((8, 128), 0) + 1024 * iota((8, 128), 1) + place["z"] * LOCAL
    forward = turn(128, 4 * LOCAL, 1)

    def body(step, factor):
        rows, low_rows = eight(step * 8), eight(step * 8 + 64)
        factors = powers(factor)
        for kk in range(4):
            x = [(blocks[4 * ka + kk, rows, :], blocks[4 * ka + kk, low_rows, :]) for ka in range(4)]
            for out, value in zip(outs, quad(twist(x, factors), 1.0)):
                out[eight(step * 8 + 128 * kk), :] = value[0]
                out[eight(step * 8 + 128 * kk + 64), :] = value[1]
        return cmul(factor, forward)

    lax.fori_loop(0, 8, body, phasor(number, 4 * LOCAL, 1))


def inv_kernel(r0, r1, r2, r3, out, bins, scratch):
    place = digits()
    blocks = (r0, r1, r2, r3)
    bins[...] = (r0[512:520, :] + r1[512:520, :]) + (r2[512:520, :] + r3[512:520, :])
    block = 4 * place["x"] + place["y"]
    number = place["z"] * LOCAL + block + 16 * iota((8, 128), 0) + 1024 * iota((8, 128), 1)
    forward = turn(128, NT, 1)

    def body(step, factor):
        for kk in range(4):
            for low in (128 * kk, 128 * kk + 64):
                rows = eight(step * 8 + low)
                for s in range(4):
                    scratch[(place["z"] - s) & 3, rows, :] = blocks[s][rows, :]
        factors = many_powers(factor)
        x = [None] * 16
        for c0 in range(4):
            for c1 in range(4):
                value = (
                    scratch[c0, eight(step * 8 + 128 * c1), :],
                    scratch[c0, eight(step * 8 + 128 * c1 + 64), :],
                )
                x[4 * c1 + c0] = cmul(value, factors[c0 + 4 * c1]) if c0 + c1 else value
        y = sixteen(x, 1.0)
        for a0 in range(4):
            for a1 in range(4):
                out[4 * a1 + a0, eight(step * 8), :] = y[a0][a1][0]
                out[4 * a1 + a0, eight(step * 8 + 64), :] = y[a0][a1][1]
        return cmul(factor, forward)

    lax.fori_loop(0, 8, body, phasor(number, NT, 1))


def frames_kernel(blocks, tail, mat, out, got):
    columns = tail[...].T
    lane = iota((128, 128), 1)
    for a in range(16):
        here = blocks[a]
        after = jnp.where(lane == 127, columns[:, a : a + 1], pltpu.roll(here, 127, 1))
        got[a] = dot_left(mat.at[:, a], jnp.concatenate([here, after], axis=0))

    def body(step, carry):
        rows, low_rows = eight(step * 8), eight(step * 8 + 128)
        y = sixteen([(got[a, rows, :], got[a, low_rows, :]) for a in range(16)], -1.0)
        for c0 in range(4):
            for c1 in range(4):
                value = y[c0][c1]
                got[c0 + 4 * c1, rows, :] = (value[0] * value[0] + value[1] * value[1]) * (1.0 / W)
        return carry

    lax.fori_loop(0, 16, body, 0)
    for c in range(16):
        out[:, 128 * c : 128 * c + 128] = got[c, 0:128, :].T


def normal_kernel(b0, b1, b2, b3, out):
    blocks = [b[...] for b in (b0, b1, b2, b3)]
    total = (blocks[0] + blocks[1]) + (blocks[2] + blocks[3])
    average = total * 0.25
    centred = [b - average for b in blocks]
    sq = [c * c for c in centred]
    variance = ((sq[0] + sq[1]) + (sq[2] + sq[3])) * 0.25
    spread = jnp.sqrt(jnp.maximum(variance, FLOOR_SHARE * average * average / BIN_WIDTH))
    grp = lax.axis_index("grp")
    for step in range(4):
        out[(grp - step) & 3] = centred[step] / spread


def correlation_kernel(own, c0, c1, c2, c3, out, side, pad, cols):
    step = pl.program_id(0)

    @pl.when(step == 0)
    def _():
        place = digits()
        at = place["z"] * 2
        for s, value in enumerate((c0, c1, c2, c3)):
            cols[:, eight(((place["y"] - s) & 3) * 8), :] = value[...]
        pad[...] = jnp.zeros((128, 128), F32)
        for r in range(4):
            for half in range(2):
                pad[2 * r + half : 2 * r + half + 1, :] = own[r, pl.ds(at + half, 1), :] * 0.25
        flipped = pad[...].T
        for r in range(4):
            for half in range(2):
                column = flipped[:, 2 * r + half : 2 * r + half + 1]
                side[r, 128 * half : 128 * half + 128, :] = jnp.broadcast_to(column, (128, 128))

    for group in range(4):
        rows = eight(step * 32 + group * 8)
        factors = [side[r, rows, :] for r in range(4)]
        for k in range(32):
            total = factors[0] * cols[0, k : k + 1, :]
            for r in range(1, 4):
                total = total + factors[r] * cols[r, k : k + 1, :]
            out[8 * group : 8 * group + 8, 128 * k : 128 * k + 128] = total


def call(kernel, outs, scratch, *args, flops=1 << 20, specs=None):
    size = sum(int(np.prod(s)) * 4 for s in outs)
    return pl.pallas_call(
        kernel,
        out_shape=[jax.ShapeDtypeStruct(s, F32) for s in outs],
        in_specs=specs or [VMEM] * len(args),
        out_specs=[VMEM] * len(outs),
        scratch_shapes=[pltpu.VMEM(s, F32) if isinstance(s, tuple) else s for s in scratch],
        compiler_params=PARAMS,
        cost_estimate=pl.CostEstimate(flops=flops, bytes_accessed=2 * size, transcendentals=0),
    )(*args)


def ring(axis, step):
    stride = 1 << SHIFT[axis]
    pairs = []
    for device in range(64):
        digit = device // stride % 4
        pairs.append((device, device + ((digit + step) % 4 - digit) * stride))
    return pairs


def swap_blocks(blocks, axis):
    moved = {step: lax.ppermute(blocks[step], "tm", ring(axis, step)) for step in (1, 3, 2)}
    return [blocks[0], moved[1], moved[2], moved[3]]


def swap_plane(value):
    groups = [[16 * x + 4 * y + z for x in range(4) for y in range(4)] for z in range(4)]
    return lax.all_to_all(
        value, "tm", split_axis=0, concat_axis=0, axis_index_groups=groups, tiled=True
    )


FWD = (16, 16, 1024)
INV = (16, 128, 128)


def on_device(seed_field):
    table = tables()
    tm = lax.axis_index("tm")
    ix, iy, iz = tm // 16, tm // 4 % 4, tm % 4

    seed = seed_field.reshape(2, HOPS, HOP)
    last = seed_field[0, :, LOCAL - TAPS :].reshape(8, 128)
    last = lax.ppermute(last, "tm", [(d, (d + 1) % 64) for d in range(64)]).reshape(2, TAPS)
    spots = (tm * LOCAL - TAPS + jnp.arange(TAPS, dtype=jnp.int32)) & (NT - 1)
    halo = ((last[0] + pulse_of(spots)) ** 2 + last[1] ** 2)[None, :]

    value = call(
        start_kernel, [FWD],
        [(136, 1024), (128, 1024), pltpu.VMEM((2, 768, 256), BF16), pltpu.SemaphoreType.DMA],
        seed, halo, table["toeplitz"], specs=[VMEM, VMEM, HBM],
    )[0]
    value = swap_plane(value)
    blocks = call(fwd_kernel, [(4, 16, 1024)] * 4, [(4, 4, 16, 1024)], value)
    blocks = swap_blocks(blocks, "z")
    value = call(mid_kernel, [FWD], [], *blocks)[0]
    value = swap_plane(value)
    number = (
        (iz + 4 * iy + 16 * ix)
        + 8192 * jnp.arange(4, dtype=jnp.int32)[:, None, None]
        + 64 * jnp.arange(128, dtype=jnp.int32)[None, :, None]
        + 32768 * jnp.arange(256, dtype=jnp.int32)[None, None, :]
    ).reshape(512, 256)
    freq = jnp.where(number < NT // 2, number, number - NT)
    angle = (2.0 * math.pi / (1 << 28)) * (freq * freq & ((1 << 28) - 1)).astype(F32)
    disp = jnp.stack([jnp.cos(angle), jnp.sin(angle)])
    value = call(
        spectrum_kernel, [(16, 136, 128)],
        [(256, 1024), (512, 512), (512, 512), (1024, 256), (128, 256), (256, 128), (128, 128)],
        value, table["hop_fwd"], table["cross"], table["sub_fwd"], disp, table["sub_inv"], table["hop_inv"],
    )[0]
    value = swap_plane(value)
    blocks = call(unmid_kernel, [(520, 128)] * 4, [], value)
    blocks = swap_blocks(blocks, "z")
    value, bins = call(inv_kernel, [INV, (8, 128)], [(4, 512, 128)], *blocks)
    value = swap_plane(value)

    tail = lax.ppermute(value[:, :, 0], "tm", [((d + 1) % 64, d) for d in range(64)])

    alike = [bins] + [
        lax.ppermute(bins, "grp", [(g, (g + step) % 4) for g in range(4)]) for step in (1, 2, 3)
    ]
    normal = call(normal_kernel, [(4, 8, 128)], [], *alike)[0]
    pairs = []
    for g in range(4):
        for d in range(64):
            pairs.append((g * 64 + d, d // 16 * 64 + g * 16 + d % 16))
    columns = lax.ppermute(normal, ("grp", "tm"), pairs)
    columns = [columns] + [lax.ppermute(columns, "tm", ring("y", step)) for step in (1, 2, 3)]

    correlation = pl.pallas_call(
        correlation_kernel,
        grid=(8,),
        out_shape=jax.ShapeDtypeStruct((256, 4096), F32),
        in_specs=[pl.BlockSpec((4, 8, 128), lambda i: (0, 0, 0))] * 5,
        out_specs=pl.BlockSpec((32, 4096), lambda i: (i, 0)),
        scratch_shapes=[
            pltpu.VMEM((4, 256, 128), F32), pltpu.VMEM((128, 128), F32), pltpu.VMEM((4, 32, 128), F32)
        ],
        compiler_params=PARAMS,
        cost_estimate=pl.CostEstimate(flops=1 << 23, bytes_accessed=1 << 22, transcendentals=0),
    )(normal, *columns)
    spectrogram = call(
        frames_kernel, [(HOPS, W)], [(16, 256, 128)], value, tail, table["frames"]
    )[0]
    return spectrogram[None], correlation


def solution(mesh):
    return jax.shard_map(
        on_device,
        mesh=mesh,
        in_specs=(P("grp", None, "tm"),),
        out_specs=(P("grp", "tm", None), P("tm", "grp")),
        check_vma=False,
    )
```

time: 202 us -> 175 us (0.87)
  waiting for transfers between devices: 116 us -> 55.7 us
  blocking collectives: 0 us -> 39.6 us
  starting transfers between devices: 58.3 us -> 45.2 us
  local copies, waits for them, and re-layouts: 3.9 us -> 10.6 us
    ppermute x27 -> x6, waiting for transfers between devices: 100 us -> 29 us  [swap_blocks(): lax.ppermute(blocks[step], 'tm', ring(axis, step))]
    all_to_all x0 -> x2, blocking collectives: none -> 39.6 us  [swap_plane(): lax.all_to_all(value, 'tm', split_axis=0, concat_axis=0, axis_index_group...]
    ppermute x27 -> x6, starting transfers between devices: 49.2 us -> 16.9 us  [swap_blocks(): lax.ppermute(blocks[step], 'tm', ring(axis, step))]
    all_to_all x0 -> x2, waiting for transfers between devices: none -> 12.5 us  [swap_plane(): lax.all_to_all(value, 'tm', split_axis=0, concat_axis=0, axis_index_group...]
    all_to_all x0 -> x2, starting transfers between devices: none -> 11.9 us  [swap_plane(): lax.all_to_all(value, 'tm', split_axis=0, concat_axis=0, axis_index_group...]
    ppermute x1 -> x4, starting transfers between devices: 3.03 us -> 9.3 us  [the longest x1 4.9 us: on_device(): lax.ppermute(value[:, :, 0], 'tm', [((d + 1) % 64, d) for d in range(64)])]
    unnamed x13 -> x15, local copies, waits for them, and re-layouts: 2.71 us -> 8.28 us
    pallas_call x10 -> x8, Pallas kernels: 16.3 us -> 14.3 us  [call(): pl.pallas_call(kernel, out_shape=[jax.ShapeDtypeStruct(s, F32) for s in o...]
  transfers between devices with their start and end apart: 33 -> 17, of which waited for: 22 -> 10; matrix products, arithmetic and copies ran while one was open for 2% -> 2% of each run, Pallas kernels for 2% -> 2%
where the time goes in v1:
time: 175 us; the launch traced here: 173 us
  waiting for transfers between devices  55.7 us (32%)
  starting transfers between devices  45.2 us (26%)
  blocking collectives  39.6 us (23%)
  Pallas kernels  18.5 us (11%)
  local copies, waits for them, and re-layouts  10.6 us (6%)
  other arithmetic  2.22 us (1%)
    all_to_all x2, blocking collectives, swap_plane(): lax.all_to_all(value, 'tm', split_axis=0, concat_axis=0, axis_index_group...  39.6 us
    ppermute x6, waiting for transfers between devices, swap_blocks(): lax.ppermute(blocks[step], 'tm', ring(axis, step))  29 us
    ppermute x6, starting transfers between devices, swap_blocks(): lax.ppermute(blocks[step], 'tm', ring(axis, step))  16.9 us
    pallas_call x8, Pallas kernels, call(): pl.pallas_call(kernel, out_shape=[jax.ShapeDtypeStruct(s, F32) for s in o...  14.3 us
    all_to_all x2, waiting for transfers between devices, swap_plane(): lax.all_to_all(value, 'tm', split_axis=0, concat_axis=0, axis_index_group...  12.5 us
    all_to_all x2, starting transfers between devices, swap_plane(): lax.all_to_all(value, 'tm', split_axis=0, concat_axis=0, axis_index_group...  11.9 us
    unnamed x15, local copies, waits for them, and re-layouts  8.28 us
    ppermute x1, waiting for transfers between devices, on_device(): columns = lax.ppermute(normal, ('grp', 'tm'), pairs)  5.68 us
  transfers between devices with their start and end apart: 17, of which 10 were waited for; matrix products, arithmetic and copies ran while one was open for 2% of the time, Pallas kernels for 2%

profile of v1, /device:TPU:4, one launch (start us, length us, event | category | flops | bytes accessed | tf_op | source)
XLA Modules:
  0.0 172.6 jit_solution(6564425523231740777)
XLA Ops:
  1.3 3.3 %collective-permute-start = (f32[8,128]{1,0:T(8,128)S(1)}, f32[8,128]{1,0:T(8,128)S(1)}, u32[]{:S(2)}, u32[]{:S(2)}) collective-permute-start(f32[8,128]{1,0:T(8,128)S(1)} %reshape_squeeze.3), channel_id=1, source_target_pairs={{0,1},{1,2},{2,3},{3,4},{4,5},{5,6},{6,7},{7,8},{8,9},{9,10},{10,1... | collective-permute-start | bytes 12296 | tf_op jit(solution)/shard_map/ppermute | solution.py:541
  6.2 5.5 %collective-permute-done = f32[8,128]{1,0:T(8,128)S(1)} collective-permute-done((f32[8,128]{1,0:T(8,128)S(1)}, f32[8,128]{1,0:T(8,128)S(1)}, u32[]{:S(2)}, u32[]{:S(2)}) %collective-permute-start) | collective-permute-done | bytes 4128 | tf_op jit(solution)/shard_map/ppermute | solution.py:541
  12.8 2.2 %shard_map.95 = f32[16,16,1024]{2,1,0:T(8,128)S(1)} custom-call(f32[2,128,1024]{2,1,0:T(8,128)S(1)} %bitcast.14, f32[1,512]{1,0:T(1,128)S(1)} %multiply_add_fusion.halo, bf16[2,768,256]{2,1,0:T(8,128)(2,1)S(1)} %copy-done.4), custom_call_target="tpu_custom_call" | custom-call | flops 1048576 | bytes 2097152 | tf_op jit(solution)/shard_map/pallas_call | solution.py:498
  15.0 19.4 %all_to_all.20.blocks = f32[16,16,1024]{2,1,0:T(8,128)S(1)} all-to-all(f32[16,16,1024]{2,1,0:T(8,128)S(1)} %shard_map.95), channel_id=1, replica_groups={{0,4,8,12,16,20,24,28,32,36,40,44,48,52,56,60},{1,5,9,13,17,21,25,29,33..., dimensions={0} | all-to-all | bytes 2097152 | tf_op jit(solution)/shard_map/all_to_all | solution.py:525
  36.7 2.9 %collective-permute-start.2 = (f32[4,16,1024]{2,1,0:T(8,128)S(1)}, f32[4,16,1024]{2,1,0:T(8,128)S(1)}, u32[]{:S(2)}, u32[]{:S(2)}) collective-permute-start(f32[4,16,1024]{2,1,0:T(8,128)S(1)} %get-tuple-element.14), channel_id=1, source_target_pairs={{0,2},{1,3},{2,0},{3,1},{4,6},{5,7},{6,4},{7,5},{8,10},{9,11},{10,... | collective-permute-start | bytes 786440 | tf_op jit(solution)/shard_map/ppermute | solution.py:519
  39.5 3.9 %collective-permute-start.3 = (f32[4,16,1024]{2,1,0:T(8,128)S(1)}, f32[4,16,1024]{2,1,0:T(8,128)S(1)}, u32[]{:S(2)}, u32[]{:S(2)}) collective-permute-start(f32[4,16,1024]{2,1,0:T(8,128)S(1)} %get-tuple-element.15), channel_id=1, source_target_pairs={{0,3},{1,0},{2,1},{3,2},{4,7},{5,4},{6,5},{7,6},{8,11},{9,8},{10,9... | collective-permute-start | bytes 786440 | tf_op jit(solution)/shard_map/ppermute | solution.py:519
  43.4 13.2 %collective-permute-done.1.r1 = f32[4,16,1024]{2,1,0:T(8,128)S(1)} collective-permute-done((f32[4,16,1024]{2,1,0:T(8,128)S(1)}, f32[4,16,1024]{2,1,0:T(8,128)S(1)}, u32[]{:S(2)}, u32[]{:S(2)}) %collective-permute-start.1) | collective-permute-done | bytes 262176 | tf_op jit(solution)/shard_map/ppermute | solution.py:519
  56.7 5.6 %collective-permute-done.3.r3 = f32[4,16,1024]{2,1,0:T(8,128)S(1)} collective-permute-done((f32[4,16,1024]{2,1,0:T(8,128)S(1)}, f32[4,16,1024]{2,1,0:T(8,128)S(1)}, u32[]{:S(2)}, u32[]{:S(2)}) %collective-permute-start.3) | collective-permute-done | bytes 262176 | tf_op jit(solution)/shard_map/ppermute | solution.py:519
  63.5 6.2 %all-to-all-start.1 = ((f32[16,16,1024]{2,1,0:T(8,128)}), f32[16,16,1024]{2,1,0:T(8,128)S(1)}, u32[]{:S(2)}, u32[]{:S(2)}) async-start(f32[16,16,1024]{2,1,0:T(8,128)} %shard_map.97), calls=%async_computation.1 | async-start | bytes 2097152 | tf_op jit(solution)/shard_map/all_to_all | solution.py:525
  71.9 12.5 %all-to-all-done.1.blocks = f32[16,16,1024]{2,1,0:T(8,128)S(1)} async-done(((f32[16,16,1024]{2,1,0:T(8,128)}), f32[16,16,1024]{2,1,0:T(8,128)S(1)}, u32[]{:S(2)}, u32[]{:S(2)}) %all-to-all-start.1) | async-done | bytes 1048608 | tf_op jit(solution)/shard_map/all_to_all | solution.py:525
  87.8 5.0 %shard_map.98 = f32[16,136,128]{2,1,0:T(8,128)} custom-call(f32[16,16,1024]{2,1,0:T(8,128)S(1)} %all-to-all-done.1.blocks, bf16[2,256,256]{2,1,0:T(8,128)(2,1)S(1)} %copy-done.6, f32[2,128,1024]{2,1,0:T(8,128)S(1)} %copy-done.3, bf16[2,512,512]{2,1,0:T(8,128)(2,1)S(1)} %copy-done.2, f32[2,512,256]{2,1,0:T(8,128)S(1)} %pad_maximum_fusion.disp, ...), custom_call_target="tpu_custom_call" | custom-call | flops 1048576 | bytes 2228224 | tf_op jit(solution)/shard_map/pallas_call | solution.py:498
  92.9 20.2 %all_to_all.21.blocks = f32[16,136,128]{2,1,0:T(8,128)S(1)} all-to-all(f32[16,136,128]{2,1,0:T(8,128)} %shard_map.98), channel_id=1, replica_groups={{0,4,8,12,16,20,24,28,32,36,40,44,48,52,56,60},{1,5,9,13,17,21,25,29,33..., dimensions={0} | all-to-all | bytes 2228224 | tf_op jit(solution)/shard_map/all_to_all | solution.py:525
  113.3 2.9 %collective-permute-start.4 = (f32[520,128]{1,0:T(8,128)S(1)}, f32[520,128]{1,0:T(8,128)S(1)}, u32[]{:S(2)}, u32[]{:S(2)}) collective-permute-start(f32[520,128]{1,0:T(8,128)S(1)} %get-tuple-element.17), channel_id=1, source_target_pairs={{0,1},{1,2},{2,3},{3,0},{4,5},{5,6},{6,7},{7,4},{8,9},{9,10},{10,1... | collective-permute-start | bytes 798728 | tf_op jit(solution)/shard_map/ppermute | solution.py:519
  116.2 2.8 %collective-permute-start.5 = (f32[520,128]{1,0:T(8,128)S(1)}, f32[520,128]{1,0:T(8,128)S(1)}, u32[]{:S(2)}, u32[]{:S(2)}) collective-permute-start(f32[520,128]{1,0:T(8,128)S(1)} %get-tuple-element.18), channel_id=1, source_target_pairs={{0,2},{1,3},{2,0},{3,1},{4,6},{5,7},{6,4},{7,5},{8,10},{9,11},{10,... | collective-permute-start | bytes 798728 | tf_op jit(solution)/shard_map/ppermute | solution.py:519
  119.0 3.1 %collective-permute-start.6 = (f32[520,128]{1,0:T(8,128)S(1)}, f32[520,128]{1,0:T(8,128)S(1)}, u32[]{:S(2)}, u32[]{:S(2)}) collective-permute-start(f32[520,128]{1,0:T(8,128)S(1)} %get-tuple-element.19), channel_id=1, source_target_pairs={{0,3},{1,0},{2,1},{3,2},{4,7},{5,4},{6,5},{7,6},{8,11},{9,8},{10,9... | collective-permute-start | bytes 798728 | tf_op jit(solution)/shard_map/ppermute | solution.py:519
  122.1 8.0 %collective-permute-done.4.r1 = f32[520,128]{1,0:T(8,128)S(1)} collective-permute-done((f32[520,128]{1,0:T(8,128)S(1)}, f32[520,128]{1,0:T(8,128)S(1)}, u32[]{:S(2)}, u32[]{:S(2)}) %collective-permute-start.4) | collective-permute-done | bytes 266272 | tf_op jit(solution)/shard_map/ppermute | solution.py:519
  134.1 5.7 %all-to-all-start.3 = ((f32[16,128,128]{1,2,0:T(8,128)}), f32[16,128,128]{1,2,0:T(8,128)S(1)}, u32[]{:S(2)}, u32[]{:S(2)}) async-start(f32[16,128,128]{1,2,0:T(8,128)} %copy.12), calls=%async_computation.3 | async-start | bytes 2097152 | tf_op jit(solution)/shard_map/all_to_all | solution.py:525
  141.2 2.3 %collective-permute-done.9.b2 = f32[8,128]{1,0:T(8,128)S(1)} collective-permute-done((f32[8,128]{1,0:T(8,128)S(1)}, f32[8,128]{1,0:T(8,128)S(1)}, u32[]{:S(2)}, u32[]{:S(2)}) %collective-permute-start.9) | collective-permute-done | bytes 4128 | tf_op jit(solution)/shard_map/ppermute | solution.py:578
  144.2 2.5 %collective-permute-start.11 = (f32[4,8,128]{2,1,0:T(8,128)S(1)}, f32[4,8,128]{2,1,0:T(8,128)S(1)}, u32[]{:S(2)}, u32[]{:S(2)}) collective-permute-start(f32[4,8,128]{2,1,0:T(8,128)S(1)} %shard_map.102.own), channel_id=1, source_target_pairs={{0,0},{1,1},{2,2},{3,3},{4,4},{5,5},{6,6},{7,7},{8,8},{9,9},{10,10... | collective-permute-start | bytes 49160 | tf_op jit(solution)/shard_map/ppermute | solution.py:585
  146.7 5.7 %collective-permute-done.11.c0 = f32[4,8,128]{2,1,0:T(8,128)S(1)} collective-permute-done((f32[4,8,128]{2,1,0:T(8,128)S(1)}, f32[4,8,128]{2,1,0:T(8,128)S(1)}, u32[]{:S(2)}, u32[]{:S(2)}) %collective-permute-start.11) | collective-permute-done | bytes 16416 | tf_op jit(solution)/shard_map/ppermute | solution.py:585
  152.4 2.7 %collective-permute-start.14 = (f32[4,8,128]{2,1,0:T(8,128)S(1)}, f32[4,8,128]{2,1,0:T(8,128)S(1)}, u32[]{:S(2)}, u32[]{:S(2)}) collective-permute-start(f32[4,8,128]{2,1,0:T(8,128)S(1)} %collective-permute-done.11.c0), channel_id=1, source_target_pairs={{0,12},{1,13},{2,14},{3,15},{4,0},{5,1},{6,2},{7,3},{8,4},{9,5},{1... | collective-permute-start | bytes 49160 | tf_op jit(solution)/shard_map/ppermute | solution.py:586
  156.8 4.9 %collective-permute-start.7 = (f32[16,128]{1,0:T(8,128)S(1)}, f32[16,128]{1,0:T(8,128)S(1)}, u32[]{:S(2)}, u32[]{:S(2)}) collective-permute-start(f32[16,128]{1,0:T(8,128)S(1)} %bitcast.18), channel_id=1, source_target_pairs={{1,0},{2,1},{3,2},{4,3},{5,4},{6,5},{7,6},{8,7},{9,8},{10,9},{11,1... | collective-permute-start | bytes 24584 | tf_op jit(solution)/shard_map/ppermute | solution.py:575
  161.7 4.2 %shard_map.103 = f32[256,4096]{1,0:T(8,128)} custom-call(f32[4,8,128]{2,1,0:T(8,128)S(1)} %shard_map.102.own, f32[4,8,128]{2,1,0:T(8,128)S(1)} %collective-permute-done.11.c0, f32[4,8,128]{2,1,0:T(8,128)S(1)} %collective-permute-done.12.c1, f32[4,8,128]{2,1,0:T(8,128)S(1)} %collective-permute-done.13.c2, f32[4,8,128]{2,1,0:T(8,128)S(1)} %collective-permute-done.14.c3), custom_call_target="tpu_custom_call" | custom-call | flops 8388608 | bytes 4194304 | tf_op jit(solution)/shard_map/pallas_call | solution.py:588
  168.5 4.2 %shard_map.101 = f32[128,2048]{1,0:T(8,128)} custom-call(f32[16,128,128]{2,1,0:T(8,128)S(1)} %copy.14.blocks, f32[16,128]{1,0:T(8,128)S(1)} %collective-permute-done.7.tail, bf16[2,16,256,256]{3,2,1,0:T(8,128)(2,1)S(1)} %copy-done), custom_call_target="tpu_custom_call" | custom-call | flops 1048576 | bytes 2097152 | tf_op jit(solution)/shard_map/pallas_call | solution.py:498
  (50 shorter events, 23.1 us)
Async XLA Ops:
  1.3 10.3 %collective-permute-start = (f32[8,128]{1,0:T(8,128)S(1)}, f32[8,128]{1,0:T(8,128)S(1)}, u32[]{:S(2)}, u32[]{:S(2)}) collective-permute-start(f32[8,128]{1,0:T(8,128)S(1)} %reshape_squeeze.3), channel_id=1, source_target_pairs={{0,1},{1,2},{2,3},{3,4},{4,5},{5,6},{6,7},{7,8},{8,9},{9,10},{10,1... | collective-permute-start | bytes 12296 | tf_op jit(solution)/shard_map/ppermute | solution.py:541
  11.7 1.1 copy-start.4
  34.5 50.0 %copy-start.1 = (bf16[2,512,512]{2,1,0:T(8,128)(2,1)S(1)}, bf16[2,512,512]{2,1,0:T(8,128)(2,1)}, u32[]{:S(2)}) copy-start(bf16[2,512,512]{2,1,0:T(8,128)(2,1)} %constant.94.clone.inv) | copy-start | bytes 3145732
  34.5 50.0 %copy-start.5 = (bf16[2,256,256]{2,1,0:T(8,128)(2,1)S(1)}, bf16[2,256,256]{2,1,0:T(8,128)(2,1)}, u32[]{:S(2)}) copy-start(bf16[2,256,256]{2,1,0:T(8,128)(2,1)} %constant.95.clone.unhop) | copy-start | bytes 786436
  35.2 21.4 %collective-permute-start.1 = (f32[4,16,1024]{2,1,0:T(8,128)S(1)}, f32[4,16,1024]{2,1,0:T(8,128)S(1)}, u32[]{:S(2)}, u32[]{:S(2)}) collective-permute-start(f32[4,16,1024]{2,1,0:T(8,128)S(1)} %get-tuple-element.13), channel_id=1, source_target_pairs={{0,1},{1,2},{2,3},{3,0},{4,5},{5,6},{6,7},{7,4},{8,9},{9,10},{10,1... | collective-permute-start | bytes 786440 | tf_op jit(solution)/shard_map/ppermute | solution.py:519
  36.7 20.0 %collective-permute-start.2 = (f32[4,16,1024]{2,1,0:T(8,128)S(1)}, f32[4,16,1024]{2,1,0:T(8,128)S(1)}, u32[]{:S(2)}, u32[]{:S(2)}) collective-permute-start(f32[4,16,1024]{2,1,0:T(8,128)S(1)} %get-tuple-element.14), channel_id=1, source_target_pairs={{0,2},{1,3},{2,0},{3,1},{4,6},{5,7},{6,4},{7,5},{8,10},{9,11},{10,... | collective-permute-start | bytes 786440 | tf_op jit(solution)/shard_map/ppermute | solution.py:519
  39.5 22.7 %collective-permute-start.3 = (f32[4,16,1024]{2,1,0:T(8,128)S(1)}, f32[4,16,1024]{2,1,0:T(8,128)S(1)}, u32[]{:S(2)}, u32[]{:S(2)}) collective-permute-start(f32[4,16,1024]{2,1,0:T(8,128)S(1)} %get-tuple-element.15), channel_id=1, source_target_pairs={{0,3},{1,0},{2,1},{3,2},{4,7},{5,4},{6,5},{7,6},{8,11},{9,8},{10,9... | collective-permute-start | bytes 786440 | tf_op jit(solution)/shard_map/ppermute | solution.py:519
  63.5 20.9 %all-to-all-start.1 = ((f32[16,16,1024]{2,1,0:T(8,128)}), f32[16,16,1024]{2,1,0:T(8,128)S(1)}, u32[]{:S(2)}, u32[]{:S(2)}) async-start(f32[16,16,1024]{2,1,0:T(8,128)} %shard_map.97), calls=%async_computation.1 | async-start | bytes 2097152 | tf_op jit(solution)/shard_map/all_to_all | solution.py:525
  84.4 1.2 copy-start.2
  85.7 1.2 copy-start.3
  86.9 0.9 copy-start.6
  113.3 16.8 %collective-permute-start.4 = (f32[520,128]{1,0:T(8,128)S(1)}, f32[520,128]{1,0:T(8,128)S(1)}, u32[]{:S(2)}, u32[]{:S(2)}) collective-permute-start(f32[520,128]{1,0:T(8,128)S(1)} %get-tuple-element.17), channel_id=1, source_target_pairs={{0,1},{1,2},{2,3},{3,0},{4,5},{5,6},{6,7},{7,4},{8,9},{9,10},{10,1... | collective-permute-start | bytes 798728 | tf_op jit(solution)/shard_map/ppermute | solution.py:519
  116.2 14.1 %collective-permute-start.5 = (f32[520,128]{1,0:T(8,128)S(1)}, f32[520,128]{1,0:T(8,128)S(1)}, u32[]{:S(2)}, u32[]{:S(2)}) collective-permute-start(f32[520,128]{1,0:T(8,128)S(1)} %get-tuple-element.18), channel_id=1, source_target_pairs={{0,2},{1,3},{2,0},{3,1},{4,6},{5,7},{6,4},{7,5},{8,10},{9,11},{10,... | collective-permute-start | bytes 798728 | tf_op jit(solution)/shard_map/ppermute | solution.py:519
  119.0 13.2 %collective-permute-start.6 = (f32[520,128]{1,0:T(8,128)S(1)}, f32[520,128]{1,0:T(8,128)S(1)}, u32[]{:S(2)}, u32[]{:S(2)}) collective-permute-start(f32[520,128]{1,0:T(8,128)S(1)} %get-tuple-element.19), channel_id=1, source_target_pairs={{0,3},{1,0},{2,1},{3,2},{4,7},{5,4},{6,5},{7,6},{8,11},{9,8},{10,9... | collective-permute-start | bytes 798728 | tf_op jit(solution)/shard_map/ppermute | solution.py:519
  134.1 22.7 %all-to-all-start.3 = ((f32[16,128,128]{1,2,0:T(8,128)}), f32[16,128,128]{1,2,0:T(8,128)S(1)}, u32[]{:S(2)}, u32[]{:S(2)}) async-start(f32[16,128,128]{1,2,0:T(8,128)} %copy.12), calls=%async_computation.3 | async-start | bytes 2097152 | tf_op jit(solution)/shard_map/all_to_all | solution.py:525
  139.8 1.4 collective-permute-start.10
  139.8 3.7 %collective-permute-start.9 = (f32[8,128]{1,0:T(8,128)S(1)}, f32[8,128]{1,0:T(8,128)S(1)}, u32[]{:S(2)}, u32[]{:S(2)}) collective-permute-start(f32[8,128]{1,0:T(8,128)S(1)} %get-tuple-element.21.b0), channel_id=1, source_target_pairs={{0,128},{64,192},{128,0},{192,64},{1,129},{65,193},{129,1},{193,65... | collective-permute-start | bytes 12296 | tf_op jit(solution)/shard_map/ppermute | solution.py:578
  141.2 3.0 %collective-permute-start.8 = (f32[8,128]{1,0:T(8,128)S(1)}, f32[8,128]{1,0:T(8,128)S(1)}, u32[]{:S(2)}, u32[]{:S(2)}) collective-permute-start(f32[8,128]{1,0:T(8,128)S(1)} %get-tuple-element.21.b0), channel_id=1, source_target_pairs={{0,64},{64,128},{128,192},{192,0},{1,65},{65,129},{129,193},{193,1... | collective-permute-start | bytes 12296 | tf_op jit(solution)/shard_map/ppermute | solution.py:578
  144.2 8.1 %collective-permute-start.11 = (f32[4,8,128]{2,1,0:T(8,128)S(1)}, f32[4,8,128]{2,1,0:T(8,128)S(1)}, u32[]{:S(2)}, u32[]{:S(2)}) collective-permute-start(f32[4,8,128]{2,1,0:T(8,128)S(1)} %shard_map.102.own), channel_id=1, source_target_pairs={{0,0},{1,1},{2,2},{3,3},{4,4},{5,5},{6,6},{7,7},{8,8},{9,9},{10,10... | collective-permute-start | bytes 49160 | tf_op jit(solution)/shard_map/ppermute | solution.py:585
  152.4 9.3 %collective-permute-start.14 = (f32[4,8,128]{2,1,0:T(8,128)S(1)}, f32[4,8,128]{2,1,0:T(8,128)S(1)}, u32[]{:S(2)}, u32[]{:S(2)}) collective-permute-start(f32[4,8,128]{2,1,0:T(8,128)S(1)} %collective-permute-done.11.c0), channel_id=1, source_target_pairs={{0,12},{1,13},{2,14},{3,15},{4,0},{5,1},{6,2},{7,3},{8,4},{9,5},{1... | collective-permute-start | bytes 49160 | tf_op jit(solution)/shard_map/ppermute | solution.py:586
  155.1 6.6 %collective-permute-start.13 = (f32[4,8,128]{2,1,0:T(8,128)S(1)}, f32[4,8,128]{2,1,0:T(8,128)S(1)}, u32[]{:S(2)}, u32[]{:S(2)}) collective-permute-start(f32[4,8,128]{2,1,0:T(8,128)S(1)} %collective-permute-done.11.c0), channel_id=1, source_target_pairs={{0,8},{1,9},{2,10},{3,11},{4,12},{5,13},{6,14},{7,15},{8,0},{9,1},... | collective-permute-start | bytes 49160 | tf_op jit(solution)/shard_map/ppermute | solution.py:586
  155.9 5.8 %collective-permute-start.12 = (f32[4,8,128]{2,1,0:T(8,128)S(1)}, f32[4,8,128]{2,1,0:T(8,128)S(1)}, u32[]{:S(2)}, u32[]{:S(2)}) collective-permute-start(f32[4,8,128]{2,1,0:T(8,128)S(1)} %collective-permute-done.11.c0), channel_id=1, source_target_pairs={{0,4},{1,5},{2,6},{3,7},{4,8},{5,9},{6,10},{7,11},{8,12},{9,13},{1... | collective-permute-start | bytes 49160 | tf_op jit(solution)/shard_map/ppermute | solution.py:586
  156.8 9.5 %collective-permute-start.7 = (f32[16,128]{1,0:T(8,128)S(1)}, f32[16,128]{1,0:T(8,128)S(1)}, u32[]{:S(2)}, u32[]{:S(2)}) collective-permute-start(f32[16,128]{1,0:T(8,128)S(1)} %bitcast.18), channel_id=1, source_target_pairs={{1,0},{2,1},{3,2},{4,3},{5,4},{6,5},{7,6},{8,7},{9,8},{10,9},{11,1... | collective-permute-start | bytes 24584 | tf_op jit(solution)/shard_map/ppermute | solution.py:575
  166.3 2.2 %copy-start = (bf16[2,16,256,256]{3,2,1,0:T(8,128)(2,1)S(1)}, bf16[2,16,256,256]{3,2,1,0:T(8,128)(2,1)}, u32[]{:S(2)}) copy-start(bf16[2,16,256,256]{3,2,1,0:T(8,128)(2,1)} %constant.96.clone.mat) | copy-start | bytes 12582916

commit v2 on v1

--- a/solution.py
+++ b/solution.py
@@ -29,7 +29,7 @@
 BF16 = jnp.bfloat16
 VMEM = pl.BlockSpec(memory_space=pltpu.VMEM)
 HBM = pl.BlockSpec(memory_space=pltpu.HBM)
-PARAMS = pltpu.CompilerParams(vmem_limit_bytes=48 * 1024 * 1024)
+PARAMS = pltpu.CompilerParams(vmem_limit_bytes=24 << 20)
 
 
 def split_const(table):
@@ -70,22 +70,13 @@
         blocks.append(np.where(inside, response[np.clip(position, 0, TAPS - 1)], 0.0))
     out["toeplitz"] = split_const(np.concatenate(blocks, 0))
     rows = np.arange(256).reshape(2, 16, 8).transpose(1, 0, 2).reshape(256)
-    out["hop_fwd"] = split_const(left_form(dft(128, -1))[:, rows])
-    cross = np.exp(-2j * np.pi * np.arange(128)[:, None] * np.arange(1024)[None, :] / LOCAL)
-    out["cross"] = np.stack([cross.real, cross.imag]).astype(np.float32)
-    out["sub_fwd"] = split_const(right_form(dft(256, -1)))
-    out["sub_inv"] = split_const(left_form(dft(256, 1)[row_order()]) / NT)
-    out["hop_inv"] = split_const(right_form(dft(128, 1)))
+    forward = dft(256, -1)
+    inverse = dft(256, 1)[row_order()] / NT
+    squares = [left_form(dft(128, -1))[:, rows], right_form(dft(128, 1))]
+    squares += [forward.real, forward.imag, inverse.real, inverse.imag]
+    out["squares"] = np.concatenate([split_const(square) for square in squares])
     order = np.arange(256).reshape(2, 2, 64).transpose(1, 0, 2).reshape(256)
-    inner = np.arange(128)
-    window = np.sin(np.pi / W * np.arange(W)) ** 2
-    frames = []
-    for a in range(16):
-        block = np.exp(-2j * np.pi * (inner[:, None] * inner[None, :] % 128) / 128)
-        block = block * window[a + 16 * inner][None, :]
-        block = block * np.exp(-2j * np.pi * a * inner / 2048)[:, None]
-        frames.append(left_form(block)[:, order])
-    out["frames"] = split_const(np.stack(frames))
+    out["frames"] = split_const(left_form(dft(128, -1))[:, order])
     return out
 
 
@@ -299,34 +290,39 @@
     lax.fori_loop(0, 8, body, phasor(number, 4 * LOCAL, -1))
 
 
-def spectrum_kernel(
-    blocks, hop, cross, mat, disp, inv, unhop, out, wide, work, back, rows_w, bins, flip, flat
-):
+def spectrum_kernel(blocks, squares, disp, out, wide, work, back, rows_w, bins, flip, flat):
+    hop, unhop = squares.at[0:2], squares.at[2:4]
+    fwd_c, fwd_s, inv_c, inv_s = [squares.at[2 * k : 2 * k + 2] for k in range(2, 6)]
     for part in range(4):
         lanes = slice(256 * part, 256 * part + 256)
         wide[:, lanes] = dot_left(hop, blocks[:, :, lanes].reshape(256, 256))
     lane_f = powers(phasor(iota((8, 256), 1), 1024, -1))
+    number = [256 * part + iota((8, 256), 1) for part in range(4)]
+    cross_first = tuple(phasor(iota((8, 256), 0) * n, LOCAL, -1) for n in number)
+    cross_step = [phasor(8 * n, LOCAL, -1) for n in number]
 
     def body(step, carry):
         rows, low_rows = eight(step * 8), eight(step * 8 + 128)
         x = []
         for part in range(4):
             lanes = slice(256 * part, 256 * part + 256)
-            factor = (cross[0, rows, lanes], cross[1, rows, lanes])
-            x.append(cmul((wide[rows, lanes], wide[low_rows, lanes]), factor))
+            x.append(cmul((wide[rows, lanes], wide[low_rows, lanes]), carry[part]))
         y = twist(quad(x, -1.0), lane_f)
         for k in range(4):
             at = eight(step * 8 + 128 * k)
             work[at, 0:256] = y[k][0]
             work[at, 256:512] = y[k][1]
-        return carry
-
-    lax.fori_loop(0, 16, body, 0)
+        return tuple(cmul(value, move) for value, move in zip(carry, cross_step))
+
+    lax.fori_loop(0, 16, body, cross_first)
     bins[64:128, :] = jnp.zeros((64, 256), F32)
     for k in range(4):
         rows = slice(128 * k, 128 * k + 128)
-        got = dot_right(work[rows, :], mat)
-        re, im = got[:, :256], got[:, 256:]
+        re, im = work[rows, 0:256], work[rows, 256:512]
+        re, im = (
+            dot_right(re, fwd_c) - dot_right(im, fwd_s),
+            dot_right(re, fwd_s) + dot_right(im, fwd_c),
+        )
         power = (re * re + im * im).reshape(16, 8, 256)
         bins[16 * k : 16 * k + 16, :] = jnp.sum(power, axis=1) * (1.0 / (NT * BIN_WIDTH))
         re, im = cmul((re, im), (disp[0, rows, :], disp[1, rows, :]))
@@ -337,7 +333,9 @@
     flat[...] = flip[pl.ds(0, 128, stride=2), :] + pltpu.roll(flip[pl.ds(1, 128, stride=2), :], 64, 1)
     for dest in range(16):
         out[dest, 128:136, :] = flat[8 * dest : 8 * dest + 8, :]
-    back[...] = dot_left(inv, work[...], NT_FORM)
+    re, im = work[:, 0:256], work[:, 256:512]
+    back[0:256, :] = dot_left(inv_c, re, NT_FORM) - dot_left(inv_s, im, NT_FORM)
+    back[256:512, :] = dot_left(inv_c, im, NT_FORM) + dot_left(inv_s, re, NT_FORM)
     first = phasor(16 * iota((8, 128), 0), 1024, 1)
     forward, half_turn = turn(1, 1024, 1), turn(128, 1024, 1)
     freq = iota((8, 128), 1)
@@ -378,7 +376,7 @@
     for k in range(1, 16):
         total = total + blocks[k, 128:136, :]
     for out in outs:
-        out[512:520, :] = total
+        out[520:528, :] = total
     block = 4 * place["x"] + place["y"]
     number = block + 16 * iota((8, 128), 0) + 1024 * iota((8, 128), 1) + place["z"] * LOCAL
     forward = turn(128, 4 * LOCAL, 1)
@@ -394,32 +392,43 @@
         return cmul(factor, forward)
 
     lax.fori_loop(0, 8, body, phasor(number, 4 * LOCAL, 1))
-
-
-def inv_kernel(r0, r1, r2, r3, out, bins, scratch):
+    pick = jnp.where(iota((16, 128), 1) == 0, 1.0, 0.0).astype(BF16)
+    for j in range(4):
+        high, low = halves(outs[(j + 1) % 4][0:512, :])
+        row = lax.dot_general(pick, high, dims(NT_FORM), preferred_element_type=F32)
+        row = row + lax.dot_general(pick, low, dims(NT_FORM), preferred_element_type=F32)
+        for kk in range(4):
+            outs[j][512 + kk : 513 + kk, :] = row[0:1, 128 * kk : 128 * kk + 128]
+        outs[j][516:520, :] = jnp.zeros((4, 128), F32)
+
+
+def unsixteen(x, factors):
+    line = [None] * 16
+    for c0 in range(4):
+        for c1 in range(4):
+            value = x[c0][c1]
+            line[4 * c1 + c0] = cmul(value, factors[c0 + 4 * c1]) if c0 + c1 else value
+    return sixteen(line, 1.0)
+
+
+def inv_kernel(r0, r1, r2, r3, out, bins, blocks):
     place = digits()
-    blocks = (r0, r1, r2, r3)
-    bins[...] = (r0[512:520, :] + r1[512:520, :]) + (r2[512:520, :] + r3[512:520, :])
+    bins[...] = (r0[520:528, :] + r1[520:528, :]) + (r2[520:528, :] + r3[520:528, :])
+    for s, value in enumerate((r0, r1, r2, r3)):
+        blocks[(place["z"] - s) & 3] = value[0:520, :]
     block = 4 * place["x"] + place["y"]
     number = place["z"] * LOCAL + block + 16 * iota((8, 128), 0) + 1024 * iota((8, 128), 1)
     forward = turn(128, NT, 1)
 
     def body(step, factor):
-        for kk in range(4):
-            for low in (128 * kk, 128 * kk + 64):
-                rows = eight(step * 8 + low)
-                for s in range(4):
-                    scratch[(place["z"] - s) & 3, rows, :] = blocks[s][rows, :]
-        factors = many_powers(factor)
-        x = [None] * 16
-        for c0 in range(4):
-            for c1 in range(4):
-                value = (
-                    scratch[c0, eight(step * 8 + 128 * c1), :],
-                    scratch[c0, eight(step * 8 + 128 * c1 + 64), :],
-                )
-                x[4 * c1 + c0] = cmul(value, factors[c0 + 4 * c1]) if c0 + c1 else value
-        y = sixteen(x, 1.0)
+        x = [
+            [
+                (blocks[c0, eight(step * 8 + 128 * c1), :], blocks[c0, eight(step * 8 + 128 * c1 + 64), :])
+                for c1 in range(4)
+            ]
+            for c0 in range(4)
+        ]
+        y = unsixteen(x, many_powers(factor))
         for a0 in range(4):
             for a1 in range(4):
                 out[4 * a1 + a0, eight(step * 8), :] = y[a0][a1][0]
@@ -427,26 +436,52 @@
         return cmul(factor, forward)
 
     lax.fori_loop(0, 8, body, phasor(number, NT, 1))
-
-
-def frames_kernel(blocks, tail, mat, out, got):
-    columns = tail[...].T
+    after = (place["z"] + 1) & 3
+    lane = iota((8, 128), 1)
+    factors = many_powers(phasor(after * LOCAL + block + 16 * (lane & 63), NT, 1))
+    x = []
+    for c0 in range(4):
+        rows = [
+            jnp.broadcast_to(blocks[c0, 512 + c1 : 513 + c1, :], (8, 128)) for c1 in range(4)
+        ]
+        x.append([(row, pltpu.roll(row, 64, 1)) for row in rows])
+    y = unsixteen(x, factors)
+    flat = []
+    for t in range(16):
+        re, im = y[t % 4][t // 4]
+        flat.append(jnp.where(lane < 64, re, pltpu.roll(im, 64, 1)))
+    wrap = after == 0
+    for t in range(16):
+        out[t, 128:136, :] = jnp.where(wrap, flat[(t + 1) % 16], flat[t])
+
+
+def frames_kernel(blocks, mat, out, got):
+    columns = jnp.concatenate([blocks[a, 128:129, :] for a in range(16)], axis=0).T
     lane = iota((128, 128), 1)
+    wave = phasor(16 * iota((64, 128), 0), W, 1)
     for a in range(16):
-        here = blocks[a]
+        here = blocks[a, 0:128, :]
         after = jnp.where(lane == 127, columns[:, a : a + 1], pltpu.roll(here, 127, 1))
-        got[a] = dot_left(mat.at[:, a], jnp.concatenate([here, after], axis=0))
-
-    def body(step, carry):
+        late = 0.5 + 0.5 * wave[0]
+        early = 0.5 - 0.5 * wave[0]
+        pieces = [here[0:64] * early, here[64:128] * early, after[0:64] * late, after[64:128] * late]
+        got[a] = dot_left(mat, jnp.concatenate(pieces, axis=0))
+        wave = cmul(wave, turn(1, W, 1))
+    first = phasor(iota((8, 128), 0), W, -1)
+    forward = turn(8, W, -1)
+
+    def body(step, factor):
         rows, low_rows = eight(step * 8), eight(step * 8 + 128)
-        y = sixteen([(got[a, rows, :], got[a, low_rows, :]) for a in range(16)], -1.0)
+        factors = many_powers(factor)
+        x = [(got[a, rows, :], got[a, low_rows, :]) for a in range(16)]
+        y = sixteen([cmul(x[a], factors[a]) if a else x[a] for a in range(16)], -1.0)
         for c0 in range(4):
             for c1 in range(4):
                 value = y[c0][c1]
                 got[c0 + 4 * c1, rows, :] = (value[0] * value[0] + value[1] * value[1]) * (1.0 / W)
-        return carry
-
-    lax.fori_loop(0, 16, body, 0)
+        return cmul(factor, forward)
+
+    lax.fori_loop(0, 16, body, first)
     for c in range(16):
         out[:, 128 * c : 128 * c + 128] = got[c, 0:128, :].T
 
@@ -483,14 +518,17 @@
                 column = flipped[:, 2 * r + half : 2 * r + half + 1]
                 side[r, 128 * half : 128 * half + 128, :] = jnp.broadcast_to(column, (128, 128))
 
-    for group in range(4):
-        rows = eight(step * 32 + group * 8)
-        factors = [side[r, rows, :] for r in range(4)]
+    for half in range(2):
+        base = 32 * half
+        factors = [[side[r, eight(step * 64 + base + g * 8), :] for r in range(4)] for g in range(4)]
         for k in range(32):
-            total = factors[0] * cols[0, k : k + 1, :]
-            for r in range(1, 4):
-                total = total + factors[r] * cols[r, k : k + 1, :]
-            out[8 * group : 8 * group + 8, 128 * k : 128 * k + 128] = total
+            line = [jnp.broadcast_to(cols[r, k : k + 1, :], (8, 128)) for r in range(4)]
+            for g in range(4):
+                total = (factors[g][0] * line[0] + factors[g][1] * line[1]) + (
+                    factors[g][2] * line[2] + factors[g][3] * line[3]
+                )
+                at = base + 8 * g
+                out[at : at + 8, 128 * k : 128 * k + 128] = total
 
 
 def call(kernel, outs, scratch, *args, flops=1 << 20, specs=None):
@@ -515,8 +553,8 @@
     return pairs
 
 
-def swap_blocks(blocks, axis):
-    moved = {step: lax.ppermute(blocks[step], "tm", ring(axis, step)) for step in (1, 3, 2)}
+def swap_z(blocks):
+    moved = {step: lax.ppermute(blocks[step], "tm", ring("z", step)) for step in (2, 1, 3)}
     return [blocks[0], moved[1], moved[2], moved[3]]
 
 
@@ -528,7 +566,6 @@
 
 
 FWD = (16, 16, 1024)
-INV = (16, 128, 128)
 
 
 def on_device(seed_field):
@@ -549,7 +586,7 @@
     )[0]
     value = swap_plane(value)
     blocks = call(fwd_kernel, [(4, 16, 1024)] * 4, [(4, 4, 16, 1024)], value)
-    blocks = swap_blocks(blocks, "z")
+    blocks = swap_z(blocks)
     value = call(mid_kernel, [FWD], [], *blocks)[0]
     value = swap_plane(value)
     number = (
@@ -564,42 +601,41 @@
     value = call(
         spectrum_kernel, [(16, 136, 128)],
         [(256, 1024), (512, 512), (512, 512), (1024, 256), (128, 256), (256, 128), (128, 128)],
-        value, table["hop_fwd"], table["cross"], table["sub_fwd"], disp, table["sub_inv"], table["hop_inv"],
+        value, table["squares"], disp,
     )[0]
     value = swap_plane(value)
-    blocks = call(unmid_kernel, [(520, 128)] * 4, [], value)
-    blocks = swap_blocks(blocks, "z")
-    value, bins = call(inv_kernel, [INV, (8, 128)], [(4, 512, 128)], *blocks)
+    blocks = call(unmid_kernel, [(528, 128)] * 4, [], value)
+    blocks = swap_z(blocks)
+    value, bins = call(inv_kernel, [(16, 136, 128), (8, 128)], [(4, 520, 128)], *blocks)
     value = swap_plane(value)
-
-    tail = lax.ppermute(value[:, :, 0], "tm", [((d + 1) % 64, d) for d in range(64)])
 
     alike = [bins] + [
         lax.ppermute(bins, "grp", [(g, (g + step) % 4) for g in range(4)]) for step in (1, 2, 3)
     ]
     normal = call(normal_kernel, [(4, 8, 128)], [], *alike)[0]
-    pairs = []
-    for g in range(4):
-        for d in range(64):
-            pairs.append((g * 64 + d, d // 16 * 64 + g * 16 + d % 16))
-    columns = lax.ppermute(normal, ("grp", "tm"), pairs)
-    columns = [columns] + [lax.ppermute(columns, "tm", ring("y", step)) for step in (1, 2, 3)]
-
+    columns = []
+    for step in range(4):
+        pairs = []
+        for g in range(4):
+            for d in range(64):
+                x, y, z = d // 16, d // 4 % 4, d % 4
+                pairs.append((g * 64 + d, x * 64 + g * 16 + (y + step) % 4 * 4 + z))
+        columns.append(lax.ppermute(normal, ("grp", "tm"), pairs))
+
+    spectrogram = call(frames_kernel, [(HOPS, W)], [(16, 256, 128)], value, table["frames"])[0]
+    spectrogram, normal, *columns = lax.optimization_barrier((spectrogram, normal, *columns))
     correlation = pl.pallas_call(
         correlation_kernel,
-        grid=(8,),
+        grid=(4,),
         out_shape=jax.ShapeDtypeStruct((256, 4096), F32),
         in_specs=[pl.BlockSpec((4, 8, 128), lambda i: (0, 0, 0))] * 5,
-        out_specs=pl.BlockSpec((32, 4096), lambda i: (i, 0)),
+        out_specs=pl.BlockSpec((64, 4096), lambda i: (i, 0)),
         scratch_shapes=[
             pltpu.VMEM((4, 256, 128), F32), pltpu.VMEM((128, 128), F32), pltpu.VMEM((4, 32, 128), F32)
         ],
         compiler_params=PARAMS,
         cost_estimate=pl.CostEstimate(flops=1 << 23, bytes_accessed=1 << 22, transcendentals=0),
     )(normal, *columns)
-    spectrogram = call(
-        frames_kernel, [(HOPS, W)], [(16, 256, 128)], value, tail, table["frames"]
-    )[0]
     return spectrogram[None], correlation
 
 

time: 175 us -> 164 us (0.937)
  local copies, waits for them, and re-layouts: 10.6 us -> 3.76 us
  waiting for transfers between devices: 55.7 us -> 50.6 us
  starting transfers between devices: 45.2 us -> 47.2 us
    unnamed x15 -> x7, local copies, waits for them, and re-layouts: 8.28 us -> 2.98 us
    ppermute x11 -> x10, waiting for transfers between devices: 34.7 us -> 29.6 us  [the longest x6 29.6 us: swap_z(): lax.ppermute(blocks[step], 'tm', ring('z', step))]
    ppermute x11 -> x10, starting transfers between devices: 28.7 us -> 30.6 us  [the longest x6 17 us: swap_z(): lax.ppermute(blocks[step], 'tm', ring('z', step))]
  transfers between devices with their start and end apart: 17 -> 16, of which waited for: 10 -> 11; matrix products, arithmetic and copies ran while one was open for 2% -> 2% of each run, Pallas kernels for 2% -> 3%
where the time goes in v2:
time: 164 us; the launch traced here: 163 us
  waiting for transfers between devices  50.6 us (31%)
  starting transfers between devices  47.2 us (29%)
  blocking collectives  39.5 us (24%)
  Pallas kernels  19.1 us (12%)
  local copies, waits for them, and re-layouts  3.76 us (2%)
  other arithmetic  2.22 us (1%)
    all_to_all x2, blocking collectives, swap_plane(): lax.all_to_all(value, 'tm', split_axis=0, concat_axis=0, axis_index_group...  39.5 us
    ppermute x6, waiting for transfers between devices, swap_z(): lax.ppermute(blocks[step], 'tm', ring('z', step))  29.6 us
    ppermute x6, starting transfers between devices, swap_z(): lax.ppermute(blocks[step], 'tm', ring('z', step))  17 us
    pallas_call x8, Pallas kernels, call(): pl.pallas_call(kernel, out_shape=[jax.ShapeDtypeStruct(s, F32) for s in o...  16 us
    ppermute x4, starting transfers between devices, on_device(): columns.append(lax.ppermute(normal, ('grp', 'tm'), pairs))  13.5 us
    all_to_all x2, waiting for transfers between devices, swap_plane(): lax.all_to_all(value, 'tm', split_axis=0, concat_axis=0, axis_index_group...  12.5 us
    all_to_all x2, starting transfers between devices, swap_plane(): lax.all_to_all(value, 'tm', split_axis=0, concat_axis=0, axis_index_group...  12.1 us
    ppermute x1, waiting for transfers between devices, on_device(): lax.ppermute(last, 'tm', [(d, (d + 1) % 64) for d in range(64)])  5.47 us
  transfers between devices with their start and end apart: 16, of which 11 were waited for; matrix products, arithmetic and copies ran while one was open for 2% of the time, Pallas kernels for 3%

profile of v2, /device:TPU:4, one launch (start us, length us, event | category | flops | bytes accessed | tf_op | source)
XLA Modules:
  0.0 163.2 jit_solution(10923610893213363924)
XLA Ops:
  1.4 3.3 %collective-permute-start = (f32[8,128]{1,0:T(8,128)S(1)}, f32[8,128]{1,0:T(8,128)S(1)}, u32[]{:S(2)}, u32[]{:S(2)}) collective-permute-start(f32[8,128]{1,0:T(8,128)S(1)} %reshape_squeeze.3), channel_id=1, source_target_pairs={{0,1},{1,2},{2,3},{3,4},{4,5},{5,6},{6,7},{7,8},{8,9},{9,10},{10,1... | collective-permute-start | bytes 12296 | tf_op jit(solution)/shard_map/ppermute | solution.py:578
  6.3 5.5 %collective-permute-done = f32[8,128]{1,0:T(8,128)S(1)} collective-permute-done((f32[8,128]{1,0:T(8,128)S(1)}, f32[8,128]{1,0:T(8,128)S(1)}, u32[]{:S(2)}, u32[]{:S(2)}) %collective-permute-start) | collective-permute-done | bytes 4128 | tf_op jit(solution)/shard_map/ppermute | solution.py:578
  11.8 2.2 %shard_map.59 = f32[16,16,1024]{2,1,0:T(8,128)S(1)} custom-call(f32[2,128,1024]{2,1,0:T(8,128)S(1)} %bitcast.11, f32[1,512]{1,0:T(1,128)S(1)} %multiply_add_fusion.halo, bf16[2,768,256]{2,1,0:T(8,128)(2,1)S(1)} %copy-done.1), custom_call_target="tpu_custom_call" | custom-call | flops 1048576 | bytes 2097152 | tf_op jit(solution)/shard_map/pallas_call | solution.py:536
  14.0 19.4 %all_to_all.20.blocks = f32[16,16,1024]{2,1,0:T(8,128)S(1)} all-to-all(f32[16,16,1024]{2,1,0:T(8,128)S(1)} %shard_map.59), channel_id=1, replica_groups={{0,4,8,12,16,20,24,28,32,36,40,44,48,52,56,60},{1,5,9,13,17,21,25,29,33..., dimensions={0} | all-to-all | bytes 2097152 | tf_op jit(solution)/shard_map/all_to_all | solution.py:563
  35.6 2.9 %collective-permute-start.2 = (f32[4,16,1024]{2,1,0:T(8,128)S(1)}, f32[4,16,1024]{2,1,0:T(8,128)S(1)}, u32[]{:S(2)}, u32[]{:S(2)}) collective-permute-start(f32[4,16,1024]{2,1,0:T(8,128)S(1)} %get-tuple-element.20), channel_id=1, source_target_pairs={{0,2},{1,3},{2,0},{3,1},{4,6},{5,7},{6,4},{7,5},{8,10},{9,11},{10,... | collective-permute-start | bytes 786440 | tf_op jit(solution)/shard_map/ppermute | solution.py:557
  38.5 3.9 %collective-permute-start.3 = (f32[4,16,1024]{2,1,0:T(8,128)S(1)}, f32[4,16,1024]{2,1,0:T(8,128)S(1)}, u32[]{:S(2)}, u32[]{:S(2)}) collective-permute-start(f32[4,16,1024]{2,1,0:T(8,128)S(1)} %get-tuple-element.21), channel_id=1, source_target_pairs={{0,3},{1,0},{2,1},{3,2},{4,7},{5,4},{6,5},{7,6},{8,11},{9,8},{10,9... | collective-permute-start | bytes 786440 | tf_op jit(solution)/shard_map/ppermute | solution.py:557
  42.4 13.3 %collective-permute-done.1.r1 = f32[4,16,1024]{2,1,0:T(8,128)S(1)} collective-permute-done((f32[4,16,1024]{2,1,0:T(8,128)S(1)}, f32[4,16,1024]{2,1,0:T(8,128)S(1)}, u32[]{:S(2)}, u32[]{:S(2)}) %collective-permute-start.1) | collective-permute-done | bytes 262176 | tf_op jit(solution)/shard_map/ppermute | solution.py:557
  55.6 5.6 %collective-permute-done.3.r3 = f32[4,16,1024]{2,1,0:T(8,128)S(1)} collective-permute-done((f32[4,16,1024]{2,1,0:T(8,128)S(1)}, f32[4,16,1024]{2,1,0:T(8,128)S(1)}, u32[]{:S(2)}, u32[]{:S(2)}) %collective-permute-start.3) | collective-permute-done | bytes 262176 | tf_op jit(solution)/shard_map/ppermute | solution.py:557
  62.5 6.2 %all-to-all-start.1 = ((f32[16,16,1024]{2,1,0:T(8,128)}), f32[16,16,1024]{2,1,0:T(8,128)S(1)}, u32[]{:S(2)}, u32[]{:S(2)}) async-start(f32[16,16,1024]{2,1,0:T(8,128)} %shard_map.61), calls=%async_computation.1 | async-start | bytes 2097152 | tf_op jit(solution)/shard_map/all_to_all | solution.py:563
  70.9 12.4 %all-to-all-done.1.blocks = f32[16,16,1024]{2,1,0:T(8,128)S(1)} async-done(((f32[16,16,1024]{2,1,0:T(8,128)}), f32[16,16,1024]{2,1,0:T(8,128)S(1)}, u32[]{:S(2)}, u32[]{:S(2)}) %all-to-all-start.1) | async-done | bytes 1048608 | tf_op jit(solution)/shard_map/all_to_all | solution.py:563
  84.8 5.1 %shard_map.62 = f32[16,136,128]{2,1,0:T(8,128)S(1)} custom-call(f32[16,16,1024]{2,1,0:T(8,128)S(1)} %all-to-all-done.1.blocks, bf16[12,256,256]{2,1,0:T(8,128)(2,1)S(1)} %copy-done, f32[2,512,256]{2,1,0:T(8,128)S(1)} %pad_maximum_fusion.disp), custom_call_target="tpu_custom_call" | custom-call | flops 1048576 | bytes 2228224 | tf_op jit(solution)/shard_map/pallas_call | solution.py:536
  89.9 20.1 %all_to_all.21.blocks = f32[16,136,128]{2,1,0:T(8,128)S(1)} all-to-all(f32[16,136,128]{2,1,0:T(8,128)S(1)} %shard_map.62), channel_id=1, replica_groups={{0,4,8,12,16,20,24,28,32,36,40,44,48,52,56,60},{1,5,9,13,17,21,25,29,33..., dimensions={0} | all-to-all | bytes 2228224 | tf_op jit(solution)/shard_map/all_to_all | solution.py:563
  110.6 3.1 %collective-permute-start.4 = (f32[528,128]{1,0:T(8,128)S(1)}, f32[528,128]{1,0:T(8,128)S(1)}, u32[]{:S(2)}, u32[]{:S(2)}) collective-permute-start(f32[528,128]{1,0:T(8,128)S(1)} %get-tuple-element.23), channel_id=1, source_target_pairs={{0,1},{1,2},{2,3},{3,0},{4,5},{5,6},{6,7},{7,4},{8,9},{9,10},{10,1... | collective-permute-start | bytes 811016 | tf_op jit(solution)/shard_map/ppermute | solution.py:557
  113.6 2.7 %collective-permute-start.5 = (f32[528,128]{1,0:T(8,128)S(1)}, f32[528,128]{1,0:T(8,128)S(1)}, u32[]{:S(2)}, u32[]{:S(2)}) collective-permute-start(f32[528,128]{1,0:T(8,128)S(1)} %get-tuple-element.24), channel_id=1, source_target_pairs={{0,2},{1,3},{2,0},{3,1},{4,6},{5,7},{6,4},{7,5},{8,10},{9,11},{10,... | collective-permute-start | bytes 811016 | tf_op jit(solution)/shard_map/ppermute | solution.py:557
  116.4 3.1 %collective-permute-start.6 = (f32[528,128]{1,0:T(8,128)S(1)}, f32[528,128]{1,0:T(8,128)S(1)}, u32[]{:S(2)}, u32[]{:S(2)}) collective-permute-start(f32[528,128]{1,0:T(8,128)S(1)} %get-tuple-element.25), channel_id=1, source_target_pairs={{0,3},{1,0},{2,1},{3,2},{4,7},{5,4},{6,5},{7,6},{8,11},{9,8},{10,9... | collective-permute-start | bytes 811016 | tf_op jit(solution)/shard_map/ppermute | solution.py:557
  119.4 6.4 %collective-permute-done.4.r1 = f32[528,128]{1,0:T(8,128)S(1)} collective-permute-done((f32[528,128]{1,0:T(8,128)S(1)}, f32[528,128]{1,0:T(8,128)S(1)}, u32[]{:S(2)}, u32[]{:S(2)}) %collective-permute-start.4) | collective-permute-done | bytes 270368 | tf_op jit(solution)/shard_map/ppermute | solution.py:557
  125.8 2.6 %collective-permute-done.5.r2 = f32[528,128]{1,0:T(8,128)S(1)} collective-permute-done((f32[528,128]{1,0:T(8,128)S(1)}, f32[528,128]{1,0:T(8,128)S(1)}, u32[]{:S(2)}, u32[]{:S(2)}) %collective-permute-start.5) | collective-permute-done | bytes 270368 | tf_op jit(solution)/shard_map/ppermute | solution.py:557
  131.9 5.9 %all-to-all-start.3 = ((f32[16,136,128]{2,1,0:T(8,128)}), f32[16,136,128]{2,1,0:T(8,128)S(1)}, u32[]{:S(2)}, u32[]{:S(2)}) async-start(f32[16,136,128]{2,1,0:T(8,128)} %get-tuple-element.26), calls=%async_computation.3 | async-start | bytes 2228224 | tf_op jit(solution)/shard_map/all_to_all | solution.py:563
  139.1 2.4 %collective-permute-done.8.b2 = f32[8,128]{1,0:T(8,128)S(1)} collective-permute-done((f32[8,128]{1,0:T(8,128)S(1)}, f32[8,128]{1,0:T(8,128)S(1)}, u32[]{:S(2)}, u32[]{:S(2)}) %collective-permute-start.8) | collective-permute-done | bytes 4128 | tf_op jit(solution)/shard_map/ppermute | solution.py:613
  142.1 3.0 %collective-permute-start.13 = (f32[4,8,128]{2,1,0:T(8,128)S(1)}, f32[4,8,128]{2,1,0:T(8,128)S(1)}, u32[]{:S(2)}, u32[]{:S(2)}) collective-permute-start(f32[4,8,128]{2,1,0:T(8,128)S(1)} %shard_map.66.own), channel_id=1, source_target_pairs={{0,12},{1,13},{2,14},{3,15},{4,0},{5,1},{6,2},{7,3},{8,4},{9,5},{1... | collective-permute-start | bytes 49160 | tf_op jit(solution)/shard_map/ppermute | solution.py:623
  145.2 3.9 %collective-permute-start.12 = (f32[4,8,128]{2,1,0:T(8,128)S(1)}, f32[4,8,128]{2,1,0:T(8,128)S(1)}, u32[]{:S(2)}, u32[]{:S(2)}) collective-permute-start(f32[4,8,128]{2,1,0:T(8,128)S(1)} %shard_map.66.own), channel_id=1, source_target_pairs={{0,8},{1,9},{2,10},{3,11},{4,12},{5,13},{6,14},{7,15},{8,0},{9,1},... | collective-permute-start | bytes 49160 | tf_op jit(solution)/shard_map/ppermute | solution.py:623
  150.2 5.5 %collective-permute-start.10 = (f32[4,8,128]{2,1,0:T(8,128)S(1)}, f32[4,8,128]{2,1,0:T(8,128)S(1)}, u32[]{:S(2)}, u32[]{:S(2)}) collective-permute-start(f32[4,8,128]{2,1,0:T(8,128)S(1)} %shard_map.66.own), channel_id=1, source_target_pairs={{0,0},{1,1},{2,2},{3,3},{4,4},{5,5},{6,6},{7,7},{8,8},{9,9},{10,10... | collective-permute-start | bytes 49160 | tf_op jit(solution)/shard_map/ppermute | solution.py:623
  155.7 4.3 %shard_map.65 = f32[128,2048]{1,0:T(8,128)} custom-call(f32[16,136,128]{2,1,0:T(8,128)S(1)} %all-to-all-done.3.blocks, bf16[2,256,256]{2,1,0:T(8,128)(2,1)S(1)} %copy-done.2), custom_call_target="tpu_custom_call" | custom-call | flops 1048576 | bytes 2097152 | tf_op jit(solution)/shard_map/pallas_call | solution.py:536
  160.1 3.1 %shard_map.67 = f32[256,4096]{1,0:T(8,128)} custom-call(f32[4,8,128]{2,1,0:T(8,128)S(1)} %shard_map.66.own, f32[4,8,128]{2,1,0:T(8,128)S(1)} %collective-permute-done.10.c0, f32[4,8,128]{2,1,0:T(8,128)S(1)} %collective-permute-done.11.c1, f32[4,8,128]{2,1,0:T(8,128)S(1)} %collective-permute-done.12.c2, f32[4,8,128]{2,1,0:T(8,128)S(1)} %collective-permute-done.13.c3), custom_call_target="tpu_custom_call" | custom-call | flops 8388608 | bytes 4194304 | tf_op jit(solution)/shard_map/pallas_call | solution.py:627
  (37 shorter events, 16.7 us)
Async XLA Ops:
  0.6 11.1 %copy-start.1 = (bf16[2,768,256]{2,1,0:T(8,128)(2,1)S(1)}, bf16[2,768,256]{2,1,0:T(8,128)(2,1)}, u32[]{:S(2)}) copy-start(bf16[2,768,256]{2,1,0:T(8,128)(2,1)} %constant.82.clone.toep_hbm) | copy-start | bytes 2359300
  1.4 10.3 %collective-permute-start = (f32[8,128]{1,0:T(8,128)S(1)}, f32[8,128]{1,0:T(8,128)S(1)}, u32[]{:S(2)}, u32[]{:S(2)}) collective-permute-start(f32[8,128]{1,0:T(8,128)S(1)} %reshape_squeeze.3), channel_id=1, source_target_pairs={{0,1},{1,2},{2,3},{3,4},{4,5},{5,6},{6,7},{7,8},{8,9},{9,10},{10,1... | collective-permute-start | bytes 12296 | tf_op jit(solution)/shard_map/ppermute | solution.py:578
  34.2 21.4 %collective-permute-start.1 = (f32[4,16,1024]{2,1,0:T(8,128)S(1)}, f32[4,16,1024]{2,1,0:T(8,128)S(1)}, u32[]{:S(2)}, u32[]{:S(2)}) collective-permute-start(f32[4,16,1024]{2,1,0:T(8,128)S(1)} %get-tuple-element.19), channel_id=1, source_target_pairs={{0,1},{1,2},{2,3},{3,0},{4,5},{5,6},{6,7},{7,4},{8,9},{9,10},{10,1... | collective-permute-start | bytes 786440 | tf_op jit(solution)/shard_map/ppermute | solution.py:557
  35.6 20.0 %collective-permute-start.2 = (f32[4,16,1024]{2,1,0:T(8,128)S(1)}, f32[4,16,1024]{2,1,0:T(8,128)S(1)}, u32[]{:S(2)}, u32[]{:S(2)}) collective-permute-start(f32[4,16,1024]{2,1,0:T(8,128)S(1)} %get-tuple-element.20), channel_id=1, source_target_pairs={{0,2},{1,3},{2,0},{3,1},{4,6},{5,7},{6,4},{7,5},{8,10},{9,11},{10,... | collective-permute-start | bytes 786440 | tf_op jit(solution)/shard_map/ppermute | solution.py:557
  38.5 22.8 %collective-permute-start.3 = (f32[4,16,1024]{2,1,0:T(8,128)S(1)}, f32[4,16,1024]{2,1,0:T(8,128)S(1)}, u32[]{:S(2)}, u32[]{:S(2)}) collective-permute-start(f32[4,16,1024]{2,1,0:T(8,128)S(1)} %get-tuple-element.21), channel_id=1, source_target_pairs={{0,3},{1,0},{2,1},{3,2},{4,7},{5,4},{6,5},{7,6},{8,11},{9,8},{10,9... | collective-permute-start | bytes 786440 | tf_op jit(solution)/shard_map/ppermute | solution.py:557
  62.5 20.8 %all-to-all-start.1 = ((f32[16,16,1024]{2,1,0:T(8,128)}), f32[16,16,1024]{2,1,0:T(8,128)S(1)}, u32[]{:S(2)}, u32[]{:S(2)}) async-start(f32[16,16,1024]{2,1,0:T(8,128)} %shard_map.61), calls=%async_computation.1 | async-start | bytes 2097152 | tf_op jit(solution)/shard_map/all_to_all | solution.py:563
  83.3 1.4 copy-start
  110.6 15.2 %collective-permute-start.4 = (f32[528,128]{1,0:T(8,128)S(1)}, f32[528,128]{1,0:T(8,128)S(1)}, u32[]{:S(2)}, u32[]{:S(2)}) collective-permute-start(f32[528,128]{1,0:T(8,128)S(1)} %get-tuple-element.23), channel_id=1, source_target_pairs={{0,1},{1,2},{2,3},{3,0},{4,5},{5,6},{6,7},{7,4},{8,9},{9,10},{10,1... | collective-permute-start | bytes 811016 | tf_op jit(solution)/shard_map/ppermute | solution.py:557
  113.6 14.7 %collective-permute-start.5 = (f32[528,128]{1,0:T(8,128)S(1)}, f32[528,128]{1,0:T(8,128)S(1)}, u32[]{:S(2)}, u32[]{:S(2)}) collective-permute-start(f32[528,128]{1,0:T(8,128)S(1)} %get-tuple-element.24), channel_id=1, source_target_pairs={{0,2},{1,3},{2,0},{3,1},{4,6},{5,7},{6,4},{7,5},{8,10},{9,11},{10,... | collective-permute-start | bytes 811016 | tf_op jit(solution)/shard_map/ppermute | solution.py:557
  116.4 13.8 %collective-permute-start.6 = (f32[528,128]{1,0:T(8,128)S(1)}, f32[528,128]{1,0:T(8,128)S(1)}, u32[]{:S(2)}, u32[]{:S(2)}) collective-permute-start(f32[528,128]{1,0:T(8,128)S(1)} %get-tuple-element.25), channel_id=1, source_target_pairs={{0,3},{1,0},{2,1},{3,2},{4,7},{5,4},{6,5},{7,6},{8,11},{9,8},{10,9... | collective-permute-start | bytes 811016 | tf_op jit(solution)/shard_map/ppermute | solution.py:557
  131.9 23.9 %copy-start.2 = (bf16[2,256,256]{2,1,0:T(8,128)(2,1)S(1)}, bf16[2,256,256]{2,1,0:T(8,128)(2,1)}, u32[]{:S(2)}) copy-start(bf16[2,256,256]{2,1,0:T(8,128)(2,1)} %constant.84.clone.mat) | copy-start | bytes 786436
  131.9 23.9 %all-to-all-start.3 = ((f32[16,136,128]{2,1,0:T(8,128)}), f32[16,136,128]{2,1,0:T(8,128)S(1)}, u32[]{:S(2)}, u32[]{:S(2)}) async-start(f32[16,136,128]{2,1,0:T(8,128)} %get-tuple-element.26), calls=%async_computation.3 | async-start | bytes 2228224 | tf_op jit(solution)/shard_map/all_to_all | solution.py:563
  137.8 1.3 collective-permute-start.9
  137.8 3.7 %collective-permute-start.8 = (f32[8,128]{1,0:T(8,128)S(1)}, f32[8,128]{1,0:T(8,128)S(1)}, u32[]{:S(2)}, u32[]{:S(2)}) collective-permute-start(f32[8,128]{1,0:T(8,128)S(1)} %get-tuple-element.27.b0), channel_id=1, source_target_pairs={{0,128},{64,192},{128,0},{192,64},{1,129},{65,193},{129,1},{193,65... | collective-permute-start | bytes 12296 | tf_op jit(solution)/shard_map/ppermute | solution.py:613
  139.1 3.0 %collective-permute-start.7 = (f32[8,128]{1,0:T(8,128)S(1)}, f32[8,128]{1,0:T(8,128)S(1)}, u32[]{:S(2)}, u32[]{:S(2)}) collective-permute-start(f32[8,128]{1,0:T(8,128)S(1)} %get-tuple-element.27.b0), channel_id=1, source_target_pairs={{0,64},{64,128},{128,192},{192,0},{1,65},{65,129},{129,193},{193,1... | collective-permute-start | bytes 12296 | tf_op jit(solution)/shard_map/ppermute | solution.py:613
  142.1 17.9 %collective-permute-start.13 = (f32[4,8,128]{2,1,0:T(8,128)S(1)}, f32[4,8,128]{2,1,0:T(8,128)S(1)}, u32[]{:S(2)}, u32[]{:S(2)}) collective-permute-start(f32[4,8,128]{2,1,0:T(8,128)S(1)} %shard_map.66.own), channel_id=1, source_target_pairs={{0,12},{1,13},{2,14},{3,15},{4,0},{5,1},{6,2},{7,3},{8,4},{9,5},{1... | collective-permute-start | bytes 49160 | tf_op jit(solution)/shard_map/ppermute | solution.py:623
  145.2 14.9 %collective-permute-start.12 = (f32[4,8,128]{2,1,0:T(8,128)S(1)}, f32[4,8,128]{2,1,0:T(8,128)S(1)}, u32[]{:S(2)}, u32[]{:S(2)}) collective-permute-start(f32[4,8,128]{2,1,0:T(8,128)S(1)} %shard_map.66.own), channel_id=1, source_target_pairs={{0,8},{1,9},{2,10},{3,11},{4,12},{5,13},{6,14},{7,15},{8,0},{9,1},... | collective-permute-start | bytes 49160 | tf_op jit(solution)/shard_map/ppermute | solution.py:623
  149.0 11.0 %collective-permute-start.11 = (f32[4,8,128]{2,1,0:T(8,128)S(1)}, f32[4,8,128]{2,1,0:T(8,128)S(1)}, u32[]{:S(2)}, u32[]{:S(2)}) collective-permute-start(f32[4,8,128]{2,1,0:T(8,128)S(1)} %shard_map.66.own), channel_id=1, source_target_pairs={{0,4},{1,5},{2,6},{3,7},{4,8},{5,9},{6,10},{7,11},{8,12},{9,13},{1... | collective-permute-start | bytes 49160 | tf_op jit(solution)/shard_map/ppermute | solution.py:623
  150.2 9.9 %collective-permute-start.10 = (f32[4,8,128]{2,1,0:T(8,128)S(1)}, f32[4,8,128]{2,1,0:T(8,128)S(1)}, u32[]{:S(2)}, u32[]{:S(2)}) collective-permute-start(f32[4,8,128]{2,1,0:T(8,128)S(1)} %shard_map.66.own), channel_id=1, source_target_pairs={{0,0},{1,1},{2,2},{3,3},{4,4},{5,5},{6,6},{7,7},{8,8},{9,9},{10,10... | collective-permute-start | bytes 49160 | tf_op jit(solution)/shard_map/ppermute | solution.py:623

commit v3 on v2

--- a/solution.py
+++ b/solution.py
@@ -94,16 +94,24 @@
 NT_FORM = ((1,), (1,))
 
 
-def dot_right(value, table, contract=NN):
-    high, low = halves(value)
-    dot = lambda a, b: lax.dot_general(a, b, dims(contract), preferred_element_type=F32)
-    return dot(high, table[0]) + (dot(high, table[1]) + dot(low, table[0]))
-
-
-def dot_left(table, value, contract=NN):
-    high, low = halves(value)
-    dot = lambda a, b: lax.dot_general(a, b, dims(contract), preferred_element_type=F32)
-    return dot(table[0], high) + (dot(table[1], high) + dot(table[0], low))
+def dot_right(values, tables):
+    left, right = [], []
+    for value, table in zip(values, tables):
+        high, low = halves(value)
+        left += [low, high, high]
+        right += [table[0], table[1], table[0]]
+    left, right = jnp.concatenate(left, axis=1), jnp.concatenate(right, axis=0)
+    return jnp.dot(left, right, preferred_element_type=F32)
+
+
+def dot_left(tables, values, contract=NN):
+    left, right = [], []
+    for value, table in zip(values, tables):
+        high, low = halves(value)
+        left += [table[0], table[1], table[0]]
+        right += [low, high, high]
+    left, right = jnp.concatenate(left, axis=1), jnp.concatenate(right, axis=contract[1][0])
+    return lax.dot_general(left, right, dims(contract), preferred_element_type=F32)
 
 
 def cmul(a, b):
@@ -199,23 +207,20 @@
         buf[eight(step * 8 + 8), :] = value * value + other * other
         return carry
 
-    lax.fori_loop(0, 16, fill, 0)
+    lax.fori_loop(0, 16, fill, 0, unroll=4)
     copy.wait()
     own = [halves(buf[8:136, 256 * e : 256 * e + 256]) for e in range(4)]
     back = {e: halves(buf[7:135, 256 * e : 256 * e + 256]) for e in (2, 3)}
     for e in range(4):
-        total = None
+        left, right = [], []
         for step in range(3):
             at = e - step
             high, low = own[at] if at >= 0 else back[at + 4]
-            t_high = toep[0, 256 * step : 256 * step + 256, :]
-            t_low = toep[1, 256 * step : 256 * step + 256, :]
-            term = (
-                jnp.dot(high, t_high, preferred_element_type=F32)
-                + jnp.dot(high, t_low, preferred_element_type=F32)
-                + jnp.dot(low, t_high, preferred_element_type=F32)
-            )
-            total = term if total is None else total + term
+            rows = slice(256 * step, 256 * step + 256)
+            left += [low, high, high]
+            right += [toep[0, rows, :], toep[1, rows, :], toep[0, rows, :]]
+        left, right = jnp.concatenate(left, axis=1), jnp.concatenate(right, axis=0)
+        total = jnp.dot(left, right, preferred_element_type=F32)
         lanes = slice(256 * e, 256 * e + 256)
         phase = KERR_GAIN * ((1.0 - RAMAN_SHARE) * buf[8:136, lanes] + RAMAN_SHARE * total)
         sine, cosine = sincos(phase)
@@ -268,7 +273,7 @@
             out[:, :, lanes] = scratch[j, :, :, lanes]
         return cmul(factor, forward)
 
-    lax.fori_loop(0, 8, body, phasor(number, NT, -1))
+    lax.fori_loop(0, 8, body, phasor(number, NT, -1), unroll=4)
 
 
 def mid_kernel(r0, r1, r2, r3, out):
@@ -287,7 +292,7 @@
                 out[4 * ka + kk, 8:16, lanes] = value[1]
         return cmul(factor, forward)
 
-    lax.fori_loop(0, 8, body, phasor(number, 4 * LOCAL, -1))
+    lax.fori_loop(0, 8, body, phasor(number, 4 * LOCAL, -1), unroll=4)
 
 
 def spectrum_kernel(blocks, squares, disp, out, wide, work, back, rows_w, bins, flip, flat):
@@ -295,7 +300,7 @@
     fwd_c, fwd_s, inv_c, inv_s = [squares.at[2 * k : 2 * k + 2] for k in range(2, 6)]
     for part in range(4):
         lanes = slice(256 * part, 256 * part + 256)
-        wide[:, lanes] = dot_left(hop, blocks[:, :, lanes].reshape(256, 256))
+        wide[:, lanes] = dot_left([hop], [blocks[:, :, lanes].reshape(256, 256)])
     lane_f = powers(phasor(iota((8, 256), 1), 1024, -1))
     number = [256 * part + iota((8, 256), 1) for part in range(4)]
     cross_first = tuple(phasor(iota((8, 256), 0) * n, LOCAL, -1) for n in number)
@@ -314,15 +319,12 @@
             work[at, 256:512] = y[k][1]
         return tuple(cmul(value, move) for value, move in zip(carry, cross_step))
 
-    lax.fori_loop(0, 16, body, cross_first)
+    lax.fori_loop(0, 16, body, cross_first, unroll=4)
     bins[64:128, :] = jnp.zeros((64, 256), F32)
     for k in range(4):
         rows = slice(128 * k, 128 * k + 128)
         re, im = work[rows, 0:256], work[rows, 256:512]
-        re, im = (
-            dot_right(re, fwd_c) - dot_right(im, fwd_s),
-            dot_right(re, fwd_s) + dot_right(im, fwd_c),
-        )
+        re, im = dot_right([re, -im], [fwd_c, fwd_s]), dot_right([re, im], [fwd_s, fwd_c])
         power = (re * re + im * im).reshape(16, 8, 256)
         bins[16 * k : 16 * k + 16, :] = jnp.sum(power, axis=1) * (1.0 / (NT * BIN_WIDTH))
         re, im = cmul((re, im), (disp[0, rows, :], disp[1, rows, :]))
@@ -334,8 +336,8 @@
     for dest in range(16):
         out[dest, 128:136, :] = flat[8 * dest : 8 * dest + 8, :]
     re, im = work[:, 0:256], work[:, 256:512]
-    back[0:256, :] = dot_left(inv_c, re, NT_FORM) - dot_left(inv_s, im, NT_FORM)
-    back[256:512, :] = dot_left(inv_c, im, NT_FORM) + dot_left(inv_s, re, NT_FORM)
+    back[0:256, :] = dot_left([inv_c, inv_s], [re, -im], NT_FORM)
+    back[256:512, :] = dot_left([inv_s, inv_c], [re, im], NT_FORM)
     first = phasor(16 * iota((8, 128), 0), 1024, 1)
     forward, half_turn = turn(1, 1024, 1), turn(128, 1024, 1)
     freq = iota((8, 128), 1)
@@ -361,9 +363,9 @@
                 rows_w[at, 128:256] = value[1]
         return cmul(factor, forward), cmul(other, cross_step)
 
-    lax.fori_loop(0, 16, tail, (first, cross_first))
+    lax.fori_loop(0, 16, tail, (first, cross_first), unroll=4)
     for part in range(4):
-        got = dot_right(rows_w[256 * part : 256 * part + 256, :], unhop)
+        got = dot_right([rows_w[256 * part : 256 * part + 256, :]], [unhop])
         for a in range(4):
             out[4 * part + a, 0:64, :] = got[64 * a : 64 * a + 64, 0:128]
             out[4 * part + a, 64:128, :] = got[64 * a : 64 * a + 64, 128:256]
@@ -391,7 +393,7 @@
                 out[eight(step * 8 + 128 * kk + 64), :] = value[1]
         return cmul(factor, forward)
 
-    lax.fori_loop(0, 8, body, phasor(number, 4 * LOCAL, 1))
+    lax.fori_loop(0, 8, body, phasor(number, 4 * LOCAL, 1), unroll=4)
     pick = jnp.where(iota((16, 128), 1) == 0, 1.0, 0.0).astype(BF16)
     for j in range(4):
         high, low = halves(outs[(j + 1) % 4][0:512, :])
@@ -435,7 +437,7 @@
                 out[4 * a1 + a0, eight(step * 8 + 64), :] = y[a0][a1][1]
         return cmul(factor, forward)
 
-    lax.fori_loop(0, 8, body, phasor(number, NT, 1))
+    lax.fori_loop(0, 8, body, phasor(number, NT, 1), unroll=4)
     after = (place["z"] + 1) & 3
     lane = iota((8, 128), 1)
     factors = many_powers(phasor(after * LOCAL + block + 16 * (lane & 63), NT, 1))
@@ -455,7 +457,7 @@
         out[t, 128:136, :] = jnp.where(wrap, flat[(t + 1) % 16], flat[t])
 
 
-def frames_kernel(blocks, mat, out, got):
+def frames_kernel(blocks, mat, out_hbm, got, out, sems):
     columns = jnp.concatenate([blocks[a, 128:129, :] for a in range(16)], axis=0).T
     lane = iota((128, 128), 1)
     wave = phasor(16 * iota((64, 128), 0), W, 1)
@@ -465,7 +467,7 @@
         late = 0.5 + 0.5 * wave[0]
         early = 0.5 - 0.5 * wave[0]
         pieces = [here[0:64] * early, here[64:128] * early, after[0:64] * late, after[64:128] * late]
-        got[a] = dot_left(mat, jnp.concatenate(pieces, axis=0))
+        got[a] = dot_left([mat], [jnp.concatenate(pieces, axis=0)])
         wave = cmul(wave, turn(1, W, 1))
     first = phasor(iota((8, 128), 0), W, -1)
     forward = turn(8, W, -1)
@@ -481,12 +483,19 @@
                 got[c0 + 4 * c1, rows, :] = (value[0] * value[0] + value[1] * value[1]) * (1.0 / W)
         return cmul(factor, forward)
 
-    lax.fori_loop(0, 16, body, first)
+    lax.fori_loop(0, 16, body, first, unroll=4)
+    copies = []
     for c in range(16):
         out[:, 128 * c : 128 * c + 128] = got[c, 0:128, :].T
-
-
-def normal_kernel(b0, b1, b2, b3, out):
+        if c % 4 == 3:
+            lanes = pl.ds(128 * (c - 3), 512)
+            copies.append(pltpu.make_async_copy(out.at[:, lanes], out_hbm.at[:, lanes], sems.at[c // 4]))
+            copies[-1].start()
+    for copy in copies:
+        copy.wait()
+
+
+def normal_kernel(b0, b1, b2, b3, out, side, pad):
     blocks = [b[...] for b in (b0, b1, b2, b3)]
     total = (blocks[0] + blocks[1]) + (blocks[2] + blocks[3])
     average = total * 0.25
@@ -497,26 +506,26 @@
     grp = lax.axis_index("grp")
     for step in range(4):
         out[(grp - step) & 3] = centred[step] / spread
-
-
-def correlation_kernel(own, c0, c1, c2, c3, out, side, pad, cols):
+    at = digits()["z"] * 2
+    pad[...] = jnp.zeros((128, 128), F32)
+    for r in range(4):
+        for half in range(2):
+            pad[2 * r + half : 2 * r + half + 1, :] = out[r, pl.ds(at + half, 1), :] * 0.25
+    flipped = pad[...].T
+    for r in range(4):
+        for half in range(2):
+            column = flipped[:, 2 * r + half : 2 * r + half + 1]
+            side[r, 128 * half : 128 * half + 128, :] = jnp.broadcast_to(column, (128, 128))
+
+
+def correlation_kernel(side, c0, c1, c2, c3, out, cols):
     step = pl.program_id(0)
 
     @pl.when(step == 0)
     def _():
         place = digits()
-        at = place["z"] * 2
         for s, value in enumerate((c0, c1, c2, c3)):
             cols[:, eight(((place["y"] - s) & 3) * 8), :] = value[...]
-        pad[...] = jnp.zeros((128, 128), F32)
-        for r in range(4):
-            for half in range(2):
-                pad[2 * r + half : 2 * r + half + 1, :] = own[r, pl.ds(at + half, 1), :] * 0.25
-        flipped = pad[...].T
-        for r in range(4):
-            for half in range(2):
-                column = flipped[:, 2 * r + half : 2 * r + half + 1]
-                side[r, 128 * half : 128 * half + 128, :] = jnp.broadcast_to(column, (128, 128))
 
     for half in range(2):
         base = 32 * half
@@ -531,13 +540,13 @@
                 out[at : at + 8, 128 * k : 128 * k + 128] = total
 
 
-def call(kernel, outs, scratch, *args, flops=1 << 20, specs=None):
+def call(kernel, outs, scratch, *args, flops=1 << 20, specs=None, place=VMEM):
     size = sum(int(np.prod(s)) * 4 for s in outs)
     return pl.pallas_call(
         kernel,
         out_shape=[jax.ShapeDtypeStruct(s, F32) for s in outs],
         in_specs=specs or [VMEM] * len(args),
-        out_specs=[VMEM] * len(outs),
+        out_specs=[place] * len(outs),
         scratch_shapes=[pltpu.VMEM(s, F32) if isinstance(s, tuple) else s for s in scratch],
         compiler_params=PARAMS,
         cost_estimate=pl.CostEstimate(flops=flops, bytes_accessed=2 * size, transcendentals=0),
@@ -571,7 +580,6 @@
 def on_device(seed_field):
     table = tables()
     tm = lax.axis_index("tm")
-    ix, iy, iz = tm // 16, tm // 4 % 4, tm % 4
 
     seed = seed_field.reshape(2, HOPS, HOP)
     last = seed_field[0, :, LOCAL - TAPS :].reshape(8, 128)
@@ -586,11 +594,9 @@
     )[0]
     value = swap_plane(value)
     blocks = call(fwd_kernel, [(4, 16, 1024)] * 4, [(4, 4, 16, 1024)], value)
-    blocks = swap_z(blocks)
-    value = call(mid_kernel, [FWD], [], *blocks)[0]
-    value = swap_plane(value)
+    *blocks, late = lax.optimization_barrier((*blocks, tm))
     number = (
-        (iz + 4 * iy + 16 * ix)
+        (late % 4 + 4 * (late // 4 % 4) + 16 * (late // 16))
         + 8192 * jnp.arange(4, dtype=jnp.int32)[:, None, None]
         + 64 * jnp.arange(128, dtype=jnp.int32)[None, :, None]
         + 32768 * jnp.arange(256, dtype=jnp.int32)[None, None, :]
@@ -598,6 +604,10 @@
     freq = jnp.where(number < NT // 2, number, number - NT)
     angle = (2.0 * math.pi / (1 << 28)) * (freq * freq & ((1 << 28) - 1)).astype(F32)
     disp = jnp.stack([jnp.cos(angle), jnp.sin(angle)])
+    blocks = swap_z(blocks)
+    *blocks, disp = lax.optimization_barrier((*blocks, disp))
+    value = call(mid_kernel, [FWD], [], *blocks)[0]
+    value = swap_plane(value)
     value = call(
         spectrum_kernel, [(16, 136, 128)],
         [(256, 1024), (512, 512), (512, 512), (1024, 256), (128, 256), (256, 128), (128, 128)],
@@ -612,7 +622,7 @@
     alike = [bins] + [
         lax.ppermute(bins, "grp", [(g, (g + step) % 4) for g in range(4)]) for step in (1, 2, 3)
     ]
-    normal = call(normal_kernel, [(4, 8, 128)], [], *alike)[0]
+    normal, side = call(normal_kernel, [(4, 8, 128), (4, 256, 128)], [(128, 128)], *alike)
     columns = []
     for step in range(4):
         pairs = []
@@ -622,20 +632,22 @@
                 pairs.append((g * 64 + d, x * 64 + g * 16 + (y + step) % 4 * 4 + z))
         columns.append(lax.ppermute(normal, ("grp", "tm"), pairs))
 
-    spectrogram = call(frames_kernel, [(HOPS, W)], [(16, 256, 128)], value, table["frames"])[0]
-    spectrogram, normal, *columns = lax.optimization_barrier((spectrogram, normal, *columns))
+    spectrogram = call(
+        frames_kernel, [(HOPS, W)], [(16, 256, 128), (HOPS, W), pltpu.SemaphoreType.DMA((4,))],
+        value, table["frames"], place=HBM,
+    )[0]
+    spectrogram, side, *columns = lax.optimization_barrier((spectrogram, side, *columns))
     correlation = pl.pallas_call(
         correlation_kernel,
         grid=(4,),
         out_shape=jax.ShapeDtypeStruct((256, 4096), F32),
-        in_specs=[pl.BlockSpec((4, 8, 128), lambda i: (0, 0, 0))] * 5,
+        in_specs=[pl.BlockSpec((4, 256, 128), lambda i: (0, 0, 0))]
+        + [pl.BlockSpec((4, 8, 128), lambda i: (0, 0, 0))] * 4,
         out_specs=pl.BlockSpec((64, 4096), lambda i: (i, 0)),
-        scratch_shapes=[
-            pltpu.VMEM((4, 256, 128), F32), pltpu.VMEM((128, 128), F32), pltpu.VMEM((4, 32, 128), F32)
-        ],
+        scratch_shapes=[pltpu.VMEM((4, 32, 128), F32)],
         compiler_params=PARAMS,
         cost_estimate=pl.CostEstimate(flops=1 << 23, bytes_accessed=1 << 22, transcendentals=0),
-    )(normal, *columns)
+    )(side, *columns)
     return spectrogram[None], correlation
 
 

time: 164 us -> 162 us (0.988)
    ppermute x6, waiting for transfers between devices: 29.6 us -> 27.8 us  [swap_z(): lax.ppermute(blocks[step], 'tm', ring('z', step))]
    all_to_all x2, waiting for transfers between devices: 12.5 us -> 14.2 us  [swap_plane(): lax.all_to_all(value, 'tm', split_axis=0, concat_axis=0, axis_index_group...]
  transfers between devices with their start and end apart: 16 -> 16, of which waited for: 11 -> 8; matrix products, arithmetic and copies ran while one was open for 2% -> 2% of each run, Pallas kernels for 3% -> 3%
where the time goes in v3:
time: 162 us; the launch traced here: 161 us
  waiting for transfers between devices  50.7 us (31%)
  starting transfers between devices  46.2 us (29%)
  blocking collectives  41.1 us (25%)
  Pallas kernels  17.7 us (11%)
  local copies, waits for them, and re-layouts  2.36 us (1%)
  other arithmetic  2.22 us (1%)
    all_to_all x2, blocking collectives, swap_plane(): lax.all_to_all(value, 'tm', split_axis=0, concat_axis=0, axis_index_group...  41.1 us
    ppermute x6, waiting for transfers between devices, swap_z(): lax.ppermute(blocks[step], 'tm', ring('z', step))  27.8 us
    ppermute x6, starting transfers between devices, swap_z(): lax.ppermute(blocks[step], 'tm', ring('z', step))  15.5 us
    pallas_call x8, Pallas kernels, call(): pl.pallas_call(kernel, out_shape=[jax.ShapeDtypeStruct(s, F32) for s in o...  14.9 us
    all_to_all x2, waiting for transfers between devices, swap_plane(): lax.all_to_all(value, 'tm', split_axis=0, concat_axis=0, axis_index_group...  14.2 us
    ppermute x4, starting transfers between devices, on_device(): columns.append(lax.ppermute(normal, ('grp', 'tm'), pairs))  13.5 us
    all_to_all x2, starting transfers between devices, swap_plane(): lax.all_to_all(value, 'tm', split_axis=0, concat_axis=0, axis_index_group...  13.4 us
    ppermute x1, waiting for transfers between devices, on_device(): lax.ppermute(last, 'tm', [(d, (d + 1) % 64) for d in range(64)])  5.47 us
  transfers between devices with their start and end apart: 16, of which 8 were waited for; matrix products, arithmetic and copies ran while one was open for 2% of the time, Pallas kernels for 3%

profile of v3, /device:TPU:4, one launch (start us, length us, event | category | flops | bytes accessed | tf_op | source)
XLA Modules:
  0.0 161.1 jit_solution(5518509893881164155)
XLA Ops:
  1.4 3.3 %collective-permute-start = (f32[8,128]{1,0:T(8,128)S(1)}, f32[8,128]{1,0:T(8,128)S(1)}, u32[]{:S(2)}, u32[]{:S(2)}) collective-permute-start(f32[8,128]{1,0:T(8,128)S(1)} %reshape_squeeze.3), channel_id=1, source_target_pairs={{0,1},{1,2},{2,3},{3,4},{4,5},{5,6},{6,7},{7,8},{8,9},{9,10},{10,1... | collective-permute-start | bytes 12296 | tf_op jit(solution)/shard_map/ppermute | solution.py:586
  6.3 5.5 %collective-permute-done = f32[8,128]{1,0:T(8,128)S(1)} collective-permute-done((f32[8,128]{1,0:T(8,128)S(1)}, f32[8,128]{1,0:T(8,128)S(1)}, u32[]{:S(2)}, u32[]{:S(2)}) %collective-permute-start) | collective-permute-done | bytes 4128 | tf_op jit(solution)/shard_map/ppermute | solution.py:586
  11.8 3.0 %shard_map.59 = f32[16,16,1024]{2,1,0:T(8,128)} custom-call(f32[2,128,1024]{2,1,0:T(8,128)S(1)} %bitcast.11, f32[1,512]{1,0:T(1,128)S(1)} %multiply_add_fusion.halo, bf16[2,768,256]{2,1,0:T(8,128)(2,1)S(1)} %copy-done.1), custom_call_target="tpu_custom_call" | custom-call | flops 1048576 | bytes 2097152 | tf_op jit(solution)/shard_map/pallas_call | solution.py:545
  14.8 6.2 %all-to-all-start = ((f32[16,16,1024]{2,1,0:T(8,128)}), f32[16,16,1024]{2,1,0:T(8,128)S(1)}, u32[]{:S(2)}, u32[]{:S(2)}) async-start(f32[16,16,1024]{2,1,0:T(8,128)} %shard_map.59), calls=%async_computation | async-start | bytes 2097152 | tf_op jit(solution)/shard_map/all_to_all | solution.py:572
  21.0 14.2 %all-to-all-done.blocks = f32[16,16,1024]{2,1,0:T(8,128)S(1)} async-done(((f32[16,16,1024]{2,1,0:T(8,128)}), f32[16,16,1024]{2,1,0:T(8,128)S(1)}, u32[]{:S(2)}, u32[]{:S(2)}) %all-to-all-start) | async-done | bytes 1048608 | tf_op jit(solution)/shard_map/all_to_all | solution.py:572
  36.4 3.0 %collective-permute-start.2 = (f32[4,16,1024]{2,1,0:T(8,128)S(1)}, f32[4,16,1024]{2,1,0:T(8,128)S(1)}, u32[]{:S(2)}, u32[]{:S(2)}) collective-permute-start(f32[4,16,1024]{2,1,0:T(8,128)S(1)} %get-tuple-element.36), channel_id=1, source_target_pairs={{0,2},{1,3},{2,0},{3,1},{4,6},{5,7},{6,4},{7,5},{8,10},{9,11},{10,... | collective-permute-start | bytes 786440 | tf_op jit(solution)/shard_map/ppermute | solution.py:566
  39.4 3.9 %collective-permute-start.3 = (f32[4,16,1024]{2,1,0:T(8,128)S(1)}, f32[4,16,1024]{2,1,0:T(8,128)S(1)}, u32[]{:S(2)}, u32[]{:S(2)}) collective-permute-start(f32[4,16,1024]{2,1,0:T(8,128)S(1)} %get-tuple-element.37), channel_id=1, source_target_pairs={{0,3},{1,0},{2,1},{3,2},{4,7},{5,4},{6,5},{7,6},{8,11},{9,8},{10,9... | collective-permute-start | bytes 786440 | tf_op jit(solution)/shard_map/ppermute | solution.py:566
  45.5 11.3 %collective-permute-done.1.r1 = f32[4,16,1024]{2,1,0:T(8,128)S(1)} collective-permute-done((f32[4,16,1024]{2,1,0:T(8,128)S(1)}, f32[4,16,1024]{2,1,0:T(8,128)S(1)}, u32[]{:S(2)}, u32[]{:S(2)}) %collective-permute-start.1) | collective-permute-done | bytes 262176 | tf_op jit(solution)/shard_map/ppermute | solution.py:566
  56.8 5.9 %collective-permute-done.3.r3 = f32[4,16,1024]{2,1,0:T(8,128)S(1)} collective-permute-done((f32[4,16,1024]{2,1,0:T(8,128)S(1)}, f32[4,16,1024]{2,1,0:T(8,128)S(1)}, u32[]{:S(2)}, u32[]{:S(2)}) %collective-permute-start.3) | collective-permute-done | bytes 262176 | tf_op jit(solution)/shard_map/ppermute | solution.py:566
  63.1 21.2 %all_to_all.20.blocks = f32[16,16,1024]{2,1,0:T(8,128)S(1)} all-to-all(f32[16,16,1024]{2,1,0:T(8,128)S(1)} %shard_map.61), channel_id=1, replica_groups={{0,4,8,12,16,20,24,28,32,36,40,44,48,52,56,60},{1,5,9,13,17,21,25,29,33..., dimensions={0} | all-to-all | bytes 2097152 | tf_op jit(solution)/shard_map/all_to_all | solution.py:572
  84.3 4.4 %shard_map.62 = f32[16,136,128]{2,1,0:T(8,128)S(1)} custom-call(f32[16,16,1024]{2,1,0:T(8,128)S(1)} %all_to_all.20.blocks, bf16[12,256,256]{2,1,0:T(8,128)(2,1)S(1)} %copy-done, f32[2,512,256]{2,1,0:T(8,128)S(1)} %pad_maximum_fusion.disp), custom_call_target="tpu_custom_call" | custom-call | flops 1048576 | bytes 2228224 | tf_op jit(solution)/shard_map/pallas_call | solution.py:545
  88.6 19.9 %all_to_all.21.blocks = f32[16,136,128]{2,1,0:T(8,128)S(1)} all-to-all(f32[16,136,128]{2,1,0:T(8,128)S(1)} %shard_map.62), channel_id=1, replica_groups={{0,4,8,12,16,20,24,28,32,36,40,44,48,52,56,60},{1,5,9,13,17,21,25,29,33..., dimensions={0} | all-to-all | bytes 2228224 | tf_op jit(solution)/shard_map/all_to_all | solution.py:572
  109.1 2.4 %collective-permute-start.4 = (f32[528,128]{1,0:T(8,128)S(1)}, f32[528,128]{1,0:T(8,128)S(1)}, u32[]{:S(2)}, u32[]{:S(2)}) collective-permute-start(f32[528,128]{1,0:T(8,128)S(1)} %get-tuple-element.45), channel_id=1, source_target_pairs={{0,1},{1,2},{2,3},{3,0},{4,5},{5,6},{6,7},{7,4},{8,9},{9,10},{10,1... | collective-permute-start | bytes 811016 | tf_op jit(solution)/shard_map/ppermute | solution.py:566
  111.5 3.2 %collective-permute-start.5 = (f32[528,128]{1,0:T(8,128)S(1)}, f32[528,128]{1,0:T(8,128)S(1)}, u32[]{:S(2)}, u32[]{:S(2)}) collective-permute-start(f32[528,128]{1,0:T(8,128)S(1)} %get-tuple-element.46), channel_id=1, source_target_pairs={{0,2},{1,3},{2,0},{3,1},{4,6},{5,7},{6,4},{7,5},{8,10},{9,11},{10,... | collective-permute-start | bytes 811016 | tf_op jit(solution)/shard_map/ppermute | solution.py:566
  114.7 2.5 %collective-permute-start.6 = (f32[528,128]{1,0:T(8,128)S(1)}, f32[528,128]{1,0:T(8,128)S(1)}, u32[]{:S(2)}, u32[]{:S(2)}) collective-permute-start(f32[528,128]{1,0:T(8,128)S(1)} %get-tuple-element.47), channel_id=1, source_target_pairs={{0,3},{1,0},{2,1},{3,2},{4,7},{5,4},{6,5},{7,6},{8,11},{9,8},{10,9... | collective-permute-start | bytes 811016 | tf_op jit(solution)/shard_map/ppermute | solution.py:566
  117.1 6.1 %collective-permute-done.4.r1 = f32[528,128]{1,0:T(8,128)S(1)} collective-permute-done((f32[528,128]{1,0:T(8,128)S(1)}, f32[528,128]{1,0:T(8,128)S(1)}, u32[]{:S(2)}, u32[]{:S(2)}) %collective-permute-start.4) | collective-permute-done | bytes 270368 | tf_op jit(solution)/shard_map/ppermute | solution.py:566
  123.3 4.4 %collective-permute-done.5.r2 = f32[528,128]{1,0:T(8,128)S(1)} collective-permute-done((f32[528,128]{1,0:T(8,128)S(1)}, f32[528,128]{1,0:T(8,128)S(1)}, u32[]{:S(2)}, u32[]{:S(2)}) %collective-permute-start.5) | collective-permute-done | bytes 270368 | tf_op jit(solution)/shard_map/ppermute | solution.py:566
  129.4 7.2 %all-to-all-start.3 = ((f32[16,136,128]{2,1,0:T(8,128)}), f32[16,136,128]{2,1,0:T(8,128)S(1)}, u32[]{:S(2)}, u32[]{:S(2)}) async-start(f32[16,136,128]{2,1,0:T(8,128)} %get-tuple-element.48), calls=%async_computation.3 | async-start | bytes 2228224 | tf_op jit(solution)/shard_map/all_to_all | solution.py:572
  137.9 2.4 %collective-permute-done.8.b2 = f32[8,128]{1,0:T(8,128)S(1)} collective-permute-done((f32[8,128]{1,0:T(8,128)S(1)}, f32[8,128]{1,0:T(8,128)S(1)}, u32[]{:S(2)}, u32[]{:S(2)}) %collective-permute-start.8) | collective-permute-done | bytes 4128 | tf_op jit(solution)/shard_map/ppermute | solution.py:623
  140.6 3.6 %collective-permute-start.13 = (f32[4,8,128]{2,1,0:T(8,128)S(1)}, f32[4,8,128]{2,1,0:T(8,128)S(1)}, u32[]{:S(2)}, u32[]{:S(2)}) collective-permute-start(f32[4,8,128]{2,1,0:T(8,128)S(1)} %get-tuple-element.51), channel_id=1, source_target_pairs={{0,12},{1,13},{2,14},{3,15},{4,0},{5,1},{6,2},{7,3},{8,4},{9,5},{1... | collective-permute-start | bytes 49160 | tf_op jit(solution)/shard_map/ppermute | solution.py:633
  144.2 3.3 %collective-permute-start.12 = (f32[4,8,128]{2,1,0:T(8,128)S(1)}, f32[4,8,128]{2,1,0:T(8,128)S(1)}, u32[]{:S(2)}, u32[]{:S(2)}) collective-permute-start(f32[4,8,128]{2,1,0:T(8,128)S(1)} %get-tuple-element.51), channel_id=1, source_target_pairs={{0,8},{1,9},{2,10},{3,11},{4,12},{5,13},{6,14},{7,15},{8,0},{9,1},... | collective-permute-start | bytes 49160 | tf_op jit(solution)/shard_map/ppermute | solution.py:633
  149.3 4.9 %collective-permute-start.10 = (f32[4,8,128]{2,1,0:T(8,128)S(1)}, f32[4,8,128]{2,1,0:T(8,128)S(1)}, u32[]{:S(2)}, u32[]{:S(2)}) collective-permute-start(f32[4,8,128]{2,1,0:T(8,128)S(1)} %get-tuple-element.51), channel_id=1, source_target_pairs={{0,0},{1,1},{2,2},{3,3},{4,4},{5,5},{6,6},{7,7},{8,8},{9,9},{10,10... | collective-permute-start | bytes 49160 | tf_op jit(solution)/shard_map/ppermute | solution.py:633
  154.2 4.1 %shard_map.65 = f32[128,2048]{1,0:T(8,128)} custom-call(f32[16,136,128]{2,1,0:T(8,128)S(1)} %all-to-all-done.3.blocks, bf16[2,256,256]{2,1,0:T(8,128)(2,1)S(1)} %copy-done.2), custom_call_target="tpu_custom_call" | custom-call | flops 1048576 | bytes 2097152 | tf_op jit(solution)/shard_map/pallas_call | solution.py:545
  158.3 2.8 %shard_map.67 = f32[256,4096]{1,0:T(8,128)} custom-call(f32[4,256,128]{2,1,0:T(8,128)S(1)} %get-tuple-element.53.side, f32[4,8,128]{2,1,0:T(8,128)S(1)} %collective-permute-done.10.c0, f32[4,8,128]{2,1,0:T(8,128)S(1)} %collective-permute-done.11.c1, f32[4,8,128]{2,1,0:T(8,128)S(1)} %collective-permute-done.12.c2, f32[4,8,128]{2,1,0:T(8,128)S(1)} %collective-permute-done.13.c3), custom_call_target="tpu_custom_call" | custom-call | flops 8388608 | bytes 4194304 | tf_op jit(solution)/shard_map/pallas_call | solution.py:640
  (37 shorter events, 11.8 us)
Async XLA Ops:
  0.6 11.1 %copy-start.1 = (bf16[2,768,256]{2,1,0:T(8,128)(2,1)S(1)}, bf16[2,768,256]{2,1,0:T(8,128)(2,1)}, u32[]{:S(2)}) copy-start(bf16[2,768,256]{2,1,0:T(8,128)(2,1)} %constant.82.clone.toep_hbm) | copy-start | bytes 2359300
  1.4 10.3 %collective-permute-start = (f32[8,128]{1,0:T(8,128)S(1)}, f32[8,128]{1,0:T(8,128)S(1)}, u32[]{:S(2)}, u32[]{:S(2)}) collective-permute-start(f32[8,128]{1,0:T(8,128)S(1)} %reshape_squeeze.3), channel_id=1, source_target_pairs={{0,1},{1,2},{2,3},{3,4},{4,5},{5,6},{6,7},{7,8},{8,9},{9,10},{10,1... | collective-permute-start | bytes 12296 | tf_op jit(solution)/shard_map/ppermute | solution.py:586
  14.8 20.4 %all-to-all-start = ((f32[16,16,1024]{2,1,0:T(8,128)}), f32[16,16,1024]{2,1,0:T(8,128)S(1)}, u32[]{:S(2)}, u32[]{:S(2)}) async-start(f32[16,16,1024]{2,1,0:T(8,128)} %shard_map.59), calls=%async_computation | async-start | bytes 2097152 | tf_op jit(solution)/shard_map/all_to_all | solution.py:572
  35.8 21.0 %collective-permute-start.1 = (f32[4,16,1024]{2,1,0:T(8,128)S(1)}, f32[4,16,1024]{2,1,0:T(8,128)S(1)}, u32[]{:S(2)}, u32[]{:S(2)}) collective-permute-start(f32[4,16,1024]{2,1,0:T(8,128)S(1)} %get-tuple-element.35), channel_id=1, source_target_pairs={{0,1},{1,2},{2,3},{3,0},{4,5},{5,6},{6,7},{7,4},{8,9},{9,10},{10,1... | collective-permute-start | bytes 786440 | tf_op jit(solution)/shard_map/ppermute | solution.py:566
  36.4 20.4 %collective-permute-start.2 = (f32[4,16,1024]{2,1,0:T(8,128)S(1)}, f32[4,16,1024]{2,1,0:T(8,128)S(1)}, u32[]{:S(2)}, u32[]{:S(2)}) collective-permute-start(f32[4,16,1024]{2,1,0:T(8,128)S(1)} %get-tuple-element.36), channel_id=1, source_target_pairs={{0,2},{1,3},{2,0},{3,1},{4,6},{5,7},{6,4},{7,5},{8,10},{9,11},{10,... | collective-permute-start | bytes 786440 | tf_op jit(solution)/shard_map/ppermute | solution.py:566
  39.4 23.3 %collective-permute-start.3 = (f32[4,16,1024]{2,1,0:T(8,128)S(1)}, f32[4,16,1024]{2,1,0:T(8,128)S(1)}, u32[]{:S(2)}, u32[]{:S(2)}) collective-permute-start(f32[4,16,1024]{2,1,0:T(8,128)S(1)} %get-tuple-element.37), channel_id=1, source_target_pairs={{0,3},{1,0},{2,1},{3,2},{4,7},{5,4},{6,5},{7,6},{8,11},{9,8},{10,9... | collective-permute-start | bytes 786440 | tf_op jit(solution)/shard_map/ppermute | solution.py:566
  63.1 21.2 %copy-start = (bf16[12,256,256]{2,1,0:T(8,128)(2,1)S(1)}, bf16[12,256,256]{2,1,0:T(8,128)(2,1)}, u32[]{:S(2)}) copy-start(bf16[12,256,256]{2,1,0:T(8,128)(2,1)} %constant.83.clone.squares) | copy-start | bytes 4718596
  109.1 14.2 %collective-permute-start.4 = (f32[528,128]{1,0:T(8,128)S(1)}, f32[528,128]{1,0:T(8,128)S(1)}, u32[]{:S(2)}, u32[]{:S(2)}) collective-permute-start(f32[528,128]{1,0:T(8,128)S(1)} %get-tuple-element.45), channel_id=1, source_target_pairs={{0,1},{1,2},{2,3},{3,0},{4,5},{5,6},{6,7},{7,4},{8,9},{9,10},{10,1... | collective-permute-start | bytes 811016 | tf_op jit(solution)/shard_map/ppermute | solution.py:566
  111.5 16.2 %collective-permute-start.5 = (f32[528,128]{1,0:T(8,128)S(1)}, f32[528,128]{1,0:T(8,128)S(1)}, u32[]{:S(2)}, u32[]{:S(2)}) collective-permute-start(f32[528,128]{1,0:T(8,128)S(1)} %get-tuple-element.46), channel_id=1, source_target_pairs={{0,2},{1,3},{2,0},{3,1},{4,6},{5,7},{6,4},{7,5},{8,10},{9,11},{10,... | collective-permute-start | bytes 811016 | tf_op jit(solution)/shard_map/ppermute | solution.py:566
  114.7 13.0 %collective-permute-start.6 = (f32[528,128]{1,0:T(8,128)S(1)}, f32[528,128]{1,0:T(8,128)S(1)}, u32[]{:S(2)}, u32[]{:S(2)}) collective-permute-start(f32[528,128]{1,0:T(8,128)S(1)} %get-tuple-element.47), channel_id=1, source_target_pairs={{0,3},{1,0},{2,1},{3,2},{4,7},{5,4},{6,5},{7,6},{8,11},{9,8},{10,9... | collective-permute-start | bytes 811016 | tf_op jit(solution)/shard_map/ppermute | solution.py:566
  129.4 24.8 %copy-start.2 = (bf16[2,256,256]{2,1,0:T(8,128)(2,1)S(1)}, bf16[2,256,256]{2,1,0:T(8,128)(2,1)}, u32[]{:S(2)}) copy-start(bf16[2,256,256]{2,1,0:T(8,128)(2,1)} %constant.84.clone.mat) | copy-start | bytes 786436
  129.4 24.8 %all-to-all-start.3 = ((f32[16,136,128]{2,1,0:T(8,128)}), f32[16,136,128]{2,1,0:T(8,128)S(1)}, u32[]{:S(2)}, u32[]{:S(2)}) async-start(f32[16,136,128]{2,1,0:T(8,128)} %get-tuple-element.48), calls=%async_computation.3 | async-start | bytes 2228224 | tf_op jit(solution)/shard_map/all_to_all | solution.py:572
  136.5 1.3 collective-permute-start.9
  136.5 3.7 %collective-permute-start.8 = (f32[8,128]{1,0:T(8,128)S(1)}, f32[8,128]{1,0:T(8,128)S(1)}, u32[]{:S(2)}, u32[]{:S(2)}) collective-permute-start(f32[8,128]{1,0:T(8,128)S(1)} %get-tuple-element.49.b0), channel_id=1, source_target_pairs={{0,128},{64,192},{128,0},{192,64},{1,129},{65,193},{129,1},{193,65... | collective-permute-start | bytes 12296 | tf_op jit(solution)/shard_map/ppermute | solution.py:623
  136.6 3.6 %collective-permute-start.7 = (f32[8,128]{1,0:T(8,128)S(1)}, f32[8,128]{1,0:T(8,128)S(1)}, u32[]{:S(2)}, u32[]{:S(2)}) collective-permute-start(f32[8,128]{1,0:T(8,128)S(1)} %get-tuple-element.49.b0), channel_id=1, source_target_pairs={{0,64},{64,128},{128,192},{192,0},{1,65},{65,129},{129,193},{193,1... | collective-permute-start | bytes 12296 | tf_op jit(solution)/shard_map/ppermute | solution.py:623
  140.6 17.6 %collective-permute-start.13 = (f32[4,8,128]{2,1,0:T(8,128)S(1)}, f32[4,8,128]{2,1,0:T(8,128)S(1)}, u32[]{:S(2)}, u32[]{:S(2)}) collective-permute-start(f32[4,8,128]{2,1,0:T(8,128)S(1)} %get-tuple-element.51), channel_id=1, source_target_pairs={{0,12},{1,13},{2,14},{3,15},{4,0},{5,1},{6,2},{7,3},{8,4},{9,5},{1... | collective-permute-start | bytes 49160 | tf_op jit(solution)/shard_map/ppermute | solution.py:633
  144.2 14.0 %collective-permute-start.12 = (f32[4,8,128]{2,1,0:T(8,128)S(1)}, f32[4,8,128]{2,1,0:T(8,128)S(1)}, u32[]{:S(2)}, u32[]{:S(2)}) collective-permute-start(f32[4,8,128]{2,1,0:T(8,128)S(1)} %get-tuple-element.51), channel_id=1, source_target_pairs={{0,8},{1,9},{2,10},{3,11},{4,12},{5,13},{6,14},{7,15},{8,0},{9,1},... | collective-permute-start | bytes 49160 | tf_op jit(solution)/shard_map/ppermute | solution.py:633
  147.5 10.7 %collective-permute-start.11 = (f32[4,8,128]{2,1,0:T(8,128)S(1)}, f32[4,8,128]{2,1,0:T(8,128)S(1)}, u32[]{:S(2)}, u32[]{:S(2)}) collective-permute-start(f32[4,8,128]{2,1,0:T(8,128)S(1)} %get-tuple-element.51), channel_id=1, source_target_pairs={{0,4},{1,5},{2,6},{3,7},{4,8},{5,9},{6,10},{7,11},{8,12},{9,13},{1... | collective-permute-start | bytes 49160 | tf_op jit(solution)/shard_map/ppermute | solution.py:633
  149.3 9.0 %collective-permute-start.10 = (f32[4,8,128]{2,1,0:T(8,128)S(1)}, f32[4,8,128]{2,1,0:T(8,128)S(1)}, u32[]{:S(2)}, u32[]{:S(2)}) collective-permute-start(f32[4,8,128]{2,1,0:T(8,128)S(1)} %get-tuple-element.51), channel_id=1, source_target_pairs={{0,0},{1,1},{2,2},{3,3},{4,4},{5,5},{6,6},{7,7},{8,8},{9,9},{10,10... | collective-permute-start | bytes 49160 | tf_op jit(solution)/shard_map/ppermute | solution.py:633

commit v4 on v3

--- a/solution.py
+++ b/solution.py
@@ -595,12 +595,14 @@
     value = swap_plane(value)
     blocks = call(fwd_kernel, [(4, 16, 1024)] * 4, [(4, 4, 16, 1024)], value)
     *blocks, late = lax.optimization_barrier((*blocks, tm))
+    row = lax.broadcasted_iota(jnp.int32, (512, 256), 0)
     number = (
         (late % 4 + 4 * (late // 4 % 4) + 16 * (late // 16))
-        + 8192 * jnp.arange(4, dtype=jnp.int32)[:, None, None]
-        + 64 * jnp.arange(128, dtype=jnp.int32)[None, :, None]
-        + 32768 * jnp.arange(256, dtype=jnp.int32)[None, None, :]
-    ).reshape(512, 256)
+        + 64 * (row & 127)
+        + 8192 * (row >> 7)
+        + 32768 * late
+        + 32768 * (lax.broadcasted_iota(jnp.int32, (512, 256), 1) - late)
+    )
     freq = jnp.where(number < NT // 2, number, number - NT)
     angle = (2.0 * math.pi / (1 << 28)) * (freq * freq & ((1 << 28) - 1)).astype(F32)
     disp = jnp.stack([jnp.cos(angle), jnp.sin(angle)])

time: 162 us -> 159 us (0.981)
  blocking collectives: 41.1 us -> 59.8 us
  waiting for transfers between devices: 50.7 us -> 34.9 us
  starting transfers between devices: 46.2 us -> 40.5 us
    all_to_all x2 -> x3, blocking collectives: 41.1 us -> 59.8 us  [swap_plane(): lax.all_to_all(value, 'tm', split_axis=0, concat_axis=0, axis_index_group...]
    all_to_all x2 -> x1, waiting for transfers between devices: 14.2 us -> 0.01 us  [swap_plane(): lax.all_to_all(value, 'tm', split_axis=0, concat_axis=0, axis_index_group...]
    all_to_all x2 -> x1, starting transfers between devices: 13.4 us -> 5.95 us  [swap_plane(): lax.all_to_all(value, 'tm', split_axis=0, concat_axis=0, axis_index_group...]
    ppermute x6, starting transfers between devices: 15.5 us -> 17.3 us  [swap_z(): lax.ppermute(blocks[step], 'tm', ring('z', step))]
    ppermute x6, waiting for transfers between devices: 27.8 us -> 26.2 us  [swap_z(): lax.ppermute(blocks[step], 'tm', ring('z', step))]
  transfers between devices with their start and end apart: 16 -> 15, of which waited for: 8 -> 7; matrix products, arithmetic and copies ran while one was open for 2% -> 2% of each run, Pallas kernels for 3% -> 3%
where the time goes in v4:
time: 159 us; the launch traced here: 157 us
  blocking collectives  59.8 us (38%)
  starting transfers between devices  40.5 us (25%)
  waiting for transfers between devices  34.9 us (22%)
  Pallas kernels  16.7 us (11%)
  local copies, waits for them, and re-layouts  2.35 us (1%)
  other arithmetic  2.15 us (1%)
    all_to_all x3, blocking collectives, swap_plane(): lax.all_to_all(value, 'tm', split_axis=0, concat_axis=0, axis_index_group...  59.8 us
    ppermute x6, waiting for transfers between devices, swap_z(): lax.ppermute(blocks[step], 'tm', ring('z', step))  26.2 us
    ppermute x6, starting transfers between devices, swap_z(): lax.ppermute(blocks[step], 'tm', ring('z', step))  17.3 us
    pallas_call x8, Pallas kernels, call(): pl.pallas_call(kernel, out_shape=[jax.ShapeDtypeStruct(s, F32) for s in o...  13.9 us
    ppermute x4, starting transfers between devices, on_device(): columns.append(lax.ppermute(normal, ('grp', 'tm'), pairs))  13.5 us
    all_to_all x1, starting transfers between devices, swap_plane(): lax.all_to_all(value, 'tm', split_axis=0, concat_axis=0, axis_index_group...  5.95 us
    ppermute x1, waiting for transfers between devices, on_device(): lax.ppermute(last, 'tm', [(d, (d + 1) % 64) for d in range(64)])  5.47 us
    ppermute x1, starting transfers between devices, on_device(): lax.ppermute(last, 'tm', [(d, (d + 1) % 64) for d in range(64)])  3.27 us
  transfers between devices with their start and end apart: 15, of which 7 were waited for; matrix products, arithmetic and copies ran while one was open for 2% of the time, Pallas kernels for 3%

profile of v4, /device:TPU:4, one launch (start us, length us, event | category | flops | bytes accessed | tf_op | source)
XLA Modules:
  0.0 157.3 jit_solution(3389991903481247042)
XLA Ops:
  1.4 3.3 %collective-permute-start = (f32[8,128]{1,0:T(8,128)S(1)}, f32[8,128]{1,0:T(8,128)S(1)}, u32[]{:S(2)}, u32[]{:S(2)}) collective-permute-start(f32[8,128]{1,0:T(8,128)S(1)} %reshape_squeeze.3), channel_id=1, source_target_pairs={{0,1},{1,2},{2,3},{3,4},{4,5},{5,6},{6,7},{7,8},{8,9},{9,10},{10,1... | collective-permute-start | bytes 12296 | tf_op jit(solution)/shard_map/ppermute | solution.py:586
  6.3 5.5 %collective-permute-done = f32[8,128]{1,0:T(8,128)S(1)} collective-permute-done((f32[8,128]{1,0:T(8,128)S(1)}, f32[8,128]{1,0:T(8,128)S(1)}, u32[]{:S(2)}, u32[]{:S(2)}) %collective-permute-start) | collective-permute-done | bytes 4128 | tf_op jit(solution)/shard_map/ppermute | solution.py:586
  11.8 2.0 %shard_map.59 = f32[16,16,1024]{2,1,0:T(8,128)S(1)} custom-call(f32[2,128,1024]{2,1,0:T(8,128)S(1)} %bitcast.8, f32[1,512]{1,0:T(1,128)S(1)} %multiply_add_fusion.halo, bf16[2,768,256]{2,1,0:T(8,128)(2,1)S(1)} %copy-done.1), custom_call_target="tpu_custom_call" | custom-call | flops 1048576 | bytes 2097152 | tf_op jit(solution)/shard_map/pallas_call | solution.py:545
  13.8 19.4 %all_to_all.20.blocks = f32[16,16,1024]{2,1,0:T(8,128)S(1)} all-to-all(f32[16,16,1024]{2,1,0:T(8,128)S(1)} %shard_map.59), channel_id=1, replica_groups={{0,4,8,12,16,20,24,28,32,36,40,44,48,52,56,60},{1,5,9,13,17,21,25,29,33..., dimensions={0} | all-to-all | bytes 2097152 | tf_op jit(solution)/shard_map/all_to_all | solution.py:572
  35.3 2.9 %collective-permute-start.2 = (f32[4,16,1024]{2,1,0:T(8,128)S(1)}, f32[4,16,1024]{2,1,0:T(8,128)S(1)}, u32[]{:S(2)}, u32[]{:S(2)}) collective-permute-start(f32[4,16,1024]{2,1,0:T(8,128)S(1)} %get-tuple-element.36), channel_id=1, source_target_pairs={{0,2},{1,3},{2,0},{3,1},{4,6},{5,7},{6,4},{7,5},{8,10},{9,11},{10,... | collective-permute-start | bytes 786440 | tf_op jit(solution)/shard_map/ppermute | solution.py:566
  38.2 3.9 %collective-permute-start.3 = (f32[4,16,1024]{2,1,0:T(8,128)S(1)}, f32[4,16,1024]{2,1,0:T(8,128)S(1)}, u32[]{:S(2)}, u32[]{:S(2)}) collective-permute-start(f32[4,16,1024]{2,1,0:T(8,128)S(1)} %get-tuple-element.37), channel_id=1, source_target_pairs={{0,3},{1,0},{2,1},{3,2},{4,7},{5,4},{6,5},{7,6},{8,11},{9,8},{10,9... | collective-permute-start | bytes 786440 | tf_op jit(solution)/shard_map/ppermute | solution.py:566
  42.0 2.0 %fusion.5 = (f32[1,512,256]{2,1,0:T(8,128)S(1)}, f32[1,512,256]{2,1,0:T(8,128)S(1)}) fusion(s32[256]{0:T(256)S(1)} %subtract_multiply_fusion, s32[512]{0:T(512)S(1)} %add_add_fusion), kind=kLoop, calls=%fused_computation.8 | loop fusion | flops 1048576 | bytes 1051648 | tf_op jit(solution)/shard_map/cos | solution.py:608
  44.1 11.1 %collective-permute-done.1.r1 = f32[4,16,1024]{2,1,0:T(8,128)S(1)} collective-permute-done((f32[4,16,1024]{2,1,0:T(8,128)S(1)}, f32[4,16,1024]{2,1,0:T(8,128)S(1)}, u32[]{:S(2)}, u32[]{:S(2)}) %collective-permute-start.1) | collective-permute-done | bytes 262176 | tf_op jit(solution)/shard_map/ppermute | solution.py:566
  55.3 5.6 %collective-permute-done.3.r3 = f32[4,16,1024]{2,1,0:T(8,128)S(1)} collective-permute-done((f32[4,16,1024]{2,1,0:T(8,128)S(1)}, f32[4,16,1024]{2,1,0:T(8,128)S(1)}, u32[]{:S(2)}, u32[]{:S(2)}) %collective-permute-start.3) | collective-permute-done | bytes 262176 | tf_op jit(solution)/shard_map/ppermute | solution.py:566
  61.3 20.5 %all_to_all.21.blocks = f32[16,16,1024]{2,1,0:T(8,128)S(1)} all-to-all(f32[16,16,1024]{2,1,0:T(8,128)S(1)} %shard_map.61), channel_id=1, replica_groups={{0,4,8,12,16,20,24,28,32,36,40,44,48,52,56,60},{1,5,9,13,17,21,25,29,33..., dimensions={0} | all-to-all | bytes 2097152 | tf_op jit(solution)/shard_map/all_to_all | solution.py:572
  81.8 4.4 %shard_map.62 = f32[16,136,128]{2,1,0:T(8,128)S(1)} custom-call(f32[16,16,1024]{2,1,0:T(8,128)S(1)} %all_to_all.21.blocks, bf16[12,256,256]{2,1,0:T(8,128)(2,1)S(1)} %copy-done, f32[2,512,256]{2,1,0:T(8,128)S(1)} %pad_maximum_fusion.disp), custom_call_target="tpu_custom_call" | custom-call | flops 1048576 | bytes 2228224 | tf_op jit(solution)/shard_map/pallas_call | solution.py:545
  86.2 19.8 %all_to_all.22.blocks = f32[16,136,128]{2,1,0:T(8,128)S(1)} all-to-all(f32[16,136,128]{2,1,0:T(8,128)S(1)} %shard_map.62), channel_id=1, replica_groups={{0,4,8,12,16,20,24,28,32,36,40,44,48,52,56,60},{1,5,9,13,17,21,25,29,33..., dimensions={0} | all-to-all | bytes 2228224 | tf_op jit(solution)/shard_map/all_to_all | solution.py:572
  106.6 3.3 %collective-permute-start.4 = (f32[528,128]{1,0:T(8,128)S(1)}, f32[528,128]{1,0:T(8,128)S(1)}, u32[]{:S(2)}, u32[]{:S(2)}) collective-permute-start(f32[528,128]{1,0:T(8,128)S(1)} %get-tuple-element.45), channel_id=1, source_target_pairs={{0,1},{1,2},{2,3},{3,0},{4,5},{5,6},{6,7},{7,4},{8,9},{9,10},{10,1... | collective-permute-start | bytes 811016 | tf_op jit(solution)/shard_map/ppermute | solution.py:566
  109.9 2.7 %collective-permute-start.5 = (f32[528,128]{1,0:T(8,128)S(1)}, f32[528,128]{1,0:T(8,128)S(1)}, u32[]{:S(2)}, u32[]{:S(2)}) collective-permute-start(f32[528,128]{1,0:T(8,128)S(1)} %get-tuple-element.46), channel_id=1, source_target_pairs={{0,2},{1,3},{2,0},{3,1},{4,6},{5,7},{6,4},{7,5},{8,10},{9,11},{10,... | collective-permute-start | bytes 811016 | tf_op jit(solution)/shard_map/ppermute | solution.py:566
  112.6 3.1 %collective-permute-start.6 = (f32[528,128]{1,0:T(8,128)S(1)}, f32[528,128]{1,0:T(8,128)S(1)}, u32[]{:S(2)}, u32[]{:S(2)}) collective-permute-start(f32[528,128]{1,0:T(8,128)S(1)} %get-tuple-element.47), channel_id=1, source_target_pairs={{0,3},{1,0},{2,1},{3,2},{4,7},{5,4},{6,5},{7,6},{8,11},{9,8},{10,9... | collective-permute-start | bytes 811016 | tf_op jit(solution)/shard_map/ppermute | solution.py:566
  115.7 4.1 %collective-permute-done.4.r1 = f32[528,128]{1,0:T(8,128)S(1)} collective-permute-done((f32[528,128]{1,0:T(8,128)S(1)}, f32[528,128]{1,0:T(8,128)S(1)}, u32[]{:S(2)}, u32[]{:S(2)}) %collective-permute-start.4) | collective-permute-done | bytes 270368 | tf_op jit(solution)/shard_map/ppermute | solution.py:566
  119.7 5.4 %collective-permute-done.5.r2 = f32[528,128]{1,0:T(8,128)S(1)} collective-permute-done((f32[528,128]{1,0:T(8,128)S(1)}, f32[528,128]{1,0:T(8,128)S(1)}, u32[]{:S(2)}, u32[]{:S(2)}) %collective-permute-start.5) | collective-permute-done | bytes 270368 | tf_op jit(solution)/shard_map/ppermute | solution.py:566
  126.7 6.0 %all-to-all-start.3 = ((f32[16,136,128]{2,1,0:T(8,128)}), f32[16,136,128]{2,1,0:T(8,128)S(1)}, u32[]{:S(2)}, u32[]{:S(2)}) async-start(f32[16,136,128]{2,1,0:T(8,128)} %get-tuple-element.48), calls=%async_computation.3 | async-start | bytes 2228224 | tf_op jit(solution)/shard_map/all_to_all | solution.py:572
  134.0 2.4 %collective-permute-done.8.b2 = f32[8,128]{1,0:T(8,128)S(1)} collective-permute-done((f32[8,128]{1,0:T(8,128)S(1)}, f32[8,128]{1,0:T(8,128)S(1)}, u32[]{:S(2)}, u32[]{:S(2)}) %collective-permute-start.8) | collective-permute-done | bytes 4128 | tf_op jit(solution)/shard_map/ppermute | solution.py:625
  136.8 3.6 %collective-permute-start.13 = (f32[4,8,128]{2,1,0:T(8,128)S(1)}, f32[4,8,128]{2,1,0:T(8,128)S(1)}, u32[]{:S(2)}, u32[]{:S(2)}) collective-permute-start(f32[4,8,128]{2,1,0:T(8,128)S(1)} %get-tuple-element.51), channel_id=1, source_target_pairs={{0,12},{1,13},{2,14},{3,15},{4,0},{5,1},{6,2},{7,3},{8,4},{9,5},{1... | collective-permute-start | bytes 49160 | tf_op jit(solution)/shard_map/ppermute | solution.py:635
  140.4 3.3 %collective-permute-start.12 = (f32[4,8,128]{2,1,0:T(8,128)S(1)}, f32[4,8,128]{2,1,0:T(8,128)S(1)}, u32[]{:S(2)}, u32[]{:S(2)}) collective-permute-start(f32[4,8,128]{2,1,0:T(8,128)S(1)} %get-tuple-element.51), channel_id=1, source_target_pairs={{0,8},{1,9},{2,10},{3,11},{4,12},{5,13},{6,14},{7,15},{8,0},{9,1},... | collective-permute-start | bytes 49160 | tf_op jit(solution)/shard_map/ppermute | solution.py:635
  145.4 4.9 %collective-permute-start.10 = (f32[4,8,128]{2,1,0:T(8,128)S(1)}, f32[4,8,128]{2,1,0:T(8,128)S(1)}, u32[]{:S(2)}, u32[]{:S(2)}) collective-permute-start(f32[4,8,128]{2,1,0:T(8,128)S(1)} %get-tuple-element.51), channel_id=1, source_target_pairs={{0,0},{1,1},{2,2},{3,3},{4,4},{5,5},{6,6},{7,7},{8,8},{9,9},{10,10... | collective-permute-start | bytes 49160 | tf_op jit(solution)/shard_map/ppermute | solution.py:635
  150.3 4.1 %shard_map.65 = f32[128,2048]{1,0:T(8,128)} custom-call(f32[16,136,128]{2,1,0:T(8,128)S(1)} %all-to-all-done.3.blocks, bf16[2,256,256]{2,1,0:T(8,128)(2,1)S(1)} %copy-done.2), custom_call_target="tpu_custom_call" | custom-call | flops 1048576 | bytes 2097152 | tf_op jit(solution)/shard_map/pallas_call | solution.py:545
  154.4 2.8 %shard_map.67 = f32[256,4096]{1,0:T(8,128)} custom-call(f32[4,256,128]{2,1,0:T(8,128)S(1)} %get-tuple-element.53.side, f32[4,8,128]{2,1,0:T(8,128)S(1)} %collective-permute-done.10.c0, f32[4,8,128]{2,1,0:T(8,128)S(1)} %collective-permute-done.11.c1, f32[4,8,128]{2,1,0:T(8,128)S(1)} %collective-permute-done.12.c2, f32[4,8,128]{2,1,0:T(8,128)S(1)} %collective-permute-done.13.c3), custom_call_target="tpu_custom_call" | custom-call | flops 8388608 | bytes 4194304 | tf_op jit(solution)/shard_map/pallas_call | solution.py:642
  (33 shorter events, 10.5 us)
Async XLA Ops:
  0.6 11.1 %copy-start.1 = (bf16[2,768,256]{2,1,0:T(8,128)(2,1)S(1)}, bf16[2,768,256]{2,1,0:T(8,128)(2,1)}, u32[]{:S(2)}) copy-start(bf16[2,768,256]{2,1,0:T(8,128)(2,1)} %constant.87.clone.toep_hbm) | copy-start | bytes 2359300
  1.4 10.3 %collective-permute-start = (f32[8,128]{1,0:T(8,128)S(1)}, f32[8,128]{1,0:T(8,128)S(1)}, u32[]{:S(2)}, u32[]{:S(2)}) collective-permute-start(f32[8,128]{1,0:T(8,128)S(1)} %reshape_squeeze.3), channel_id=1, source_target_pairs={{0,1},{1,2},{2,3},{3,4},{4,5},{5,6},{6,7},{7,8},{8,9},{9,10},{10,1... | collective-permute-start | bytes 12296 | tf_op jit(solution)/shard_map/ppermute | solution.py:586
  33.9 21.4 %collective-permute-start.1 = (f32[4,16,1024]{2,1,0:T(8,128)S(1)}, f32[4,16,1024]{2,1,0:T(8,128)S(1)}, u32[]{:S(2)}, u32[]{:S(2)}) collective-permute-start(f32[4,16,1024]{2,1,0:T(8,128)S(1)} %get-tuple-element.35), channel_id=1, source_target_pairs={{0,1},{1,2},{2,3},{3,0},{4,5},{5,6},{6,7},{7,4},{8,9},{9,10},{10,1... | collective-permute-start | bytes 786440 | tf_op jit(solution)/shard_map/ppermute | solution.py:566
  35.3 20.0 %collective-permute-start.2 = (f32[4,16,1024]{2,1,0:T(8,128)S(1)}, f32[4,16,1024]{2,1,0:T(8,128)S(1)}, u32[]{:S(2)}, u32[]{:S(2)}) collective-permute-start(f32[4,16,1024]{2,1,0:T(8,128)S(1)} %get-tuple-element.36), channel_id=1, source_target_pairs={{0,2},{1,3},{2,0},{3,1},{4,6},{5,7},{6,4},{7,5},{8,10},{9,11},{10,... | collective-permute-start | bytes 786440 | tf_op jit(solution)/shard_map/ppermute | solution.py:566
  38.2 22.7 %collective-permute-start.3 = (f32[4,16,1024]{2,1,0:T(8,128)S(1)}, f32[4,16,1024]{2,1,0:T(8,128)S(1)}, u32[]{:S(2)}, u32[]{:S(2)}) collective-permute-start(f32[4,16,1024]{2,1,0:T(8,128)S(1)} %get-tuple-element.37), channel_id=1, source_target_pairs={{0,3},{1,0},{2,1},{3,2},{4,7},{5,4},{6,5},{7,6},{8,11},{9,8},{10,9... | collective-permute-start | bytes 786440 | tf_op jit(solution)/shard_map/ppermute | solution.py:566
  61.2 20.6 %copy-start = (bf16[12,256,256]{2,1,0:T(8,128)(2,1)S(1)}, bf16[12,256,256]{2,1,0:T(8,128)(2,1)}, u32[]{:S(2)}) copy-start(bf16[12,256,256]{2,1,0:T(8,128)(2,1)} %constant.88.clone.squares) | copy-start | bytes 4718596
  106.6 13.2 %collective-permute-start.4 = (f32[528,128]{1,0:T(8,128)S(1)}, f32[528,128]{1,0:T(8,128)S(1)}, u32[]{:S(2)}, u32[]{:S(2)}) collective-permute-start(f32[528,128]{1,0:T(8,128)S(1)} %get-tuple-element.45), channel_id=1, source_target_pairs={{0,1},{1,2},{2,3},{3,0},{4,5},{5,6},{6,7},{7,4},{8,9},{9,10},{10,1... | collective-permute-start | bytes 811016 | tf_op jit(solution)/shard_map/ppermute | solution.py:566
  109.9 15.2 %collective-permute-start.5 = (f32[528,128]{1,0:T(8,128)S(1)}, f32[528,128]{1,0:T(8,128)S(1)}, u32[]{:S(2)}, u32[]{:S(2)}) collective-permute-start(f32[528,128]{1,0:T(8,128)S(1)} %get-tuple-element.46), channel_id=1, source_target_pairs={{0,2},{1,3},{2,0},{3,1},{4,6},{5,7},{6,4},{7,5},{8,10},{9,11},{10,... | collective-permute-start | bytes 811016 | tf_op jit(solution)/shard_map/ppermute | solution.py:566
  112.6 12.5 %collective-permute-start.6 = (f32[528,128]{1,0:T(8,128)S(1)}, f32[528,128]{1,0:T(8,128)S(1)}, u32[]{:S(2)}, u32[]{:S(2)}) collective-permute-start(f32[528,128]{1,0:T(8,128)S(1)} %get-tuple-element.47), channel_id=1, source_target_pairs={{0,3},{1,0},{2,1},{3,2},{4,7},{5,4},{6,5},{7,6},{8,11},{9,8},{10,9... | collective-permute-start | bytes 811016 | tf_op jit(solution)/shard_map/ppermute | solution.py:566
  126.7 23.6 %copy-start.2 = (bf16[2,256,256]{2,1,0:T(8,128)(2,1)S(1)}, bf16[2,256,256]{2,1,0:T(8,128)(2,1)}, u32[]{:S(2)}) copy-start(bf16[2,256,256]{2,1,0:T(8,128)(2,1)} %constant.89.clone.mat) | copy-start | bytes 786436
  126.7 23.6 %all-to-all-start.3 = ((f32[16,136,128]{2,1,0:T(8,128)}), f32[16,136,128]{2,1,0:T(8,128)S(1)}, u32[]{:S(2)}, u32[]{:S(2)}) async-start(f32[16,136,128]{2,1,0:T(8,128)} %get-tuple-element.48), calls=%async_computation.3 | async-start | bytes 2228224 | tf_op jit(solution)/shard_map/all_to_all | solution.py:572
  132.7 1.3 collective-permute-start.9
  132.7 3.7 %collective-permute-start.8 = (f32[8,128]{1,0:T(8,128)S(1)}, f32[8,128]{1,0:T(8,128)S(1)}, u32[]{:S(2)}, u32[]{:S(2)}) collective-permute-start(f32[8,128]{1,0:T(8,128)S(1)} %get-tuple-element.49.b0), channel_id=1, source_target_pairs={{0,128},{64,192},{128,0},{192,64},{1,129},{65,193},{129,1},{193,65... | collective-permute-start | bytes 12296 | tf_op jit(solution)/shard_map/ppermute | solution.py:625
  132.8 3.6 %collective-permute-start.7 = (f32[8,128]{1,0:T(8,128)S(1)}, f32[8,128]{1,0:T(8,128)S(1)}, u32[]{:S(2)}, u32[]{:S(2)}) collective-permute-start(f32[8,128]{1,0:T(8,128)S(1)} %get-tuple-element.49.b0), channel_id=1, source_target_pairs={{0,64},{64,128},{128,192},{192,0},{1,65},{65,129},{129,193},{193,1... | collective-permute-start | bytes 12296 | tf_op jit(solution)/shard_map/ppermute | solution.py:625
  136.8 17.6 %collective-permute-start.13 = (f32[4,8,128]{2,1,0:T(8,128)S(1)}, f32[4,8,128]{2,1,0:T(8,128)S(1)}, u32[]{:S(2)}, u32[]{:S(2)}) collective-permute-start(f32[4,8,128]{2,1,0:T(8,128)S(1)} %get-tuple-element.51), channel_id=1, source_target_pairs={{0,12},{1,13},{2,14},{3,15},{4,0},{5,1},{6,2},{7,3},{8,4},{9,5},{1... | collective-permute-start | bytes 49160 | tf_op jit(solution)/shard_map/ppermute | solution.py:635
  140.4 14.0 %collective-permute-start.12 = (f32[4,8,128]{2,1,0:T(8,128)S(1)}, f32[4,8,128]{2,1,0:T(8,128)S(1)}, u32[]{:S(2)}, u32[]{:S(2)}) collective-permute-start(f32[4,8,128]{2,1,0:T(8,128)S(1)} %get-tuple-element.51), channel_id=1, source_target_pairs={{0,8},{1,9},{2,10},{3,11},{4,12},{5,13},{6,14},{7,15},{8,0},{9,1},... | collective-permute-start | bytes 49160 | tf_op jit(solution)/shard_map/ppermute | solution.py:635
  143.7 10.7 %collective-permute-start.11 = (f32[4,8,128]{2,1,0:T(8,128)S(1)}, f32[4,8,128]{2,1,0:T(8,128)S(1)}, u32[]{:S(2)}, u32[]{:S(2)}) collective-permute-start(f32[4,8,128]{2,1,0:T(8,128)S(1)} %get-tuple-element.51), channel_id=1, source_target_pairs={{0,4},{1,5},{2,6},{3,7},{4,8},{5,9},{6,10},{7,11},{8,12},{9,13},{1... | collective-permute-start | bytes 49160 | tf_op jit(solution)/shard_map/ppermute | solution.py:635
  145.4 9.0 %collective-permute-start.10 = (f32[4,8,128]{2,1,0:T(8,128)S(1)}, f32[4,8,128]{2,1,0:T(8,128)S(1)}, u32[]{:S(2)}, u32[]{:S(2)}) collective-permute-start(f32[4,8,128]{2,1,0:T(8,128)S(1)} %get-tuple-element.51), channel_id=1, source_target_pairs={{0,0},{1,1},{2,2},{3,3},{4,4},{5,5},{6,6},{7,7},{8,8},{9,9},{10,10... | collective-permute-start | bytes 49160 | tf_op jit(solution)/shard_map/ppermute | solution.py:635

commit v5 on v4

--- a/solution.py
+++ b/solution.py
@@ -527,9 +527,9 @@
         for s, value in enumerate((c0, c1, c2, c3)):
             cols[:, eight(((place["y"] - s) & 3) * 8), :] = value[...]
 
-    for half in range(2):
+    for half in range(4):
         base = 32 * half
-        factors = [[side[r, eight(step * 64 + base + g * 8), :] for r in range(4)] for g in range(4)]
+        factors = [[side[r, eight(step * 128 + base + g * 8), :] for r in range(4)] for g in range(4)]
         for k in range(32):
             line = [jnp.broadcast_to(cols[r, k : k + 1, :], (8, 128)) for r in range(4)]
             for g in range(4):
@@ -641,11 +641,11 @@
     spectrogram, side, *columns = lax.optimization_barrier((spectrogram, side, *columns))
     correlation = pl.pallas_call(
         correlation_kernel,
-        grid=(4,),
+        grid=(2,),
         out_shape=jax.ShapeDtypeStruct((256, 4096), F32),
         in_specs=[pl.BlockSpec((4, 256, 128), lambda i: (0, 0, 0))]
         + [pl.BlockSpec((4, 8, 128), lambda i: (0, 0, 0))] * 4,
-        out_specs=pl.BlockSpec((64, 4096), lambda i: (i, 0)),
+        out_specs=pl.BlockSpec((128, 4096), lambda i: (i, 0)),
         scratch_shapes=[pltpu.VMEM((4, 32, 128), F32)],
         compiler_params=PARAMS,
         cost_estimate=pl.CostEstimate(flops=1 << 23, bytes_accessed=1 << 22, transcendentals=0),

time: 159 us -> 158 us (level)
  no operation moved by 1% of the time
where the time goes in v5:
time: 158 us; the launch traced here: 157 us
  blocking collectives  59.8 us (38%)
  starting transfers between devices  40.5 us (26%)
  waiting for transfers between devices  34.9 us (22%)
  Pallas kernels  16.4 us (10%)
  local copies, waits for them, and re-layouts  2.35 us (1%)
  other arithmetic  2.15 us (1%)
    all_to_all x3, blocking collectives, swap_plane(): lax.all_to_all(value, 'tm', split_axis=0, concat_axis=0, axis_index_group...  59.8 us
    ppermute x6, waiting for transfers between devices, swap_z(): lax.ppermute(blocks[step], 'tm', ring('z', step))  26.2 us
    ppermute x6, starting transfers between devices, swap_z(): lax.ppermute(blocks[step], 'tm', ring('z', step))  17.3 us
    pallas_call x8, Pallas kernels, call(): pl.pallas_call(kernel, out_shape=[jax.ShapeDtypeStruct(s, F32) for s in o...  13.9 us
    ppermute x4, starting transfers between devices, on_device(): columns.append(lax.ppermute(normal, ('grp', 'tm'), pairs))  13.5 us
    all_to_all x1, starting transfers between devices, swap_plane(): lax.all_to_all(value, 'tm', split_axis=0, concat_axis=0, axis_index_group...  5.95 us
    ppermute x1, waiting for transfers between devices, on_device(): lax.ppermute(last, 'tm', [(d, (d + 1) % 64) for d in range(64)])  5.47 us
    ppermute x1, starting transfers between devices, on_device(): lax.ppermute(last, 'tm', [(d, (d + 1) % 64) for d in range(64)])  3.27 us
  transfers between devices with their start and end apart: 15, of which 7 were waited for; matrix products, arithmetic and copies ran while one was open for 2% of the time, Pallas kernels for 3%

profile of v5, /device:TPU:4, one launch (start us, length us, event | category | flops | bytes accessed | tf_op | source)
XLA Modules:
  0.0 157.0 jit_solution(11984096476309425139)
XLA Ops:
  1.4 3.3 %collective-permute-start = (f32[8,128]{1,0:T(8,128)S(1)}, f32[8,128]{1,0:T(8,128)S(1)}, u32[]{:S(2)}, u32[]{:S(2)}) collective-permute-start(f32[8,128]{1,0:T(8,128)S(1)} %reshape_squeeze.3), channel_id=1, source_target_pairs={{0,1},{1,2},{2,3},{3,4},{4,5},{5,6},{6,7},{7,8},{8,9},{9,10},{10,1... | collective-permute-start | bytes 12296 | tf_op jit(solution)/shard_map/ppermute | solution.py:586
  6.3 5.5 %collective-permute-done = f32[8,128]{1,0:T(8,128)S(1)} collective-permute-done((f32[8,128]{1,0:T(8,128)S(1)}, f32[8,128]{1,0:T(8,128)S(1)}, u32[]{:S(2)}, u32[]{:S(2)}) %collective-permute-start) | collective-permute-done | bytes 4128 | tf_op jit(solution)/shard_map/ppermute | solution.py:586
  11.8 2.0 %shard_map.59 = f32[16,16,1024]{2,1,0:T(8,128)S(1)} custom-call(f32[2,128,1024]{2,1,0:T(8,128)S(1)} %bitcast.8, f32[1,512]{1,0:T(1,128)S(1)} %multiply_add_fusion.halo, bf16[2,768,256]{2,1,0:T(8,128)(2,1)S(1)} %copy-done.1), custom_call_target="tpu_custom_call" | custom-call | flops 1048576 | bytes 2097152 | tf_op jit(solution)/shard_map/pallas_call | solution.py:545
  13.8 19.4 %all_to_all.20.blocks = f32[16,16,1024]{2,1,0:T(8,128)S(1)} all-to-all(f32[16,16,1024]{2,1,0:T(8,128)S(1)} %shard_map.59), channel_id=1, replica_groups={{0,4,8,12,16,20,24,28,32,36,40,44,48,52,56,60},{1,5,9,13,17,21,25,29,33..., dimensions={0} | all-to-all | bytes 2097152 | tf_op jit(solution)/shard_map/all_to_all | solution.py:572
  35.3 2.9 %collective-permute-start.2 = (f32[4,16,1024]{2,1,0:T(8,128)S(1)}, f32[4,16,1024]{2,1,0:T(8,128)S(1)}, u32[]{:S(2)}, u32[]{:S(2)}) collective-permute-start(f32[4,16,1024]{2,1,0:T(8,128)S(1)} %get-tuple-element.36), channel_id=1, source_target_pairs={{0,2},{1,3},{2,0},{3,1},{4,6},{5,7},{6,4},{7,5},{8,10},{9,11},{10,... | collective-permute-start | bytes 786440 | tf_op jit(solution)/shard_map/ppermute | solution.py:566
  38.2 3.9 %collective-permute-start.3 = (f32[4,16,1024]{2,1,0:T(8,128)S(1)}, f32[4,16,1024]{2,1,0:T(8,128)S(1)}, u32[]{:S(2)}, u32[]{:S(2)}) collective-permute-start(f32[4,16,1024]{2,1,0:T(8,128)S(1)} %get-tuple-element.37), channel_id=1, source_target_pairs={{0,3},{1,0},{2,1},{3,2},{4,7},{5,4},{6,5},{7,6},{8,11},{9,8},{10,9... | collective-permute-start | bytes 786440 | tf_op jit(solution)/shard_map/ppermute | solution.py:566
  42.0 2.0 %fusion.5 = (f32[1,512,256]{2,1,0:T(8,128)S(1)}, f32[1,512,256]{2,1,0:T(8,128)S(1)}) fusion(s32[256]{0:T(256)S(1)} %subtract_multiply_fusion, s32[512]{0:T(512)S(1)} %add_add_fusion), kind=kLoop, calls=%fused_computation.8 | loop fusion | flops 1048576 | bytes 1051648 | tf_op jit(solution)/shard_map/cos | solution.py:608
  44.1 11.1 %collective-permute-done.1.r1 = f32[4,16,1024]{2,1,0:T(8,128)S(1)} collective-permute-done((f32[4,16,1024]{2,1,0:T(8,128)S(1)}, f32[4,16,1024]{2,1,0:T(8,128)S(1)}, u32[]{:S(2)}, u32[]{:S(2)}) %collective-permute-start.1) | collective-permute-done | bytes 262176 | tf_op jit(solution)/shard_map/ppermute | solution.py:566
  55.3 5.6 %collective-permute-done.3.r3 = f32[4,16,1024]{2,1,0:T(8,128)S(1)} collective-permute-done((f32[4,16,1024]{2,1,0:T(8,128)S(1)}, f32[4,16,1024]{2,1,0:T(8,128)S(1)}, u32[]{:S(2)}, u32[]{:S(2)}) %collective-permute-start.3) | collective-permute-done | bytes 262176 | tf_op jit(solution)/shard_map/ppermute | solution.py:566
  61.3 20.5 %all_to_all.21.blocks = f32[16,16,1024]{2,1,0:T(8,128)S(1)} all-to-all(f32[16,16,1024]{2,1,0:T(8,128)S(1)} %shard_map.61), channel_id=1, replica_groups={{0,4,8,12,16,20,24,28,32,36,40,44,48,52,56,60},{1,5,9,13,17,21,25,29,33..., dimensions={0} | all-to-all | bytes 2097152 | tf_op jit(solution)/shard_map/all_to_all | solution.py:572
  81.8 4.4 %shard_map.62 = f32[16,136,128]{2,1,0:T(8,128)S(1)} custom-call(f32[16,16,1024]{2,1,0:T(8,128)S(1)} %all_to_all.21.blocks, bf16[12,256,256]{2,1,0:T(8,128)(2,1)S(1)} %copy-done, f32[2,512,256]{2,1,0:T(8,128)S(1)} %pad_maximum_fusion.disp), custom_call_target="tpu_custom_call" | custom-call | flops 1048576 | bytes 2228224 | tf_op jit(solution)/shard_map/pallas_call | solution.py:545
  86.2 19.8 %all_to_all.22.blocks = f32[16,136,128]{2,1,0:T(8,128)S(1)} all-to-all(f32[16,136,128]{2,1,0:T(8,128)S(1)} %shard_map.62), channel_id=1, replica_groups={{0,4,8,12,16,20,24,28,32,36,40,44,48,52,56,60},{1,5,9,13,17,21,25,29,33..., dimensions={0} | all-to-all | bytes 2228224 | tf_op jit(solution)/shard_map/all_to_all | solution.py:572
  106.6 3.3 %collective-permute-start.4 = (f32[528,128]{1,0:T(8,128)S(1)}, f32[528,128]{1,0:T(8,128)S(1)}, u32[]{:S(2)}, u32[]{:S(2)}) collective-permute-start(f32[528,128]{1,0:T(8,128)S(1)} %get-tuple-element.45), channel_id=1, source_target_pairs={{0,1},{1,2},{2,3},{3,0},{4,5},{5,6},{6,7},{7,4},{8,9},{9,10},{10,1... | collective-permute-start | bytes 811016 | tf_op jit(solution)/shard_map/ppermute | solution.py:566
  109.9 2.7 %collective-permute-start.5 = (f32[528,128]{1,0:T(8,128)S(1)}, f32[528,128]{1,0:T(8,128)S(1)}, u32[]{:S(2)}, u32[]{:S(2)}) collective-permute-start(f32[528,128]{1,0:T(8,128)S(1)} %get-tuple-element.46), channel_id=1, source_target_pairs={{0,2},{1,3},{2,0},{3,1},{4,6},{5,7},{6,4},{7,5},{8,10},{9,11},{10,... | collective-permute-start | bytes 811016 | tf_op jit(solution)/shard_map/ppermute | solution.py:566
  112.6 3.1 %collective-permute-start.6 = (f32[528,128]{1,0:T(8,128)S(1)}, f32[528,128]{1,0:T(8,128)S(1)}, u32[]{:S(2)}, u32[]{:S(2)}) collective-permute-start(f32[528,128]{1,0:T(8,128)S(1)} %get-tuple-element.47), channel_id=1, source_target_pairs={{0,3},{1,0},{2,1},{3,2},{4,7},{5,4},{6,5},{7,6},{8,11},{9,8},{10,9... | collective-permute-start | bytes 811016 | tf_op jit(solution)/shard_map/ppermute | solution.py:566
  115.7 4.1 %collective-permute-done.4.r1 = f32[528,128]{1,0:T(8,128)S(1)} collective-permute-done((f32[528,128]{1,0:T(8,128)S(1)}, f32[528,128]{1,0:T(8,128)S(1)}, u32[]{:S(2)}, u32[]{:S(2)}) %collective-permute-start.4) | collective-permute-done | bytes 270368 | tf_op jit(solution)/shard_map/ppermute | solution.py:566
  119.7 5.4 %collective-permute-done.5.r2 = f32[528,128]{1,0:T(8,128)S(1)} collective-permute-done((f32[528,128]{1,0:T(8,128)S(1)}, f32[528,128]{1,0:T(8,128)S(1)}, u32[]{:S(2)}, u32[]{:S(2)}) %collective-permute-start.5) | collective-permute-done | bytes 270368 | tf_op jit(solution)/shard_map/ppermute | solution.py:566
  126.7 6.0 %all-to-all-start.3 = ((f32[16,136,128]{2,1,0:T(8,128)}), f32[16,136,128]{2,1,0:T(8,128)S(1)}, u32[]{:S(2)}, u32[]{:S(2)}) async-start(f32[16,136,128]{2,1,0:T(8,128)} %get-tuple-element.48), calls=%async_computation.3 | async-start | bytes 2228224 | tf_op jit(solution)/shard_map/all_to_all | solution.py:572
  134.0 2.4 %collective-permute-done.8.b2 = f32[8,128]{1,0:T(8,128)S(1)} collective-permute-done((f32[8,128]{1,0:T(8,128)S(1)}, f32[8,128]{1,0:T(8,128)S(1)}, u32[]{:S(2)}, u32[]{:S(2)}) %collective-permute-start.8) | collective-permute-done | bytes 4128 | tf_op jit(solution)/shard_map/ppermute | solution.py:625
  136.8 3.6 %collective-permute-start.13 = (f32[4,8,128]{2,1,0:T(8,128)S(1)}, f32[4,8,128]{2,1,0:T(8,128)S(1)}, u32[]{:S(2)}, u32[]{:S(2)}) collective-permute-start(f32[4,8,128]{2,1,0:T(8,128)S(1)} %get-tuple-element.51), channel_id=1, source_target_pairs={{0,12},{1,13},{2,14},{3,15},{4,0},{5,1},{6,2},{7,3},{8,4},{9,5},{1... | collective-permute-start | bytes 49160 | tf_op jit(solution)/shard_map/ppermute | solution.py:635
  140.4 3.3 %collective-permute-start.12 = (f32[4,8,128]{2,1,0:T(8,128)S(1)}, f32[4,8,128]{2,1,0:T(8,128)S(1)}, u32[]{:S(2)}, u32[]{:S(2)}) collective-permute-start(f32[4,8,128]{2,1,0:T(8,128)S(1)} %get-tuple-element.51), channel_id=1, source_target_pairs={{0,8},{1,9},{2,10},{3,11},{4,12},{5,13},{6,14},{7,15},{8,0},{9,1},... | collective-permute-start | bytes 49160 | tf_op jit(solution)/shard_map/ppermute | solution.py:635
  145.4 4.9 %collective-permute-start.10 = (f32[4,8,128]{2,1,0:T(8,128)S(1)}, f32[4,8,128]{2,1,0:T(8,128)S(1)}, u32[]{:S(2)}, u32[]{:S(2)}) collective-permute-start(f32[4,8,128]{2,1,0:T(8,128)S(1)} %get-tuple-element.51), channel_id=1, source_target_pairs={{0,0},{1,1},{2,2},{3,3},{4,4},{5,5},{6,6},{7,7},{8,8},{9,9},{10,10... | collective-permute-start | bytes 49160 | tf_op jit(solution)/shard_map/ppermute | solution.py:635
  150.3 4.1 %shard_map.65 = f32[128,2048]{1,0:T(8,128)} custom-call(f32[16,136,128]{2,1,0:T(8,128)S(1)} %all-to-all-done.3.blocks, bf16[2,256,256]{2,1,0:T(8,128)(2,1)S(1)} %copy-done.2), custom_call_target="tpu_custom_call" | custom-call | flops 1048576 | bytes 2097152 | tf_op jit(solution)/shard_map/pallas_call | solution.py:545
  154.4 2.5 %shard_map.67 = f32[256,4096]{1,0:T(8,128)} custom-call(f32[4,256,128]{2,1,0:T(8,128)S(1)} %get-tuple-element.53.side, f32[4,8,128]{2,1,0:T(8,128)S(1)} %collective-permute-done.10.c0, f32[4,8,128]{2,1,0:T(8,128)S(1)} %collective-permute-done.11.c1, f32[4,8,128]{2,1,0:T(8,128)S(1)} %collective-permute-done.12.c2, f32[4,8,128]{2,1,0:T(8,128)S(1)} %collective-permute-done.13.c3), custom_call_target="tpu_custom_call" | custom-call | flops 8388608 | bytes 4194304 | tf_op jit(solution)/shard_map/pallas_call | solution.py:642
  (33 shorter events, 10.5 us)
Async XLA Ops:
  0.6 11.1 %copy-start.1 = (bf16[2,768,256]{2,1,0:T(8,128)(2,1)S(1)}, bf16[2,768,256]{2,1,0:T(8,128)(2,1)}, u32[]{:S(2)}) copy-start(bf16[2,768,256]{2,1,0:T(8,128)(2,1)} %constant.87.clone.toep_hbm) | copy-start | bytes 2359300
  1.4 10.3 %collective-permute-start = (f32[8,128]{1,0:T(8,128)S(1)}, f32[8,128]{1,0:T(8,128)S(1)}, u32[]{:S(2)}, u32[]{:S(2)}) collective-permute-start(f32[8,128]{1,0:T(8,128)S(1)} %reshape_squeeze.3), channel_id=1, source_target_pairs={{0,1},{1,2},{2,3},{3,4},{4,5},{5,6},{6,7},{7,8},{8,9},{9,10},{10,1... | collective-permute-start | bytes 12296 | tf_op jit(solution)/shard_map/ppermute | solution.py:586
  33.9 21.4 %collective-permute-start.1 = (f32[4,16,1024]{2,1,0:T(8,128)S(1)}, f32[4,16,1024]{2,1,0:T(8,128)S(1)}, u32[]{:S(2)}, u32[]{:S(2)}) collective-permute-start(f32[4,16,1024]{2,1,0:T(8,128)S(1)} %get-tuple-element.35), channel_id=1, source_target_pairs={{0,1},{1,2},{2,3},{3,0},{4,5},{5,6},{6,7},{7,4},{8,9},{9,10},{10,1... | collective-permute-start | bytes 786440 | tf_op jit(solution)/shard_map/ppermute | solution.py:566
  35.3 20.0 %collective-permute-start.2 = (f32[4,16,1024]{2,1,0:T(8,128)S(1)}, f32[4,16,1024]{2,1,0:T(8,128)S(1)}, u32[]{:S(2)}, u32[]{:S(2)}) collective-permute-start(f32[4,16,1024]{2,1,0:T(8,128)S(1)} %get-tuple-element.36), channel_id=1, source_target_pairs={{0,2},{1,3},{2,0},{3,1},{4,6},{5,7},{6,4},{7,5},{8,10},{9,11},{10,... | collective-permute-start | bytes 786440 | tf_op jit(solution)/shard_map/ppermute | solution.py:566
  38.2 22.7 %collective-permute-start.3 = (f32[4,16,1024]{2,1,0:T(8,128)S(1)}, f32[4,16,1024]{2,1,0:T(8,128)S(1)}, u32[]{:S(2)}, u32[]{:S(2)}) collective-permute-start(f32[4,16,1024]{2,1,0:T(8,128)S(1)} %get-tuple-element.37), channel_id=1, source_target_pairs={{0,3},{1,0},{2,1},{3,2},{4,7},{5,4},{6,5},{7,6},{8,11},{9,8},{10,9... | collective-permute-start | bytes 786440 | tf_op jit(solution)/shard_map/ppermute | solution.py:566
  61.2 20.6 %copy-start = (bf16[12,256,256]{2,1,0:T(8,128)(2,1)S(1)}, bf16[12,256,256]{2,1,0:T(8,128)(2,1)}, u32[]{:S(2)}) copy-start(bf16[12,256,256]{2,1,0:T(8,128)(2,1)} %constant.88.clone.squares) | copy-start | bytes 4718596
  106.6 13.2 %collective-permute-start.4 = (f32[528,128]{1,0:T(8,128)S(1)}, f32[528,128]{1,0:T(8,128)S(1)}, u32[]{:S(2)}, u32[]{:S(2)}) collective-permute-start(f32[528,128]{1,0:T(8,128)S(1)} %get-tuple-element.45), channel_id=1, source_target_pairs={{0,1},{1,2},{2,3},{3,0},{4,5},{5,6},{6,7},{7,4},{8,9},{9,10},{10,1... | collective-permute-start | bytes 811016 | tf_op jit(solution)/shard_map/ppermute | solution.py:566
  109.9 15.2 %collective-permute-start.5 = (f32[528,128]{1,0:T(8,128)S(1)}, f32[528,128]{1,0:T(8,128)S(1)}, u32[]{:S(2)}, u32[]{:S(2)}) collective-permute-start(f32[528,128]{1,0:T(8,128)S(1)} %get-tuple-element.46), channel_id=1, source_target_pairs={{0,2},{1,3},{2,0},{3,1},{4,6},{5,7},{6,4},{7,5},{8,10},{9,11},{10,... | collective-permute-start | bytes 811016 | tf_op jit(solution)/shard_map/ppermute | solution.py:566
  112.6 12.5 %collective-permute-start.6 = (f32[528,128]{1,0:T(8,128)S(1)}, f32[528,128]{1,0:T(8,128)S(1)}, u32[]{:S(2)}, u32[]{:S(2)}) collective-permute-start(f32[528,128]{1,0:T(8,128)S(1)} %get-tuple-element.47), channel_id=1, source_target_pairs={{0,3},{1,0},{2,1},{3,2},{4,7},{5,4},{6,5},{7,6},{8,11},{9,8},{10,9... | collective-permute-start | bytes 811016 | tf_op jit(solution)/shard_map/ppermute | solution.py:566
  126.7 23.6 %copy-start.2 = (bf16[2,256,256]{2,1,0:T(8,128)(2,1)S(1)}, bf16[2,256,256]{2,1,0:T(8,128)(2,1)}, u32[]{:S(2)}) copy-start(bf16[2,256,256]{2,1,0:T(8,128)(2,1)} %constant.89.clone.mat) | copy-start | bytes 786436
  126.7 23.6 %all-to-all-start.3 = ((f32[16,136,128]{2,1,0:T(8,128)}), f32[16,136,128]{2,1,0:T(8,128)S(1)}, u32[]{:S(2)}, u32[]{:S(2)}) async-start(f32[16,136,128]{2,1,0:T(8,128)} %get-tuple-element.48), calls=%async_computation.3 | async-start | bytes 2228224 | tf_op jit(solution)/shard_map/all_to_all | solution.py:572
  132.7 1.3 collective-permute-start.9
  132.7 3.7 %collective-permute-start.8 = (f32[8,128]{1,0:T(8,128)S(1)}, f32[8,128]{1,0:T(8,128)S(1)}, u32[]{:S(2)}, u32[]{:S(2)}) collective-permute-start(f32[8,128]{1,0:T(8,128)S(1)} %get-tuple-element.49.b0), channel_id=1, source_target_pairs={{0,128},{64,192},{128,0},{192,64},{1,129},{65,193},{129,1},{193,65... | collective-permute-start | bytes 12296 | tf_op jit(solution)/shard_map/ppermute | solution.py:625
  132.8 3.6 %collective-permute-start.7 = (f32[8,128]{1,0:T(8,128)S(1)}, f32[8,128]{1,0:T(8,128)S(1)}, u32[]{:S(2)}, u32[]{:S(2)}) collective-permute-start(f32[8,128]{1,0:T(8,128)S(1)} %get-tuple-element.49.b0), channel_id=1, source_target_pairs={{0,64},{64,128},{128,192},{192,0},{1,65},{65,129},{129,193},{193,1... | collective-permute-start | bytes 12296 | tf_op jit(solution)/shard_map/ppermute | solution.py:625
  136.8 17.6 %collective-permute-start.13 = (f32[4,8,128]{2,1,0:T(8,128)S(1)}, f32[4,8,128]{2,1,0:T(8,128)S(1)}, u32[]{:S(2)}, u32[]{:S(2)}) collective-permute-start(f32[4,8,128]{2,1,0:T(8,128)S(1)} %get-tuple-element.51), channel_id=1, source_target_pairs={{0,12},{1,13},{2,14},{3,15},{4,0},{5,1},{6,2},{7,3},{8,4},{9,5},{1... | collective-permute-start | bytes 49160 | tf_op jit(solution)/shard_map/ppermute | solution.py:635
  140.4 14.0 %collective-permute-start.12 = (f32[4,8,128]{2,1,0:T(8,128)S(1)}, f32[4,8,128]{2,1,0:T(8,128)S(1)}, u32[]{:S(2)}, u32[]{:S(2)}) collective-permute-start(f32[4,8,128]{2,1,0:T(8,128)S(1)} %get-tuple-element.51), channel_id=1, source_target_pairs={{0,8},{1,9},{2,10},{3,11},{4,12},{5,13},{6,14},{7,15},{8,0},{9,1},... | collective-permute-start | bytes 49160 | tf_op jit(solution)/shard_map/ppermute | solution.py:635
  143.7 10.7 %collective-permute-start.11 = (f32[4,8,128]{2,1,0:T(8,128)S(1)}, f32[4,8,128]{2,1,0:T(8,128)S(1)}, u32[]{:S(2)}, u32[]{:S(2)}) collective-permute-start(f32[4,8,128]{2,1,0:T(8,128)S(1)} %get-tuple-element.51), channel_id=1, source_target_pairs={{0,4},{1,5},{2,6},{3,7},{4,8},{5,9},{6,10},{7,11},{8,12},{9,13},{1... | collective-permute-start | bytes 49160 | tf_op jit(solution)/shard_map/ppermute | solution.py:635
  145.4 9.0 %collective-permute-start.10 = (f32[4,8,128]{2,1,0:T(8,128)S(1)}, f32[4,8,128]{2,1,0:T(8,128)S(1)}, u32[]{:S(2)}, u32[]{:S(2)}) collective-permute-start(f32[4,8,128]{2,1,0:T(8,128)S(1)} %get-tuple-element.51), channel_id=1, source_target_pairs={{0,0},{1,1},{2,2},{3,3},{4,4},{5,5},{6,6},{7,7},{8,8},{9,9},{10,10... | collective-permute-start | bytes 49160 | tf_op jit(solution)/shard_map/ppermute | solution.py:635
